TPU v7x, 32 devices: a whole 2x2x4 slice. The times are simulated.
32 devices in a mesh: rx: 16 (over z, x, core), band: 2 (over y).
Axes of the slice: x: 2, y: 2, z: 4, core: 2. Of those that a mesh axis runs over, the one named last changes fastest.
Arguments:
- spectra: bfloat16 [2, 256, 64, 2048], P(None, 'band', None, 'rx'), may hold values from -6 to 6
- source_index: int32 [16], replicated, may hold values from 0 to 2047, as said below
Outputs:
- stack: bfloat16 [2, 256, 16, 2048], P(None, 'band', None, 'rx')
Inputs may be any that keep to these rules, and one draw needn't show every extreme that they name: `source_index`: virtual source s is one of channels s * 128 to (s + 1) * 128 - 1; the first and the last channel are sources.
All inputs are finite; a program needn't handle non-finite values.
Results may differ from a plain program's by a relative error of at most 0.0059.
Values may be sent and summed in bfloat16 or wider, within the bound.
No kernel may reach another device: no remote copies, remote signals or barrier semaphores. Data moves between devices by JAX's collectives and lax.ppermute only.
A program may use at most 64 MiB of HBM per device.

v0:
```python
import jax
import jax.numpy as jnp
from jax import lax
from jax.sharding import PartitionSpec as P

HALF = 4


def padded_2(block, sides, width):
    for axis, dim in sides:
        count = lax.axis_size(axis)
        forward = [(i, i + 1) for i in range(count - 1)]
        backward = [(target, source) for source, target in forward]
        low = lax.ppermute(
            lax.slice_in_dim(block, block.shape[dim] - width, None, axis=dim), axis, forward
        )
        high = lax.ppermute(lax.slice_in_dim(block, 0, width, axis=dim), axis, backward)
        block = jnp.concatenate([low, block, high], axis=dim)
    return block


def magnitude(values_in):
    values = values_in.astype(jnp.float32)
    rounded = lax.optimization_barrier(
        jnp.sqrt(values[0] * values[0] + values[1] * values[1]).astype(jnp.bfloat16)
    )
    return rounded


def whiten(spectra):
    bin_count = spectra.shape[1]
    padded = padded_2(spectra, (("band", 1),), HALF)
    amplitude = magnitude(padded).astype(jnp.float32)
    total = amplitude[0:bin_count]
    for offset in range(1, 2 * HALF + 1):
        total = total + amplitude[offset : offset + bin_count]
    smooth = total / (2 * HALF + 1)
    return (spectra.astype(jnp.float32) / (smooth + 0.1)[None]).astype(jnp.bfloat16)


def cross_spectra(whitened, source_rows):
    bin_count = whitened.shape[1]
    window_count = whitened.shape[2]
    sources = source_rows.reshape(source_rows.shape[0], 2, bin_count, window_count)
    source_real = sources[:, 0]
    source_imag = sources[:, 1]
    coefficients = jnp.stack(
        [jnp.stack([source_real, source_imag], 0), jnp.stack([-source_imag, source_real], 0)], 0
    )
    products = jnp.einsum(
        "oqnfw,qfwc->ofnc", coefficients, whitened, preferred_element_type=jnp.float32
    )
    return (products / window_count).astype(jnp.bfloat16)


def local(spectra, source_index):
    whitened = whiten(spectra)
    device_rank = lax.axis_index("rx")
    channels_here = spectra.shape[3]
    local_column = source_index[device_rank] - device_rank * channels_here
    own_row = lax.dynamic_slice_in_dim(whitened, local_column, 1, 3).reshape(1, -1)
    collected = lax.all_gather(own_row, "rx", axis=0, tiled=True)
    return cross_spectra(whitened, collected)


def solution(mesh):
    return jax.shard_map(
        local,
        mesh=mesh,
        in_specs=(P(None, "band", None, "rx"), P()),
        out_specs=P(None, "band", None, "rx"),
        check_vma=False,
    )
```

profile of v0, /device:TPU:0, one launch (start us, length us, event | category | flops | bytes accessed | tf_op | source)
XLA Modules:
  0.0 61.4 jit_solution(15114180625359943499)
XLA Ops:
  0.0 1.0 %fusion.23 = (bf16[2,4,64,128]{3,2,1,0:T(8,128)(2,1)S(1)}, bf16[2,4,64,128]{3,2,1,0:T(8,128)(2,1)S(1)}) fusion(bf16[2,128,64,128]{3,2,1,0:T(8,128)(2,1)} %param.2), kind=kLoop, calls=%fused_computation.33 | loop fusion | bytes 524288 | tf_op jit(solution)/shard_map/slice | solution.py:15
  1.0 1.3 %collective-permute-start.1 = (bf16[2,4,64,128]{3,2,1,0:T(8,128)(2,1)S(1)}, bf16[2,4,64,128]{3,2,1,0:T(8,128)(2,1)S(1)}, u32[]{:S(2)}, u32[]{:S(2)}) collective-permute-start(bf16[2,4,64,128]{3,2,1,0:T(8,128)(2,1)S(1)} %get-tuple-element.6), channel_id=1, source_target_pairs={{1,0},{3,2},{5,4},{7,6},{9,8},{11,10},{13,12},{15,14},{17,16},{19,... | collective-permute-start | bytes 393224 | tf_op jit(solution)/shard_map/ppermute | solution.py:17
  2.3 4.9 %collective-permute-start = (bf16[2,4,64,128]{3,2,1,0:T(8,128)(2,1)S(1)}, bf16[2,4,64,128]{3,2,1,0:T(8,128)(2,1)S(1)}, u32[]{:S(2)}, u32[]{:S(2)}) collective-permute-start(bf16[2,4,64,128]{3,2,1,0:T(8,128)(2,1)S(1)} %get-tuple-element.5), channel_id=1, source_target_pairs={{0,1},{2,3},{4,5},{6,7},{8,9},{10,11},{12,13},{14,15},{16,17},{18,... | collective-permute-start | bytes 393224 | tf_op jit(solution)/shard_map/ppermute | solution.py:14
  7.2 1.2 %dynamic_slice.6 = s32[1]{0:T(128)} dynamic-slice(s32[16]{0:T(128)} %param.3, s32[]{:T(128)S(6)} %select_n.6), dynamic_slice_sizes={1} | dynamic-slice | bytes 12 | tf_op jit(solution)/shard_map/dynamic_slice | solution.py:60
  9.1 0.0 collective-permute-done.1
  9.1 0.8 %collective-permute-done = bf16[2,4,64,128]{3,2,1,0:T(8,128)(2,1)S(1)} collective-permute-done((bf16[2,4,64,128]{3,2,1,0:T(8,128)(2,1)S(1)}, bf16[2,4,64,128]{3,2,1,0:T(8,128)(2,1)S(1)}, u32[]{:S(2)}, u32[]{:S(2)}) %collective-permute-start) | collective-permute-done | bytes 131104 | tf_op jit(solution)/shard_map/ppermute | solution.py:14
  9.9 2.6 %maximum_convert_fusion = f32[2,136,64,128]{3,2,1,0:T(8,128)S(1)} fusion(bf16[2,4,64,128]{3,2,1,0:T(8,128)(2,1)S(1)} %collective-permute-done.1, bf16[2,128,64,128]{3,2,1,0:T(8,128)(2,1)} %param.2, bf16[2,4,64,128]{3,2,1,0:T(8,128)(2,1)S(1)} %collective-permute-done), kind=kLoop, calls=%fused_computation.6 | loop fusion | flops 6684672 | bytes 13369344 | tf_op jit(solution)/shard_map/convert_element_type | solution.py:23
  12.5 1.6 %fusion.7 = bf16[136,64,128]{2,1,0:T(8,128)(2,1)S(1)} fusion(f32[2,136,64,128]{3,2,1,0:T(8,128)S(1)} %maximum_convert_fusion), kind=kLoop, calls=%fused_computation.20 | loop fusion | flops 4456448 | bytes 11141120 | tf_op jit(solution)/shard_map/convert_element_type | solution.py:25
  14.1 0.5 convert_element_type.28
  14.6 0.0 copy-start
  14.6 5.1 %fusion.4 = f32[128,64,128]{2,1,0:T(8,128)S(1)} fusion(f32[136,64,128]{2,1,0:T(8,128)S(1)} %convert_element_type.28), kind=kLoop, calls=%fused_computation.9 | loop fusion | flops 10485760 | bytes 41943040 | tf_op jit(solution)/shard_map/add | solution.py:38
  19.8 0.0 copy-done
  19.8 0.0 copy-start.2
  19.8 1.5 %divide_convert_fusion = bf16[2,128,64,128]{3,2,1,0:T(8,128)(2,1)S(1)} fusion(bf16[2,128,64,128]{3,2,1,0:T(8,128)(2,1)S(1)} %copy-done, f32[128,64,128]{2,1,0:T(8,128)S(1)} %fusion.4), kind=kLoop, calls=%fused_computation | loop fusion | flops 6291456 | bytes 12582912 | tf_op jit(solution)/shard_map/convert_element_type | solution.py:38
  21.3 0.4 copy-done.2
  21.7 3.4 %dynamic-slice_reduce_fusion = bf16[2,128,64]{2,1,0:T(8,128)(2,1)S(1)} fusion(bf16[2,128,64,128]{3,2,1,0:T(8,128)(2,1)S(1)} %divide_convert_fusion, s32[]{:T(128)S(6)} %select_n.7), kind=kLoop, calls=%fused_computation.19 | loop fusion | bytes 65540 | tf_op jit(solution)/shard_map/dynamic_slice | solution.py:61
  25.1 0.1 reshape.24
  25.2 25.6 %all-gather = bf16[16,1,16384]{2,1,0:T(2,128)(2,1)S(1)} all-gather(bf16[1,1,16384]{2,1,0:T(2,128)(2,1)S(1)} %reshape.24), channel_id=1, replica_groups=mesh['rx'=16,'band'=2] {'rx'}, dimensions={0}, use_global_device_ids=true | all-gather | bytes 557056 | tf_op jit(solution)/shard_map/all_gather | solution.py:62
  50.8 3.1 %reduce.1 = bf16[16,16384]{1,0:T(8,128)(2,1)S(1)} reduce(bf16[16,1,16384]{2,1,0:T(2,128)(2,1)S(1)} %all-gather, bf16[]{:T(256)} %constant.20), dimensions={1}, to_apply=%all-gather.reduce_sub_computation | reduce | bytes 1048578 | tf_op jit(solution)/shard_map/all_gather | solution.py:62
  53.9 1.1 %reshape.23 = bf16[16,2,128,64]{3,2,1,0:T(8,128)(2,1)S(1)} reshape(bf16[16,16384]{1,0:T(8,128)(2,1)S(1)} %reduce.1) | data formatting | bytes 1048576 | tf_op jit(solution)/shard_map/reshape | solution.py:44
  55.0 0.0 copy-start.1
  55.1 0.0 copy-start.3
  55.1 0.1 fusion.24
  55.2 0.4 fusion.22
  55.5 0.7 %copy_bitcast_fusion = (bf16[1,16,128,64]{3,1,0,2:T(8,128)(2,1)S(1)}, bf16[1,16,128,64]{3,1,0,2:T(8,128)(2,1)S(1)}) fusion(bf16[16,1,128,64]{3,2,1,0:T(8,128)(2,1)S(1)} %get-tuple-element.7, bf16[16,1,128,64]{3,2,1,0:T(8,128)(2,1)S(1)} %get-tuple-element.8), kind=kLoop, calls=%fused_computation.29 | loop fusion | bytes 1048576 | tf_op jit(solution)/shard_map/stack;squeeze | solution.py:48
  56.2 0.4 maximum_bitcast_fusion
  56.6 0.6 copy-done.1
  57.2 1.3 %copy-done.3 = f32[128,64,128]{2,1,0:T(8,128)S(1)} copy-done((f32[128,64,128]{2,1,0:T(8,128)S(1)}, f32[128,64,128]{2,1,0:T(8,128)}, u32[]{:S(2)}) %copy-start.3) | copy-done | bytes 4194328
  58.5 1.8 %fusion.16 = bf16[2,128,16,128]{3,2,0,1:T(8,128)(2,1)S(1)} fusion(bf16[1,2,16,128,64]{4,2,1,0,3:T(8,128)(2,1)S(1)} %get-tuple-element.10, bf16[1,2,16,128,64]{4,2,1,0,3:T(8,128)(2,1)S(1)} %get-tuple-element.9, f32[128,64,128]{2,1,0:T(8,128)S(1)} %copy-done.3, bf16[2,128,64,128]{3,2,1,0:T(8,128)(2,1)S(1)} %copy-done.1), kind=kOutput, calls=%fused_computation.26 | convolution fusion | flops 143654912 | bytes 10485760 | tf_op jit(solution)/shard_map/oqnfw,qfwc->ofnc/dot_general | solution.py:50
  60.3 1.2 %copy.15 = bf16[2,128,16,128]{3,2,1,0:T(8,128)(2,1)} copy(bf16[2,128,16,128]{3,2,0,1:T(8,128)(2,1)S(1)} %fusion.16) | data formatting | bytes 2097152 | tf_op jit(solution)/shard_map/convert_element_type | solution.py:53
Async XLA Ops:
  1.0 8.1 %collective-permute-start.1 = (bf16[2,4,64,128]{3,2,1,0:T(8,128)(2,1)S(1)}, bf16[2,4,64,128]{3,2,1,0:T(8,128)(2,1)S(1)}, u32[]{:S(2)}, u32[]{:S(2)}) collective-permute-start(bf16[2,4,64,128]{3,2,1,0:T(8,128)(2,1)S(1)} %get-tuple-element.6), channel_id=1, source_target_pairs={{1,0},{3,2},{5,4},{7,6},{9,8},{11,10},{13,12},{15,14},{17,16},{19,... | collective-permute-start | bytes 393224 | tf_op jit(solution)/shard_map/ppermute | solution.py:17
  2.3 7.6 %collective-permute-start = (bf16[2,4,64,128]{3,2,1,0:T(8,128)(2,1)S(1)}, bf16[2,4,64,128]{3,2,1,0:T(8,128)(2,1)S(1)}, u32[]{:S(2)}, u32[]{:S(2)}) collective-permute-start(bf16[2,4,64,128]{3,2,1,0:T(8,128)(2,1)S(1)} %get-tuple-element.5), channel_id=1, source_target_pairs={{0,1},{2,3},{4,5},{6,7},{8,9},{10,11},{12,13},{14,15},{16,17},{18,... | collective-permute-start | bytes 393224 | tf_op jit(solution)/shard_map/ppermute | solution.py:14
  14.6 5.2 %copy-start = (bf16[2,128,64,128]{3,2,1,0:T(8,128)(2,1)S(1)}, bf16[2,128,64,128]{3,2,1,0:T(8,128)(2,1)}, u32[]{:S(2)}) copy-start(bf16[2,128,64,128]{3,2,1,0:T(8,128)(2,1)} %param.2) | copy-start | bytes 12582916
  19.8 1.9 %copy-start.2 = (f32[128,64,128]{2,1,0:T(8,128)}, f32[128,64,128]{2,1,0:T(8,128)S(1)}, u32[]{:S(2)}) copy-start(f32[128,64,128]{2,1,0:T(8,128)S(1)} %fusion.4) | copy-start | bytes 12582916
  55.0 2.2 %copy-start.1 = (bf16[2,128,64,128]{3,2,1,0:T(8,128)(2,1)S(1)}, bf16[2,128,64,128]{3,2,1,0:T(8,128)(2,1)}, u32[]{:S(2)}) copy-start(bf16[2,128,64,128]{3,2,1,0:T(8,128)(2,1)} %param.2) | copy-start | bytes 12582916
  55.1 3.5 %copy-start.3 = (f32[128,64,128]{2,1,0:T(8,128)S(1)}, f32[128,64,128]{2,1,0:T(8,128)}, u32[]{:S(2)}) copy-start(f32[128,64,128]{2,1,0:T(8,128)} %copy-done.2) | copy-start | bytes 12582916
where the time goes:
time: 61.6 us; the launch traced here: 61.4 us
  blocking collectives  25.6 us (42%)
  other arithmetic  15.2 us (25%)
  local copies, waits for them, and re-layouts  11 us (18%)
  starting transfers between devices  6.18 us (10%)
  matrix products  1.77 us (3%)
  waiting for transfers between devices  0.83 us (1%)
  between operations  0.83 us (1%)
    all_gather x1, blocking collectives, local(): collected = lax.all_gather(own_row, 'rx', axis=0, tiled=True)  25.6 us
    add x1, other arithmetic, whiten(): smooth + 0.1  5.14 us
    ppermute x1, starting transfers between devices, padded_2(): lax.ppermute(lax.slice_in_dim(block, block.shape[dim] - width, None, axis...  4.88 us
    dynamic_slice x1, local copies, waits for them, and re-layouts, local(): lax.dynamic_slice_in_dim(whitened, local_column, 1, 3).reshape(1, -1)  3.36 us
    all_gather x1, other arithmetic, local(): collected = lax.all_gather(own_row, 'rx', axis=0, tiled=True)  3.14 us
    convert_element_type x1, other arithmetic, magnitude(): values = values_in.astype(jnp.float32)  2.58 us
    unnamed x9, local copies, waits for them, and re-layouts  2.38 us
    dot_general x1, matrix products, cross_spectra(): jnp.einsum('oqnfw,qfwc->ofnc', coefficients, whitened, preferred_element_...  1.77 us
  transfers between devices with their start and end apart: 2, of which 1 were waited for; matrix products, arithmetic and copies ran while one was open for 2% of the time, Pallas kernels for 0%

commit v1 on v0

v1 whole, which is shorter than its diff:
```python
import functools

import jax
import jax.numpy as jnp
from jax import lax
from jax.experimental import pallas as pl
from jax.experimental.pallas import tpu as pltpu
from jax.sharding import PartitionSpec as P

HALF = 4
SPAN = 2 * HALF + 1
FLOOR = 0.1
PIECES = 4
TINY = 1e-37
VMEM_LIMIT = 48 * 1024 * 1024


def amplitude_of(power):
    return (power * lax.rsqrt(jnp.maximum(power, TINY))).astype(jnp.bfloat16)


def edge_amplitudes(spectra):
    count = lax.axis_size("band")
    rank = lax.axis_index("band")

    def amplitude(part):
        values = part.astype(jnp.float32)
        return jnp.sqrt(values[0] * values[0] + values[1] * values[1]).astype(jnp.bfloat16)

    first = amplitude(spectra[:, :HALF])
    last = amplitude(spectra[:, spectra.shape[1] - HALF :])
    if count == 2:
        received = lax.ppermute(jnp.where(rank == 0, last, first), "band", [(0, 1), (1, 0)])
        zero = jnp.zeros_like(received)
        return jnp.stack([jnp.where(rank == 1, received, zero), jnp.where(rank == 0, received, zero)])
    below = lax.ppermute(last, "band", [(i, i + 1) for i in range(count - 1)])
    above = lax.ppermute(first, "band", [(i + 1, i) for i in range(count - 1)])
    return jnp.stack([below, above])


def select_column(column, rows, width):
    channels = rows.shape[1]
    picks = (lax.broadcasted_iota(jnp.int32, (8, channels), 1) == column).astype(jnp.bfloat16)
    n = rows.shape[0] // width
    out = []
    for block in range(0, n, 8):
        part = rows[block * width : (block + 8) * width]
        flat = lax.dot_general(picks, part, (((1,), (1,)), ((), ())), preferred_element_type=jnp.float32)
        sublane = lax.broadcasted_iota(jnp.int32, (8, width), 0)
        total = jnp.zeros((8, width), jnp.float32)
        for k in range(8):
            total = jnp.where(sublane == k, flat[:, k * width : (k + 1) * width], total)
        out.append(total)
    return out


def extract_kernel(column_ref, spectra_ref, row_ref):
    bins, windows, channels = spectra_ref.shape[1:]
    parts = []
    for part in range(2):
        rows = spectra_ref[part].reshape(bins * windows, channels)
        parts.append(jnp.concatenate(select_column(column_ref[0], rows, windows), 0))
    row_ref[...] = jnp.concatenate(parts, 1).astype(jnp.bfloat16)


def extract_row(spectra, column):
    _, bins, windows, channels = spectra.shape
    step = min(16, bins)
    return pl.pallas_call(
        extract_kernel,
        grid=(bins // step,),
        in_specs=[
            pl.BlockSpec(memory_space=pltpu.SMEM),
            pl.BlockSpec((2, step, windows, channels), lambda i: (0, i, 0, 0)),
        ],
        out_specs=pl.BlockSpec((step, 2 * windows), lambda i: (i, 0)),
        out_shape=jax.ShapeDtypeStruct((bins, 2 * windows), jnp.bfloat16),
        compiler_params=pltpu.CompilerParams(vmem_limit_bytes=VMEM_LIMIT),
        cost_estimate=pl.CostEstimate(flops=2 * 8 * spectra.size, bytes_accessed=2 * spectra.size, transcendentals=0),
        name="extract_row",
    )(column, spectra)


def whiten_row_kernel(column_ref, row_ref, edge_ref, out_ref):
    bins, width = row_ref.shape
    windows = width // 2
    channels = edge_ref.shape[-1]
    rows = edge_ref[...].reshape(2 * HALF * windows, channels)
    edge = select_column(column_ref[0], rows, windows)[0]
    edge = jnp.concatenate([edge, edge], 1)
    values = row_ref[...].astype(jnp.float32)
    squares = values * values
    amplitude = amplitude_of(squares + pltpu.roll(squares, windows, 1))
    target = lax.broadcasted_iota(jnp.int32, (bins, bins), 0)
    source = lax.broadcasted_iota(jnp.int32, (bins, bins), 1)
    near = (jnp.abs(target - source) <= HALF).astype(jnp.bfloat16)
    target = lax.broadcasted_iota(jnp.int32, (bins, 2 * HALF), 0)
    index = lax.broadcasted_iota(jnp.int32, (bins, 2 * HALF), 1)
    source = jnp.where(index < HALF, index - HALF, index - HALF + bins)
    near_edge = (jnp.abs(target - source) <= HALF).astype(jnp.bfloat16)
    total = jnp.dot(near, amplitude, preferred_element_type=jnp.float32)
    total = total + jnp.dot(near_edge, edge.astype(jnp.bfloat16), preferred_element_type=jnp.float32)
    out_ref[...] = (values / (total / SPAN + FLOOR)).astype(jnp.bfloat16)


def whiten_row(row, edges, column):
    return pl.pallas_call(
        whiten_row_kernel,
        in_specs=[
            pl.BlockSpec(memory_space=pltpu.SMEM),
            pl.BlockSpec(memory_space=pltpu.VMEM),
            pl.BlockSpec(memory_space=pltpu.VMEM),
        ],
        out_specs=pl.BlockSpec(memory_space=pltpu.VMEM),
        out_shape=jax.ShapeDtypeStruct(row.shape, jnp.bfloat16),
        compiler_params=pltpu.CompilerParams(vmem_limit_bytes=VMEM_LIMIT),
        name="whiten_row",
    )(column, row, edges)


def whiten_kernel(spectra_ref, edge_ref, out_ref, amplitude_ref):
    bins = spectra_ref.shape[1]
    block = 16 if bins % 16 == 0 else 8
    amplitude_ref[0:HALF] = edge_ref[0].astype(jnp.float32)
    amplitude_ref[bins + HALF : bins + 2 * HALF] = edge_ref[1].astype(jnp.float32)

    @pl.loop(0, bins // block)
    def _(b):
        at = b * block
        real = spectra_ref[0, pl.ds(at, block)].astype(jnp.float32)
        imag = spectra_ref[1, pl.ds(at, block)].astype(jnp.float32)
        amplitude_ref[pl.ds(at + HALF, block)] = amplitude_of(real * real + imag * imag).astype(jnp.float32)

    @pl.loop(0, bins // block)
    def _(b):
        at = b * block
        one = [amplitude_ref[at + k] for k in range(block + 2 * HALF)]
        two = [one[k] + one[k + 1] for k in range(block + 2 * HALF - 1)]
        four = [two[k] + two[k + 2] for k in range(block + 2 * HALF - 3)]
        for k in range(block):
            total = (four[k] + four[k + 4]) + one[k + 8]
            scale = 1.0 / (total * (1.0 / SPAN) + FLOOR)
            out_ref[0, at + k] = (spectra_ref[0, at + k].astype(jnp.float32) * scale).astype(jnp.bfloat16)
            out_ref[1, at + k] = (spectra_ref[1, at + k].astype(jnp.float32) * scale).astype(jnp.bfloat16)


def whiten_piece(spectra, edges, piece):
    _, bins, windows, channels = spectra.shape
    width = windows // PIECES
    return pl.pallas_call(
        whiten_kernel,
        grid=(1,),
        in_specs=[
            pl.BlockSpec((2, bins, width, channels), lambda i: (0, 0, piece, 0)),
            pl.BlockSpec((2, HALF, width, channels), lambda i: (0, 0, piece, 0)),
        ],
        out_specs=pl.BlockSpec((2, bins, width, channels), lambda i: (0, 0, 0, 0)),
        out_shape=jax.ShapeDtypeStruct((2, bins, width, channels), jnp.bfloat16),
        scratch_shapes=[pltpu.VMEM((bins + 2 * HALF, width, channels), jnp.float32)],
        compiler_params=pltpu.CompilerParams(vmem_limit_bytes=VMEM_LIMIT),
        cost_estimate=pl.CostEstimate(
            flops=20 * spectra.size // PIECES, bytes_accessed=4 * spectra.size // PIECES, transcendentals=spectra.size // PIECES
        ),
        name="whiten_piece",
    )(spectra, edges)


def cross_kernel(step, offsets, rank_ref, rows_ref, *refs):
    pieces, out_ref, wide_ref = refs[:PIECES], refs[PIECES], refs[PIECES + 1]
    sources, bins, width = rows_ref.shape
    windows = width // 2
    index = pl.program_id(0)

    @pl.when(index == 0)
    def _():
        for p, offset in enumerate(offsets):
            at = pl.multiple_of((rank_ref[0] ^ offset) * bins, bins)
            wide_ref[pl.ds(at, bins)] = rows_ref[p].astype(jnp.float32) * (1.0 / windows)

    sign = jnp.where(lax.broadcasted_iota(jnp.int32, (sources, width), 1) < windows, -1.0, 1.0)
    for k in range(step):
        f = index * step + k
        first = wide_ref[pl.ds(f, sources, stride=bins)]
        second = pltpu.roll(first, windows, 1) * sign
        left = jnp.concatenate([first, second], 0).astype(jnp.bfloat16)
        right = jnp.concatenate([piece[part, k] for part in range(2) for piece in pieces], 0)
        product = jnp.dot(left, right, preferred_element_type=jnp.float32).astype(jnp.bfloat16)
        out_ref[0, k] = product[:sources]
        out_ref[1, k] = product[sources:]


def cross_spectra(rows, offsets, rank, pieces):
    sources, bins, width = rows.shape
    channels = pieces[0].shape[-1]
    step = min(16, bins)
    return pl.pallas_call(
        functools.partial(cross_kernel, step, offsets),
        grid=(bins // step,),
        in_specs=[pl.BlockSpec(memory_space=pltpu.SMEM), pl.BlockSpec(rows.shape, lambda i: (0, 0, 0))]
        + [pl.BlockSpec((2, step, width // 2 // PIECES, channels), lambda i: (0, i, 0, 0))] * PIECES,
        out_specs=pl.BlockSpec((2, step, sources, channels), lambda i: (0, i, 0, 0)),
        out_shape=jax.ShapeDtypeStruct((2, bins, sources, channels), jnp.bfloat16),
        scratch_shapes=[pltpu.VMEM((sources * bins, width), jnp.float32)],
        compiler_params=pltpu.CompilerParams(vmem_limit_bytes=VMEM_LIMIT),
        name="cross_spectra",
    )(rank, rows, *pieces)


def gather_rows(row):
    count = lax.axis_size("rx")
    rank = lax.axis_index("rx")
    rows = row[None]
    bit = count // 2
    held = []
    while bit:
        other = lax.ppermute(rows, "rx", [(i, i ^ bit) for i in range(count)])
        rows = jnp.concatenate([rows, other], 0)
        held.append(bit)
        bit //= 2
    offsets = [sum(bit for k, bit in enumerate(held) if p >> k & 1) for p in range(count)]
    return rows, offsets


def local(spectra, source_index):
    channels_here = spectra.shape[3]
    rank = lax.axis_index("rx")
    column = lax.dynamic_slice(source_index, (rank,), (1,)) - rank * channels_here
    edges = edge_amplitudes(spectra)
    row = extract_row(spectra, column)
    rows, offsets = gather_rows(whiten_row(row, edges, column))
    pieces = [whiten_piece(spectra, edges, piece) for piece in range(PIECES)]
    return cross_spectra(rows, offsets, jnp.full((1,), rank, jnp.int32), pieces)


def solution(mesh):
    return jax.shard_map(
        local,
        mesh=mesh,
        in_specs=(P(None, "band", None, "rx"), P()),
        out_specs=P(None, "band", None, "rx"),
        check_vma=False,
    )
```

time: 61.6 us -> 37.6 us (0.61)
  blocking collectives: 25.6 us -> 0 us
  Pallas kernels: 0 us -> 15.8 us
  other arithmetic: 15.2 us -> 1.22 us
  local copies, waits for them, and re-layouts: 11 us -> 3.51 us
  waiting for transfers between devices: 0.83 us -> 7.16 us
  starting transfers between devices: 6.18 us -> 8.96 us
  matrix products: 1.77 us -> 0 us
    all_gather x1 -> x0, blocking collectives: 25.6 us -> none  [local(): collected = lax.all_gather(own_row, 'rx', axis=0, tiled=True)]
    pallas_call x0 -> x7, Pallas kernels: none -> 15.8 us  [the longest x1 6.23 us: extract_row(): pl.pallas_call(extract_kernel, grid=(bins // step,), in_specs=[pl.BlockSp...]
    ppermute x2 -> x5, waiting for transfers between devices: 0.83 us -> 7.16 us  [the longest x4 7.16 us: gather_rows(): other = lax.ppermute(rows, 'rx', [(i, i ^ bit) for i in range(count)])]
    convert_element_type x4 -> x1, other arithmetic: 6.18 us -> 1.01 us  [amplitude(): values = part.astype(jnp.float32)]
    add x1 -> x0, other arithmetic: 5.14 us -> none  [whiten(): smooth + 0.1]
    dynamic_slice x2 -> x1, local copies, waits for them, and re-layouts: 4.6 us -> 1.24 us  [local(): lax.dynamic_slice(source_index, (rank,), (1,)) - rank * channels_here]
    all_gather x1 -> x0, other arithmetic: 3.14 us -> none  [local(): collected = lax.all_gather(own_row, 'rx', axis=0, tiled=True)]
    ppermute x2 -> x5, starting transfers between devices: 6.18 us -> 8.96 us  [the longest x4 5.92 us: gather_rows(): other = lax.ppermute(rows, 'rx', [(i, i ^ bit) for i in range(count)])]
  transfers between devices with their start and end apart: 2 -> 5, of which waited for: 1 -> 3; matrix products, arithmetic and copies ran while one was open for 2% -> 3% of each run, Pallas kernels for 0% -> 28%
where the time goes in v1:
time: 37.6 us; the launch traced here: 37.4 us
  Pallas kernels  15.8 us (42%)
  starting transfers between devices  8.96 us (24%)
  waiting for transfers between devices  7.16 us (19%)
  local copies, waits for them, and re-layouts  3.51 us (9%)
  other arithmetic  1.22 us (3%)
  between operations  0.78 us (2%)
    ppermute x4, waiting for transfers between devices, gather_rows(): other = lax.ppermute(rows, 'rx', [(i, i ^ bit) for i in range(count)])  7.16 us
    pallas_call x1, Pallas kernels, extract_row(): pl.pallas_call(extract_kernel, grid=(bins // step,), in_specs=[pl.BlockSp...  6.23 us
    ppermute x4, starting transfers between devices, gather_rows(): other = lax.ppermute(rows, 'rx', [(i, i ^ bit) for i in range(count)])  5.92 us
    pallas_call x1, Pallas kernels, cross_spectra(): pl.pallas_call(functools.partial(cross_kernel, step, offsets), grid=(bins...  4.54 us
    pallas_call x4, Pallas kernels, whiten_piece(): pl.pallas_call(whiten_kernel, grid=(1,), in_specs=[pl.BlockSpec((2, bins,...  4.16 us
    ppermute x1, starting transfers between devices, edge_amplitudes(): lax.ppermute(jnp.where(rank == 0, last, first), 'band', [(0, 1), (1, 0)])  3.03 us
    unnamed x8, local copies, waits for them, and re-layouts  2.23 us
    dynamic_slice x1, local copies, waits for them, and re-layouts, local(): lax.dynamic_slice(source_index, (rank,), (1,)) - rank * channels_here  1.24 us
  transfers between devices with their start and end apart: 5, of which 3 were waited for; matrix products, arithmetic and copies ran while one was open for 3% of the time, Pallas kernels for 28%

profile of v1, /device:TPU:0, one launch (start us, length us, event | category | flops | bytes accessed | tf_op | source)
XLA Modules:
  0.0 37.4 jit_solution(15198928418903581817)
XLA Ops:
  0.0 1.0 %slice_convert_fusion = (f32[2,4,64,128]{3,2,1,0:T(8,128)S(1)}, f32[2,4,64,128]{3,2,1,0:T(8,128)S(1)}) fusion(bf16[2,128,64,128]{3,2,1,0:T(8,128)(2,1)} %spectra_ref.9), kind=kLoop, calls=%fused_computation.13 | loop fusion | flops 131072 | bytes 786432 | tf_op jit(solution)/shard_map/convert_element_type | solution.py:27
  1.0 0.1 fusion.7
  1.1 3.0 %collective-permute-start = (bf16[4,64,128]{2,1,0:T(8,128)(2,1)S(1)}, bf16[4,64,128]{2,1,0:T(8,128)(2,1)S(1)}, u32[]{:S(2)}, u32[]{:S(2)}) collective-permute-start(bf16[4,64,128]{2,1,0:T(8,128)(2,1)S(1)} %fusion.7), channel_id=1, source_target_pairs={{0,1},{1,0},{2,3},{3,2},{4,5},{5,4},{6,7},{7,6},{8,9},{9,8},{10,11... | collective-permute-start | bytes 196616 | tf_op jit(solution)/shard_map/ppermute | solution.py:33
  4.2 1.2 %dynamic_slice.3 = s32[1]{0:T(128)} dynamic-slice(s32[16]{0:T(128)} %param.3, s32[]{:T(128)S(6)} %select_n.21), dynamic_slice_sizes={1} | dynamic-slice | bytes 12 | tf_op jit(solution)/shard_map/dynamic_slice | solution.py:227
  6.1 0.0 copy-start
  6.1 2.2 %copy-done = bf16[2,128,64,128]{3,2,1,0:T(8,128)(2,1)S(1)} copy-done((bf16[2,128,64,128]{3,2,1,0:T(8,128)(2,1)S(1)}, bf16[2,128,64,128]{3,2,1,0:T(8,128)(2,1)}, u32[]{:S(2)}) %copy-start) | copy-done | bytes 4194328
  8.2 0.0 copy-start.1
  8.2 6.2 %extract_row.1.row_ref = bf16[128,128]{1,0:T(8,128)(2,1)S(1)} custom-call(s32[1]{0:T(128)S(6)} %sub.7.column_ref, bf16[2,128,64,128]{3,2,1,0:T(8,128)(2,1)S(1)} %copy-done), custom_call_target="tpu_custom_call" | custom-call | flops 33554432 | bytes 4194304 | tf_op jit(solution)/shard_map/extract_row/pallas_call | solution.py:69
  14.5 0.0 collective-permute-done
  14.6 0.8 %whiten_row.1 = bf16[128,128]{1,0:T(8,128)(2,1)S(1)} custom-call(s32[1]{0:T(128)S(6)} %sub.7.column_ref, bf16[128,128]{1,0:T(8,128)(2,1)S(1)} %extract_row.1.row_ref, bf16[2,4,64,128]{3,2,1,0:T(8,128)(2,1)S(1)} %pad_maximum_fusion.1.edge_ref), custom_call_target="tpu_custom_call" | custom-call | tf_op jit(solution)/shard_map/whiten_row/pallas_call | solution.py:107
  15.4 2.7 %collective-permute-start.1 = (bf16[1,128,128]{2,1,0:T(8,128)(2,1)S(1)}, bf16[1,128,128]{2,1,0:T(8,128)(2,1)S(1)}, u32[]{:S(2)}, u32[]{:S(2)}) collective-permute-start(bf16[1,128,128]{2,1,0:T(8,128)(2,1)S(1)} %bitcast.10), channel_id=1, source_target_pairs={{0,16},{2,18},{4,20},{6,22},{8,24},{10,26},{12,28},{14,30},{16,0},... | collective-permute-start | bytes 98312 | tf_op jit(solution)/shard_map/ppermute | solution.py:216
  18.0 2.2 %collective-permute-done.1 = bf16[1,128,128]{2,1,0:T(8,128)(2,1)S(1)} collective-permute-done((bf16[1,128,128]{2,1,0:T(8,128)(2,1)S(1)}, bf16[1,128,128]{2,1,0:T(8,128)(2,1)S(1)}, u32[]{:S(2)}, u32[]{:S(2)}) %collective-permute-start.1) | collective-permute-done | bytes 32800 | tf_op jit(solution)/shard_map/ppermute | solution.py:216
  20.3 1.6 %collective-permute-start.2 = (bf16[2,128,128]{2,1,0:T(8,128)(2,1)S(1)}, bf16[2,128,128]{2,1,0:T(8,128)(2,1)S(1)}, u32[]{:S(2)}, u32[]{:S(2)}) collective-permute-start(bf16[2,128,128]{2,1,0:T(8,128)(2,1)S(1)} %pad_maximum_fusion.3), channel_id=1, source_target_pairs={{0,8},{2,10},{4,12},{6,14},{8,0},{10,2},{12,4},{14,6},{16,24},{18,... | collective-permute-start | bytes 196616 | tf_op jit(solution)/shard_map/ppermute | solution.py:216
  21.9 0.0 copy-done.1
  21.9 1.0 %whiten_piece.7.refs_3_ = bf16[2,128,16,128]{3,2,1,0:T(8,128)(2,1)S(1)} custom-call(bf16[2,128,64,128]{3,2,1,0:T(8,128)(2,1)S(1)} %copy-done.1, bf16[2,4,64,128]{3,2,1,0:T(8,128)(2,1)S(1)} %pad_maximum_fusion.1.edge_ref), custom_call_target="tpu_custom_call" | custom-call | flops 10485760 | bytes 2097152 | tf_op jit(solution)/shard_map/whiten_piece/pallas_call | solution.py:150
  23.0 1.0 %whiten_piece.6.refs_2_ = bf16[2,128,16,128]{3,2,1,0:T(8,128)(2,1)S(1)} custom-call(bf16[2,128,64,128]{3,2,1,0:T(8,128)(2,1)S(1)} %copy-done.1, bf16[2,4,64,128]{3,2,1,0:T(8,128)(2,1)S(1)} %pad_maximum_fusion.1.edge_ref), custom_call_target="tpu_custom_call" | custom-call | flops 10485760 | bytes 2097152 | tf_op jit(solution)/shard_map/whiten_piece/pallas_call | solution.py:150
  24.0 1.0 %whiten_piece.5.refs_1_ = bf16[2,128,16,128]{3,2,1,0:T(8,128)(2,1)S(1)} custom-call(bf16[2,128,64,128]{3,2,1,0:T(8,128)(2,1)S(1)} %copy-done.1, bf16[2,4,64,128]{3,2,1,0:T(8,128)(2,1)S(1)} %pad_maximum_fusion.1.edge_ref), custom_call_target="tpu_custom_call" | custom-call | flops 10485760 | bytes 2097152 | tf_op jit(solution)/shard_map/whiten_piece/pallas_call | solution.py:150
  25.1 1.0 %whiten_piece.4.refs_0_ = bf16[2,128,16,128]{3,2,1,0:T(8,128)(2,1)S(1)} custom-call(bf16[2,128,64,128]{3,2,1,0:T(8,128)(2,1)S(1)} %copy-done.1, bf16[2,4,64,128]{3,2,1,0:T(8,128)(2,1)S(1)} %pad_maximum_fusion.1.edge_ref), custom_call_target="tpu_custom_call" | custom-call | flops 10485760 | bytes 2097152 | tf_op jit(solution)/shard_map/whiten_piece/pallas_call | solution.py:150
  26.1 0.0 collective-permute-done.2
  26.1 1.6 %collective-permute-start.3 = (bf16[4,128,128]{2,1,0:T(8,128)(2,1)S(1)}, bf16[4,128,128]{2,1,0:T(8,128)(2,1)S(1)}, u32[]{:S(2)}, u32[]{:S(2)}) collective-permute-start(bf16[4,128,128]{2,1,0:T(8,128)(2,1)S(1)} %pad_maximum_fusion.2), channel_id=1, source_target_pairs={{0,4},{2,6},{4,0},{6,2},{8,12},{10,14},{12,8},{14,10},{16,20},{18,... | collective-permute-start | bytes 393224 | tf_op jit(solution)/shard_map/ppermute | solution.py:216
  27.7 3.5 %collective-permute-done.3 = bf16[4,128,128]{2,1,0:T(8,128)(2,1)S(1)} collective-permute-done((bf16[4,128,128]{2,1,0:T(8,128)(2,1)S(1)}, bf16[4,128,128]{2,1,0:T(8,128)(2,1)S(1)}, u32[]{:S(2)}, u32[]{:S(2)}) %collective-permute-start.3) | collective-permute-done | bytes 131104 | tf_op jit(solution)/shard_map/ppermute | solution.py:216
  31.2 0.1 collective-permute-start.4
  31.3 1.5 %collective-permute-done.4 = bf16[8,128,128]{2,1,0:T(8,128)(2,1)S(1)} collective-permute-done((bf16[8,128,128]{2,1,0:T(8,128)(2,1)S(1)}, bf16[8,128,128]{2,1,0:T(8,128)(2,1)S(1)}, u32[]{:S(2)}, u32[]{:S(2)}) %collective-permute-start.4) | collective-permute-done | bytes 262176 | tf_op jit(solution)/shard_map/ppermute | solution.py:216
  32.8 4.5 %cross_spectra.1 = bf16[2,128,16,128]{3,2,1,0:T(8,128)(2,1)} custom-call(s32[1]{0:T(128)} %bitcast.rank_ref, bf16[16,128,128]{2,1,0:T(8,128)(2,1)S(1)} %constant_dynamic-update-slice_fusion.rows_ref, bf16[2,128,16,128]{3,2,1,0:T(8,128)(2,1)S(1)} %whiten_piece.4.refs_0_, bf16[2,128,16,128]{3,2,1,0:T(8,128)(2,1)S(1)} %whiten_piece.5.refs_1_, ...), custom_call_target="tpu_custom_call" | custom-call | tf_op jit(solution)/shard_map/cross_spectra/pallas_call | solution.py:196
  (10 shorter events, 0.2 us)
Async XLA Ops:
  1.1 13.3 %collective-permute-start = (bf16[4,64,128]{2,1,0:T(8,128)(2,1)S(1)}, bf16[4,64,128]{2,1,0:T(8,128)(2,1)S(1)}, u32[]{:S(2)}, u32[]{:S(2)}) collective-permute-start(bf16[4,64,128]{2,1,0:T(8,128)(2,1)S(1)} %fusion.7), channel_id=1, source_target_pairs={{0,1},{1,0},{2,3},{3,2},{4,5},{5,4},{6,7},{7,6},{8,9},{9,8},{10,11... | collective-permute-start | bytes 196616 | tf_op jit(solution)/shard_map/ppermute | solution.py:33
  6.1 2.2 %copy-start = (bf16[2,128,64,128]{3,2,1,0:T(8,128)(2,1)S(1)}, bf16[2,128,64,128]{3,2,1,0:T(8,128)(2,1)}, u32[]{:S(2)}) copy-start(bf16[2,128,64,128]{3,2,1,0:T(8,128)(2,1)} %spectra_ref.9) | copy-start | bytes 12582916
  8.2 13.7 %copy-start.1 = (bf16[2,128,64,128]{3,2,1,0:T(8,128)(2,1)S(1)}, bf16[2,128,64,128]{3,2,1,0:T(8,128)(2,1)}, u32[]{:S(2)}) copy-start(bf16[2,128,64,128]{3,2,1,0:T(8,128)(2,1)} %spectra_ref.9) | copy-start | bytes 12582916
  15.4 4.9 %collective-permute-start.1 = (bf16[1,128,128]{2,1,0:T(8,128)(2,1)S(1)}, bf16[1,128,128]{2,1,0:T(8,128)(2,1)S(1)}, u32[]{:S(2)}, u32[]{:S(2)}) collective-permute-start(bf16[1,128,128]{2,1,0:T(8,128)(2,1)S(1)} %bitcast.10), channel_id=1, source_target_pairs={{0,16},{2,18},{4,20},{6,22},{8,24},{10,26},{12,28},{14,30},{16,0},... | collective-permute-start | bytes 98312 | tf_op jit(solution)/shard_map/ppermute | solution.py:216
  20.3 5.8 %collective-permute-start.2 = (bf16[2,128,128]{2,1,0:T(8,128)(2,1)S(1)}, bf16[2,128,128]{2,1,0:T(8,128)(2,1)S(1)}, u32[]{:S(2)}, u32[]{:S(2)}) collective-permute-start(bf16[2,128,128]{2,1,0:T(8,128)(2,1)S(1)} %pad_maximum_fusion.3), channel_id=1, source_target_pairs={{0,8},{2,10},{4,12},{6,14},{8,0},{10,2},{12,4},{14,6},{16,24},{18,... | collective-permute-start | bytes 196616 | tf_op jit(solution)/shard_map/ppermute | solution.py:216
  26.1 5.0 %collective-permute-start.3 = (bf16[4,128,128]{2,1,0:T(8,128)(2,1)S(1)}, bf16[4,128,128]{2,1,0:T(8,128)(2,1)S(1)}, u32[]{:S(2)}, u32[]{:S(2)}) collective-permute-start(bf16[4,128,128]{2,1,0:T(8,128)(2,1)S(1)} %pad_maximum_fusion.2), channel_id=1, source_target_pairs={{0,4},{2,6},{4,0},{6,2},{8,12},{10,14},{12,8},{14,10},{16,20},{18,... | collective-permute-start | bytes 393224 | tf_op jit(solution)/shard_map/ppermute | solution.py:216
  31.2 1.6 %collective-permute-start.4 = (bf16[8,128,128]{2,1,0:T(8,128)(2,1)S(1)}, bf16[8,128,128]{2,1,0:T(8,128)(2,1)S(1)}, u32[]{:S(2)}, u32[]{:S(2)}) collective-permute-start(bf16[8,128,128]{2,1,0:T(8,128)(2,1)S(1)} %pad_maximum_fusion), channel_id=1, source_target_pairs={{0,2},{2,0},{4,6},{6,4},{8,10},{10,8},{12,14},{14,12},{16,18},{18,... | collective-permute-start | bytes 786440 | tf_op jit(solution)/shard_map/ppermute | solution.py:216

commit v2 on v0

v2 whole, which is shorter than its diff:
```python
import functools

import jax
import jax.numpy as jnp
from jax import lax
from jax.experimental import pallas as pl
from jax.experimental.pallas import tpu as pltpu
from jax.sharding import PartitionSpec as P

HALF = 4
SPAN = 2 * HALF + 1
FLOOR = 0.1
PIECES = 4
TINY = 1e-37
MIB = 1024 * 1024
VMEM = pl.BlockSpec(memory_space=pltpu.VMEM)
SMEM = pl.BlockSpec(memory_space=pltpu.SMEM)
HBM = pl.BlockSpec(memory_space=pltpu.HBM)


def params(mib=24):
    return pltpu.CompilerParams(vmem_limit_bytes=mib * MIB)


def amplitude_of(power):
    return (power * lax.rsqrt(jnp.maximum(power, TINY))).astype(jnp.bfloat16)


def dtype_of(shape, dtype=jnp.bfloat16):
    return jax.ShapeDtypeStruct(shape, dtype)


def edge_kernel(spectra_ref, *refs):
    outs, buffer, sem = refs[:-2], refs[-2], refs[-1]
    bins = spectra_ref.shape[1]
    for out in outs:
        if len(outs) == 2:
            start = bins - HALF if out is outs[0] else 0
        else:
            start = jnp.where(lax.axis_index("band") == 0, bins - HALF, 0)
        copy = pltpu.make_async_copy(spectra_ref.at[:, pl.ds(start, HALF)], buffer, sem)
        copy.start()
        copy.wait()
        real = buffer[0].astype(jnp.float32)
        imag = buffer[1].astype(jnp.float32)
        out[...] = amplitude_of(real * real + imag * imag)


def edge_amplitudes(spectra):
    count = lax.axis_size("band")
    _, _, windows, channels = spectra.shape
    ends = 1 if count == 2 else 2
    sent = pl.pallas_call(
        edge_kernel,
        in_specs=[HBM],
        out_specs=[VMEM] * ends,
        out_shape=[dtype_of((HALF, windows, channels))] * ends,
        scratch_shapes=[pltpu.VMEM((2, HALF, windows, channels), spectra.dtype), pltpu.SemaphoreType.DMA],
        compiler_params=params(48),
        name="edge_amplitude",
    )(spectra)
    if count == 2:
        received = lax.ppermute(sent[0], "band", [(0, 1), (1, 0)])
        return received, received
    below = lax.ppermute(sent[0], "band", [(i, i + 1) for i in range(count - 1)])
    above = lax.ppermute(sent[1], "band", [(i + 1, i) for i in range(count - 1)])
    return below, above


def inside(edge_refs, index):
    band, count = lax.axis_index("band"), lax.axis_size("band")
    below = edge_refs[0][index].astype(jnp.float32) * (band > 0).astype(jnp.float32)
    above = edge_refs[1][index].astype(jnp.float32) * (band < count - 1).astype(jnp.float32)
    return below, above


def select_column(column, blocks):
    lane = lax.broadcasted_iota(jnp.int32, (16, 256), 1)
    half = lax.broadcasted_iota(jnp.int32, (16, 256), 0) // 8
    picks = (lane == column + half * 128).astype(jnp.bfloat16)

    def scoped(*accumulators):
        for k, pair in enumerate(blocks):
            pltpu.matmul_push_rhs(jnp.concatenate(pair, 1), (k // 2) % 2, k % 2, transpose=True)
            pltpu.matmul_acc_lhs(accumulators[k], picks, load_staged_rhs=(k // 2) % 2)
        return [pltpu.matmul_pop(accumulator) for accumulator in accumulators]

    found = pl.run_scoped(scoped, *[pltpu.ACC(k % 2)((16, 256), jnp.float32) for k in range(len(blocks))])
    return [(both[:8], both[8:]) for both in found]


def rows_of(found, windows):
    left = lax.broadcasted_iota(jnp.int32, (8, 2 * windows), 1) < windows
    sublane = lax.broadcasted_iota(jnp.int32, (8, 2 * windows), 0)
    out = []
    for k in range(0, len(found), 2):
        total = jnp.zeros((8, 2 * windows), jnp.float32)
        for j in range(8):
            pair = found[k + j // 4]
            at = (j % 4) // 2 * 2 * windows
            real, imag = (part[:, at : at + 2 * windows] for part in pair)
            if j % 2 == 0:
                value = jnp.where(left, real, pltpu.roll(imag, windows, 1))
            else:
                value = jnp.where(left, pltpu.roll(real, windows, 1), imag)
            total = jnp.where(sublane == j, value, total)
        out.append(total)
    return out


def source_column(index_ref, channels):
    rank = lax.axis_index("rx")
    return index_ref[rank] - rank * channels


def extract_kernel(chunks, index_ref, spectra_ref, row_ref, total_ref, held_ref, amplitude_ref, sem):
    _, bins, windows, channels = spectra_ref.shape
    column = source_column(index_ref, channels)
    size = bins // chunks
    copies = []
    for k in range(chunks):
        part = (slice(None), pl.ds(k * size, size))
        copy = pltpu.make_async_copy(spectra_ref.at[part], held_ref.at[part], sem.at[k])
        copy.start()
        copies.append(copy)
    for k in range(chunks):
        copies[k].wait()
        blocks = []
        for f in range(k * size, (k + 1) * size, 4):
            blocks.append([held_ref[part, f : f + 4].reshape(4 * windows, channels) for part in range(2)])
        rows = rows_of(select_column(column, blocks), windows)
        row_ref[k * size : (k + 1) * size] = jnp.concatenate(rows, 0)
    values = row_ref[...]
    squares = values * values
    amplitude = amplitude_of(squares + pltpu.roll(squares, windows, 1)).astype(jnp.float32)
    amplitude_ref[0:8] = jnp.zeros((8, 2 * windows), jnp.float32)
    amplitude_ref[8 : bins + 8] = amplitude
    amplitude_ref[bins + 8 : bins + 16] = jnp.zeros((8, 2 * windows), jnp.float32)
    total = amplitude
    for k in range(1, HALF + 1):
        total = total + (amplitude_ref[8 - k : bins + 8 - k] + amplitude_ref[8 + k : bins + 8 + k])
    total_ref[...] = total


def extract_row(spectra, source_index):
    _, bins, windows, _ = spectra.shape
    chunks = min(8, bins // 8)
    return pl.pallas_call(
        functools.partial(extract_kernel, chunks),
        in_specs=[SMEM, HBM],
        out_specs=[VMEM] * 3,
        out_shape=[
            dtype_of((bins, 2 * windows), jnp.float32),
            dtype_of((bins, 2 * windows), jnp.float32),
            dtype_of(spectra.shape, spectra.dtype),
        ],
        scratch_shapes=[pltpu.VMEM((bins + 16, 2 * windows), jnp.float32), pltpu.SemaphoreType.DMA((chunks,))],
        compiler_params=params(48),
        cost_estimate=pl.CostEstimate(flops=0, bytes_accessed=4 * spectra.size, transcendentals=0),
        name="extract_row",
    )(source_index, spectra)


def whiten_row_kernel(index_ref, row_ref, total_ref, below_ref, above_ref, out_ref):
    bins, width = row_ref.shape
    _, windows, channels = below_ref.shape
    column = source_column(index_ref, channels)
    pair = [edge[...].reshape(HALF * windows, channels) for edge in (below_ref, above_ref)]
    ((below, above),) = select_column(column, [pair])
    band, count = lax.axis_index("band"), lax.axis_size("band")
    below = below * (band > 0).astype(jnp.float32)
    above = above * (band < count - 1).astype(jnp.float32)
    sublane = lax.broadcasted_iota(jnp.int32, (8, windows), 0)
    low = jnp.zeros((8, windows), jnp.float32)
    high = jnp.zeros((8, windows), jnp.float32)
    for j in range(HALF):
        part = slice(j * windows, (j + 1) * windows)
        low = low + jnp.where(sublane <= j, below[:, part], 0.0)
        high = high + jnp.where(sublane >= 8 - HALF + j, above[:, part], 0.0)
    low = jnp.concatenate([low, low], 1)
    high = jnp.concatenate([high, high], 1)
    total = jnp.concatenate([total_ref[:8] + low, total_ref[8 : bins - 8], total_ref[bins - 8 :] + high], 0)
    out_ref[0] = (row_ref[...] / (total * (1.0 / SPAN) + FLOOR)).astype(jnp.bfloat16)


def whiten_row(source_index, row, total, edges):
    return pl.pallas_call(
        whiten_row_kernel,
        in_specs=[SMEM] + [VMEM] * 4,
        out_specs=VMEM,
        out_shape=dtype_of((1,) + row.shape),
        compiler_params=params(),
        name="whiten_row",
    )(source_index, row, total, *edges)


def whiten_kernel(pieces, spectra_ref, below_ref, above_ref, *refs):
    outs, amplitude_ref = refs[-1 - len(pieces) : -1], refs[-1]
    bins = spectra_ref.shape[1]
    width = outs[0].shape[2]
    block = 16
    for piece, out_ref in zip(pieces, outs, strict=True):
        window = slice(piece * width, (piece + 1) * width)
        below, above = inside((below_ref, above_ref), (slice(None), window))
        amplitude_ref[0:HALF] = below
        amplitude_ref[bins + HALF : bins + 2 * HALF] = above

        @pl.loop(0, bins // block)
        def _(b):
            at = b * block
            real = spectra_ref[0, pl.ds(at, block), window].astype(jnp.float32)
            imag = spectra_ref[1, pl.ds(at, block), window].astype(jnp.float32)
            amplitude_ref[pl.ds(at + HALF, block)] = amplitude_of(real * real + imag * imag).astype(jnp.float32)

        @pl.loop(0, bins // block)
        def _(b):
            at = b * block
            one = [amplitude_ref[at + k] for k in range(block + 2 * HALF)]
            two = [one[k] + one[k + 1] for k in range(block + 2 * HALF - 1)]
            four = [two[k] + two[k + 2] for k in range(block + 2 * HALF - 3)]
            for k in range(block):
                total = (four[k] + four[k + 4]) + one[k + 8]
                scale = 1.0 / (total * (1.0 / SPAN) + FLOOR)
                for part in range(2):
                    value = spectra_ref[part, at + k, window].astype(jnp.float32)
                    out_ref[part, at + k] = (value * scale).astype(jnp.bfloat16)


def whiten_pieces(spectra, edges, pieces, after):
    _, bins, windows, channels = spectra.shape
    width = windows // PIECES
    share = len(pieces) * spectra.size // PIECES
    return pl.pallas_call(
        functools.partial(whiten_kernel, pieces),
        in_specs=[VMEM] * 4,
        out_specs=[VMEM] * len(pieces),
        out_shape=[dtype_of((2, bins, width, channels))] * len(pieces),
        scratch_shapes=[pltpu.VMEM((bins + 2 * HALF, width, channels), jnp.float32)],
        compiler_params=params(),
        cost_estimate=pl.CostEstimate(flops=20 * share, bytes_accessed=4 * share, transcendentals=share),
        name="whiten_windows",
    )(spectra, *edges, after)


def merge_kernel(mine_ref, other_ref, *refs):
    out_ref = refs[-1]
    rows = mine_ref.shape[0]
    out_ref[:rows] = mine_ref[...]
    out_ref[rows:] = other_ref[...]


def merge(mine, other, done):
    return pl.pallas_call(
        merge_kernel,
        in_specs=[VMEM] * (2 + len(done)),
        out_specs=VMEM,
        out_shape=dtype_of((2 * mine.shape[0],) + mine.shape[1:]),
        compiler_params=params(),
        name="merge_rows",
    )(mine, other, *done)


def cross_kernel(offsets, chunks, first_ref, second_ref, *refs):
    pieces, out_ref, wide_ref, buffer, sem = refs[:PIECES], *refs[PIECES:]
    half, bins, width = first_ref.shape
    windows = width // 2
    sources = 2 * half
    rank = lax.axis_index("rx")
    for p, offset in enumerate(offsets):
        at = pl.multiple_of((rank ^ offset) * bins, bins)
        row = first_ref[p] if p < half else second_ref[p - half]
        wide_ref[pl.ds(at, bins)] = row.astype(jnp.float32) * (1.0 / windows)
    sign = jnp.where(lax.broadcasted_iota(jnp.int32, (sources, width), 1) < windows, -1.0, 1.0)
    size = bins // chunks
    copies = []
    for chunk in range(chunks):
        for f in range(chunk * size, (chunk + 1) * size):
            first = wide_ref[pl.ds(f, sources, stride=bins)]
            second = pltpu.roll(first, windows, 1) * sign
            left = jnp.concatenate([first, second], 0).astype(jnp.bfloat16)
            right = jnp.concatenate([piece[part, f] for part in range(2) for piece in pieces], 0)
            product = jnp.dot(left, right, preferred_element_type=jnp.float32).astype(jnp.bfloat16)
            buffer[0, f] = product[:sources]
            buffer[1, f] = product[sources:]
        part = (slice(None), pl.ds(chunk * size, size))
        copy = pltpu.make_async_copy(buffer.at[part], out_ref.at[part], sem.at[chunk])
        copy.start()
        copies.append(copy)
    for copy in copies:
        copy.wait()


def cross_spectra(first, second, offsets, pieces):
    half, bins, width = first.shape
    sources = 2 * half
    channels = pieces[0].shape[-1]
    chunks = min(8, bins // 8)
    shape = (2, bins, sources, channels)
    return pl.pallas_call(
        functools.partial(cross_kernel, offsets, chunks),
        in_specs=[VMEM] * (2 + PIECES),
        out_specs=HBM,
        out_shape=dtype_of(shape),
        scratch_shapes=[
            pltpu.VMEM((sources * bins, width), jnp.float32),
            pltpu.VMEM(shape, jnp.bfloat16),
            pltpu.SemaphoreType.DMA((chunks,)),
        ],
        compiler_params=params(),
        name="cross_spectra",
    )(first, second, *pieces)


def local(spectra, source_index):
    edges = edge_amplitudes(spectra)
    row, total, held = extract_row(spectra, source_index)
    rows = whiten_row(source_index, row, total, edges)

    count = lax.axis_size("rx")
    bits = [1 << k for k in reversed(range(count.bit_length() - 1))]
    plan = {0: (0, 1), 1: (2, 3)}
    pieces = []
    other = None
    for step, bit in enumerate(bits):
        other = lax.ppermute(rows, "rx", [(i, i ^ bit) for i in range(count)])
        done = whiten_pieces(held, edges, plan[step], rows) if step in plan else []
        pieces += done
        if step < len(bits) - 1:
            rows = merge(rows, other, done)
    offsets = [sum(bit for k, bit in enumerate(bits) if p >> k & 1) for p in range(count)]
    return cross_spectra(rows, other, offsets, pieces)


def solution(mesh):
    def placed(spectra, source_index):
        with jax.sharding.use_abstract_mesh(mesh.abstract_mesh):
            return body(spectra, source_index)

    body = jax.shard_map(
        local,
        mesh=mesh,
        in_specs=(P(None, "band", None, "rx"), P()),
        out_specs=P(None, "band", None, "rx"),
        check_vma=False,
    )
    return placed
```

time: 61.6 us -> 28.7 us (0.47)
  blocking collectives: 25.6 us -> 0 us
  other arithmetic: 15.2 us -> 0 us
  Pallas kernels: 0 us -> 11.1 us
  local copies, waits for them, and re-layouts: 11 us -> 2.19 us
  waiting for transfers between devices: 0.83 us -> 6.26 us
  starting transfers between devices: 6.18 us -> 8.88 us
  matrix products: 1.77 us -> 0 us
  between operations: 0.83 us -> 0.05 us
    all_gather x1 -> x0, blocking collectives: 25.6 us -> none  [local(): collected = lax.all_gather(own_row, 'rx', axis=0, tiled=True)]
    pallas_call x0 -> x9, Pallas kernels: none -> 11.1 us  [the longest x1 4.4 us: extract_row(): pl.pallas_call(functools.partial(extract_kernel, chunks), in_specs=[SMEM,...]
    convert_element_type x4 -> x0, other arithmetic: 6.18 us -> none  [the longest x1 2.58 us: magnitude(): values = values_in.astype(jnp.float32)]
    ppermute x2 -> x5, waiting for transfers between devices: 0.83 us -> 6.26 us  [the longest x4 6.26 us: local(): other = lax.ppermute(rows, 'rx', [(i, i ^ bit) for i in range(count)])]
    add x1 -> x0, other arithmetic: 5.14 us -> none  [whiten(): smooth + 0.1]
    dynamic_slice x2 -> x0, local copies, waits for them, and re-layouts: 4.6 us -> none  [the longest x1 3.36 us: local(): lax.dynamic_slice_in_dim(whitened, local_column, 1, 3).reshape(1, -1)]
    all_gather x1 -> x0, other arithmetic: 3.14 us -> none  [local(): collected = lax.all_gather(own_row, 'rx', axis=0, tiled=True)]
    ppermute x2 -> x5, starting transfers between devices: 6.18 us -> 8.88 us  [the longest x4 5.85 us: local(): other = lax.ppermute(rows, 'rx', [(i, i ^ bit) for i in range(count)])]
  transfers between devices with their start and end apart: 2 -> 5, of which waited for: 1 -> 4; matrix products, arithmetic and copies ran while one was open for 2% -> 0% of each run, Pallas kernels for 0% -> 28%
where the time goes in v2:
time: 28.7 us; the launch traced here: 28.5 us
  Pallas kernels  11.1 us (39%)
  starting transfers between devices  8.88 us (31%)
  waiting for transfers between devices  6.26 us (22%)
  local copies, waits for them, and re-layouts  2.19 us (8%)
    ppermute x4, waiting for transfers between devices, local(): other = lax.ppermute(rows, 'rx', [(i, i ^ bit) for i in range(count)])  6.26 us
    ppermute x4, starting transfers between devices, local(): other = lax.ppermute(rows, 'rx', [(i, i ^ bit) for i in range(count)])  5.85 us
    pallas_call x1, Pallas kernels, extract_row(): pl.pallas_call(functools.partial(extract_kernel, chunks), in_specs=[SMEM,...  4.4 us
    pallas_call x2, Pallas kernels, whiten_pieces(): pl.pallas_call(functools.partial(whiten_kernel, pieces), in_specs=[VMEM]...  3.65 us
    ppermute x1, starting transfers between devices, edge_amplitudes(): received = lax.ppermute(sent[0], 'band', [(0, 1), (1, 0)])  3.03 us
    unnamed x4, local copies, waits for them, and re-layouts  2.19 us
    pallas_call x1, Pallas kernels, cross_spectra(): pl.pallas_call(functools.partial(cross_kernel, offsets, chunks), in_specs...  2.08 us
    pallas_call x1, Pallas kernels, whiten_row(): pl.pallas_call(whiten_row_kernel, in_specs=[SMEM] + [VMEM] * 4, out_specs...  0.86 us
  transfers between devices with their start and end apart: 5, of which 4 were waited for; matrix products, arithmetic and copies ran while one was open for 0% of the time, Pallas kernels for 28%

profile of v2, /device:TPU:0, one launch (start us, length us, event | category | flops | bytes accessed | tf_op | source)
XLA Modules:
  0.0 28.5 jit_solution(11801847271288383355)
XLA Ops:
  0.0 0.0 copy-start
  0.0 2.2 %copy-done = bf16[2,128,64,128]{3,2,1,0:T(8,128)(2,1)S(1)} copy-done((bf16[2,128,64,128]{3,2,1,0:T(8,128)(2,1)S(1)}, bf16[2,128,64,128]{3,2,1,0:T(8,128)(2,1)}, u32[]{:S(2)}) %copy-start) | copy-done | bytes 4194328
  2.2 0.0 copy-start.1
  2.2 0.1 edge_amplitude.1
  2.3 3.0 %collective-permute-start = (bf16[4,64,128]{2,1,0:T(8,128)(2,1)S(1)}, bf16[4,64,128]{2,1,0:T(8,128)(2,1)S(1)}, u32[]{:S(2)}, u32[]{:S(2)}) collective-permute-start(bf16[4,64,128]{2,1,0:T(8,128)(2,1)S(1)} %edge_amplitude.1), channel_id=1, source_target_pairs={{0,1},{1,0},{2,3},{3,2},{4,5},{5,4},{6,7},{7,6},{8,9},{9,8},{10,11... | collective-permute-start | bytes 196616 | tf_op jit(solution)/shard_map/ppermute | solution.py:63
  5.4 0.0 copy-done.1
  5.4 4.4 %extract_row.1 = (f32[128,128]{1,0:T(8,128)S(1)}, f32[128,128]{1,0:T(8,128)S(1)}, bf16[2,128,64,128]{3,2,1,0:T(8,128)(2,1)S(1)}) custom-call(s32[16]{0:T(128)S(1)} %copy-done.1, bf16[2,128,64,128]{3,2,1,0:T(8,128)(2,1)} %spectra_ref.3), custom_call_target="tpu_custom_call" | custom-call | bytes 8388608 | tf_op jit(solution)/shard_map/extract_row/pallas_call | solution.py:148
  9.8 0.0 collective-permute-done.below_ref.above_ref
  9.8 0.9 %whiten_row.1.refs_0_.mine_ref = bf16[1,128,128]{2,1,0:T(8,128)(2,1)S(1)} custom-call(s32[16]{0:T(128)S(1)} %copy-done.1, f32[128,128]{1,0:T(8,128)S(1)} %get-tuple-element.12.row_ref, f32[128,128]{1,0:T(8,128)S(1)} %get-tuple-element.13.total_ref, bf16[4,64,128]{2,1,0:T(8,128)(2,1)S(1)} %collective-permute-done.below_ref.above_ref, ...), custom_call_target="tpu_custom_call" | custom-call | tf_op jit(solution)/shard_map/whiten_row/pallas_call | solution.py:187
  10.6 2.6 %collective-permute-start.1 = (bf16[1,128,128]{2,1,0:T(8,128)(2,1)S(1)}, bf16[1,128,128]{2,1,0:T(8,128)(2,1)S(1)}, u32[]{:S(2)}, u32[]{:S(2)}) collective-permute-start(bf16[1,128,128]{2,1,0:T(8,128)(2,1)S(1)} %whiten_row.1.refs_0_.mine_ref), channel_id=1, source_target_pairs={{0,16},{2,18},{4,20},{6,22},{8,24},{10,26},{12,28},{14,30},{16,0},... | collective-permute-start | bytes 98312 | tf_op jit(solution)/shard_map/ppermute | solution.py:325
  13.3 1.8 %whiten_windows.2 = (bf16[2,128,16,128]{3,2,1,0:T(8,128)(2,1)S(1)}, bf16[2,128,16,128]{3,2,1,0:T(8,128)(2,1)S(1)}) custom-call(bf16[2,128,64,128]{3,2,1,0:T(8,128)(2,1)S(1)} %get-tuple-element.14.spectra_ref, bf16[4,64,128]{2,1,0:T(8,128)(2,1)S(1)} %collective-permute-done.below_ref.above_ref, ...), custom_call_target="tpu_custom_call" | custom-call | flops 20971520 | bytes 4194304 | tf_op jit(solution)/shard_map/whiten_windows/pallas_call | solution.py:233
  15.1 0.4 %collective-permute-done.1.other_ref = bf16[1,128,128]{2,1,0:T(8,128)(2,1)S(1)} collective-permute-done((bf16[1,128,128]{2,1,0:T(8,128)(2,1)S(1)}, bf16[1,128,128]{2,1,0:T(8,128)(2,1)S(1)}, u32[]{:S(2)}, u32[]{:S(2)}) %collective-permute-start.1) | collective-permute-done | bytes 32800 | tf_op jit(solution)/shard_map/ppermute | solution.py:325
  15.5 1.6 %collective-permute-start.2 = (bf16[2,128,128]{2,1,0:T(8,128)(2,1)S(1)}, bf16[2,128,128]{2,1,0:T(8,128)(2,1)S(1)}, u32[]{:S(2)}, u32[]{:S(2)}) collective-permute-start(bf16[2,128,128]{2,1,0:T(8,128)(2,1)S(1)} %merge_rows.3.refs_0_.mine_ref), channel_id=1, source_target_pairs={{0,8},{2,10},{4,12},{6,14},{8,0},{10,2},{12,4},{14,6},{16,24},{18,... | collective-permute-start | bytes 196616 | tf_op jit(solution)/shard_map/ppermute | solution.py:325
  17.1 1.8 %whiten_windows.3 = (bf16[2,128,16,128]{3,2,1,0:T(8,128)(2,1)S(1)}, bf16[2,128,16,128]{3,2,1,0:T(8,128)(2,1)S(1)}) custom-call(bf16[2,128,64,128]{3,2,1,0:T(8,128)(2,1)S(1)} %get-tuple-element.14.spectra_ref, bf16[4,64,128]{2,1,0:T(8,128)(2,1)S(1)} %collective-permute-done.below_ref.above_ref, ...), custom_call_target="tpu_custom_call" | custom-call | flops 20971520 | bytes 4194304 | tf_op jit(solution)/shard_map/whiten_windows/pallas_call | solution.py:233
  18.9 0.9 %collective-permute-done.2.other_ref = bf16[2,128,128]{2,1,0:T(8,128)(2,1)S(1)} collective-permute-done((bf16[2,128,128]{2,1,0:T(8,128)(2,1)S(1)}, bf16[2,128,128]{2,1,0:T(8,128)(2,1)S(1)}, u32[]{:S(2)}, u32[]{:S(2)}) %collective-permute-start.2) | collective-permute-done | bytes 65568 | tf_op jit(solution)/shard_map/ppermute | solution.py:325
  19.8 1.6 %collective-permute-start.3 = (bf16[4,128,128]{2,1,0:T(8,128)(2,1)S(1)}, bf16[4,128,128]{2,1,0:T(8,128)(2,1)S(1)}, u32[]{:S(2)}, u32[]{:S(2)}) collective-permute-start(bf16[4,128,128]{2,1,0:T(8,128)(2,1)S(1)} %merge_rows.4.mine_ref), channel_id=1, source_target_pairs={{0,4},{2,6},{4,0},{6,2},{8,12},{10,14},{12,8},{14,10},{16,20},{18,... | collective-permute-start | bytes 393224 | tf_op jit(solution)/shard_map/ppermute | solution.py:325
  21.3 3.5 %collective-permute-done.3.other_ref = bf16[4,128,128]{2,1,0:T(8,128)(2,1)S(1)} collective-permute-done((bf16[4,128,128]{2,1,0:T(8,128)(2,1)S(1)}, bf16[4,128,128]{2,1,0:T(8,128)(2,1)S(1)}, u32[]{:S(2)}, u32[]{:S(2)}) %collective-permute-start.3) | collective-permute-done | bytes 131104 | tf_op jit(solution)/shard_map/ppermute | solution.py:325
  24.8 0.1 collective-permute-start.4
  24.9 1.5 %collective-permute-done.4.second_ref = bf16[8,128,128]{2,1,0:T(8,128)(2,1)S(1)} collective-permute-done((bf16[8,128,128]{2,1,0:T(8,128)(2,1)S(1)}, bf16[8,128,128]{2,1,0:T(8,128)(2,1)S(1)}, u32[]{:S(2)}, u32[]{:S(2)}) %collective-permute-start.4) | collective-permute-done | bytes 262176 | tf_op jit(solution)/shard_map/ppermute | solution.py:325
  26.4 2.1 %cross_spectra.1 = bf16[2,128,16,128]{3,2,1,0:T(8,128)(2,1)} custom-call(bf16[8,128,128]{2,1,0:T(8,128)(2,1)S(1)} %merge_rows.5.first_ref, bf16[8,128,128]{2,1,0:T(8,128)(2,1)S(1)} %collective-permute-done.4.second_ref, bf16[2,128,16,128]{3,2,1,0:T(8,128)(2,1)S(1)} %get-tuple-element.15.refs_0_, bf16[2,128,16,128]{3,2,1,0:T(8,128)(2,1)S(1)} %get-tuple-element.16.refs_1_, ...), custom_call_target="tpu_custom_call" | custom-call | tf_op jit(solution)/shard_map/cross_spectra/pallas_call | solution.py:299
  (3 shorter events, 0.0 us)
Async XLA Ops:
  0.0 2.2 %copy-start = (bf16[2,128,64,128]{3,2,1,0:T(8,128)(2,1)S(1)}, bf16[2,128,64,128]{3,2,1,0:T(8,128)(2,1)}, u32[]{:S(2)}) copy-start(bf16[2,128,64,128]{3,2,1,0:T(8,128)(2,1)} %spectra_ref.3) | copy-start | bytes 12582916
  2.2 3.2 %copy-start.1 = (s32[16]{0:T(128)S(1)}, s32[16]{0:T(128)}, u32[]{:S(2)}) copy-start(s32[16]{0:T(128)} %index_ref.3) | copy-start | bytes 196
  2.3 7.4 %collective-permute-start = (bf16[4,64,128]{2,1,0:T(8,128)(2,1)S(1)}, bf16[4,64,128]{2,1,0:T(8,128)(2,1)S(1)}, u32[]{:S(2)}, u32[]{:S(2)}) collective-permute-start(bf16[4,64,128]{2,1,0:T(8,128)(2,1)S(1)} %edge_amplitude.1), channel_id=1, source_target_pairs={{0,1},{1,0},{2,3},{3,2},{4,5},{5,4},{6,7},{7,6},{8,9},{9,8},{10,11... | collective-permute-start | bytes 196616 | tf_op jit(solution)/shard_map/ppermute | solution.py:63
  10.6 4.9 %collective-permute-start.1 = (bf16[1,128,128]{2,1,0:T(8,128)(2,1)S(1)}, bf16[1,128,128]{2,1,0:T(8,128)(2,1)S(1)}, u32[]{:S(2)}, u32[]{:S(2)}) collective-permute-start(bf16[1,128,128]{2,1,0:T(8,128)(2,1)S(1)} %whiten_row.1.refs_0_.mine_ref), channel_id=1, source_target_pairs={{0,16},{2,18},{4,20},{6,22},{8,24},{10,26},{12,28},{14,30},{16,0},... | collective-permute-start | bytes 98312 | tf_op jit(solution)/shard_map/ppermute | solution.py:325
  15.5 4.3 %collective-permute-start.2 = (bf16[2,128,128]{2,1,0:T(8,128)(2,1)S(1)}, bf16[2,128,128]{2,1,0:T(8,128)(2,1)S(1)}, u32[]{:S(2)}, u32[]{:S(2)}) collective-permute-start(bf16[2,128,128]{2,1,0:T(8,128)(2,1)S(1)} %merge_rows.3.refs_0_.mine_ref), channel_id=1, source_target_pairs={{0,8},{2,10},{4,12},{6,14},{8,0},{10,2},{12,4},{14,6},{16,24},{18,... | collective-permute-start | bytes 196616 | tf_op jit(solution)/shard_map/ppermute | solution.py:325
  19.8 5.0 %collective-permute-start.3 = (bf16[4,128,128]{2,1,0:T(8,128)(2,1)S(1)}, bf16[4,128,128]{2,1,0:T(8,128)(2,1)S(1)}, u32[]{:S(2)}, u32[]{:S(2)}) collective-permute-start(bf16[4,128,128]{2,1,0:T(8,128)(2,1)S(1)} %merge_rows.4.mine_ref), channel_id=1, source_target_pairs={{0,4},{2,6},{4,0},{6,2},{8,12},{10,14},{12,8},{14,10},{16,20},{18,... | collective-permute-start | bytes 393224 | tf_op jit(solution)/shard_map/ppermute | solution.py:325
  24.8 1.6 %collective-permute-start.4 = (bf16[8,128,128]{2,1,0:T(8,128)(2,1)S(1)}, bf16[8,128,128]{2,1,0:T(8,128)(2,1)S(1)}, u32[]{:S(2)}, u32[]{:S(2)}) collective-permute-start(bf16[8,128,128]{2,1,0:T(8,128)(2,1)S(1)} %merge_rows.5.first_ref), channel_id=1, source_target_pairs={{0,2},{2,0},{4,6},{6,4},{8,10},{10,8},{12,14},{14,12},{16,18},{18,... | collective-permute-start | bytes 786440 | tf_op jit(solution)/shard_map/ppermute | solution.py:325

commit v3 on v2

--- a/solution.py
+++ b/solution.py
@@ -30,41 +30,57 @@
     return jax.ShapeDtypeStruct(shape, dtype)
 
 
-def edge_kernel(spectra_ref, *refs):
-    outs, buffer, sem = refs[:-2], refs[-2], refs[-1]
-    bins = spectra_ref.shape[1]
-    for out in outs:
-        if len(outs) == 2:
-            start = bins - HALF if out is outs[0] else 0
-        else:
-            start = jnp.where(lax.axis_index("band") == 0, bins - HALF, 0)
-        copy = pltpu.make_async_copy(spectra_ref.at[:, pl.ds(start, HALF)], buffer, sem)
+def edge_kernel(index_ref, spectra_ref, *refs):
+    *out_refs, picks_ref, buffer, scalars, sem, index_sem = refs
+    bins, channels = spectra_ref.shape[1], spectra_ref.shape[3]
+    index_copy = pltpu.make_async_copy(index_ref, scalars, index_sem)
+    index_copy.start()
+    if len(out_refs) == 1:
+        starts = [jnp.where(lax.axis_index("band") == 0, bins - HALF, 0)]
+    else:
+        starts = [bins - HALF, 0]
+    copies = []
+    for k, start in enumerate(starts):
+        copy = pltpu.make_async_copy(spectra_ref.at[:, pl.ds(start, HALF)], buffer.at[k], sem.at[k])
         copy.start()
-        copy.wait()
-        real = buffer[0].astype(jnp.float32)
-        imag = buffer[1].astype(jnp.float32)
-        out[...] = amplitude_of(real * real + imag * imag)
-
-
-def edge_amplitudes(spectra):
+        copies.append(copy)
+    index_copy.wait()
+    rank = lax.axis_index("rx")
+    column = scalars[rank] - rank * channels
+    lane = lax.broadcasted_iota(jnp.int32, (16, 256), 1)
+    half = lax.broadcasted_iota(jnp.int32, (16, 256), 0) // 8
+    picks_ref[...] = (lane == column + half * channels).astype(jnp.bfloat16)
+    for k, out_ref in enumerate(out_refs):
+        copies[k].wait()
+        real = buffer[k, 0].astype(jnp.float32)
+        imag = buffer[k, 1].astype(jnp.float32)
+        out_ref[...] = amplitude_of(real * real + imag * imag)
+
+
+def edge_amplitudes(spectra, source_index):
     count = lax.axis_size("band")
     _, _, windows, channels = spectra.shape
     ends = 1 if count == 2 else 2
-    sent = pl.pallas_call(
+    *sent, picks = pl.pallas_call(
         edge_kernel,
-        in_specs=[HBM],
-        out_specs=[VMEM] * ends,
-        out_shape=[dtype_of((HALF, windows, channels))] * ends,
-        scratch_shapes=[pltpu.VMEM((2, HALF, windows, channels), spectra.dtype), pltpu.SemaphoreType.DMA],
-        compiler_params=params(48),
+        in_specs=[HBM, HBM],
+        out_specs=[VMEM] * (ends + 1),
+        out_shape=[dtype_of((HALF, windows, channels))] * ends + [dtype_of((16, 256))],
+        scratch_shapes=[
+            pltpu.VMEM((ends, 2, HALF, windows, channels), spectra.dtype),
+            pltpu.SMEM(source_index.shape, source_index.dtype),
+            pltpu.SemaphoreType.DMA((ends,)),
+            pltpu.SemaphoreType.DMA,
+        ],
+        compiler_params=params(),
         name="edge_amplitude",
-    )(spectra)
+    )(source_index, spectra)
     if count == 2:
         received = lax.ppermute(sent[0], "band", [(0, 1), (1, 0)])
-        return received, received
+        return (received, received), picks
     below = lax.ppermute(sent[0], "band", [(i, i + 1) for i in range(count - 1)])
     above = lax.ppermute(sent[1], "band", [(i + 1, i) for i in range(count - 1)])
-    return below, above
+    return (below, above), picks
 
 
 def inside(edge_refs, index):
@@ -74,11 +90,7 @@
     return below, above
 
 
-def select_column(column, blocks):
-    lane = lax.broadcasted_iota(jnp.int32, (16, 256), 1)
-    half = lax.broadcasted_iota(jnp.int32, (16, 256), 0) // 8
-    picks = (lane == column + half * 128).astype(jnp.bfloat16)
-
+def select_column(picks, blocks):
     def scoped(*accumulators):
         for k, pair in enumerate(blocks):
             pltpu.matmul_push_rhs(jnp.concatenate(pair, 1), (k // 2) % 2, k % 2, transpose=True)
@@ -108,14 +120,9 @@
     return out
 
 
-def source_column(index_ref, channels):
-    rank = lax.axis_index("rx")
-    return index_ref[rank] - rank * channels
-
-
-def extract_kernel(chunks, index_ref, spectra_ref, row_ref, total_ref, held_ref, amplitude_ref, sem):
+def extract_kernel(chunks, picks_ref, spectra_ref, row_ref, total_ref, held_ref, amplitude_ref, sem):
     _, bins, windows, channels = spectra_ref.shape
-    column = source_column(index_ref, channels)
+    picks = picks_ref[...]
     size = bins // chunks
     copies = []
     for k in range(chunks):
@@ -128,7 +135,7 @@
         blocks = []
         for f in range(k * size, (k + 1) * size, 4):
             blocks.append([held_ref[part, f : f + 4].reshape(4 * windows, channels) for part in range(2)])
-        rows = rows_of(select_column(column, blocks), windows)
+        rows = rows_of(select_column(picks, blocks), windows)
         row_ref[k * size : (k + 1) * size] = jnp.concatenate(rows, 0)
     values = row_ref[...]
     squares = values * values
@@ -142,12 +149,12 @@
     total_ref[...] = total
 
 
-def extract_row(spectra, source_index):
+def extract_row(spectra, picks):
     _, bins, windows, _ = spectra.shape
-    chunks = min(8, bins // 8)
+    chunks = 2
     return pl.pallas_call(
         functools.partial(extract_kernel, chunks),
-        in_specs=[SMEM, HBM],
+        in_specs=[VMEM, HBM],
         out_specs=[VMEM] * 3,
         out_shape=[
             dtype_of((bins, 2 * windows), jnp.float32),
@@ -158,15 +165,14 @@
         compiler_params=params(48),
         cost_estimate=pl.CostEstimate(flops=0, bytes_accessed=4 * spectra.size, transcendentals=0),
         name="extract_row",
-    )(source_index, spectra)
-
-
-def whiten_row_kernel(index_ref, row_ref, total_ref, below_ref, above_ref, out_ref):
+    )(picks, spectra)
+
+
+def whiten_row_kernel(picks_ref, row_ref, total_ref, below_ref, above_ref, out_ref):
     bins, width = row_ref.shape
     _, windows, channels = below_ref.shape
-    column = source_column(index_ref, channels)
     pair = [edge[...].reshape(HALF * windows, channels) for edge in (below_ref, above_ref)]
-    ((below, above),) = select_column(column, [pair])
+    ((below, above),) = select_column(picks_ref[...], [pair])
     band, count = lax.axis_index("band"), lax.axis_size("band")
     below = below * (band > 0).astype(jnp.float32)
     above = above * (band < count - 1).astype(jnp.float32)
@@ -183,15 +189,15 @@
     out_ref[0] = (row_ref[...] / (total * (1.0 / SPAN) + FLOOR)).astype(jnp.bfloat16)
 
 
-def whiten_row(source_index, row, total, edges):
+def whiten_row(picks, row, total, edges):
     return pl.pallas_call(
         whiten_row_kernel,
-        in_specs=[SMEM] + [VMEM] * 4,
+        in_specs=[VMEM] * 5,
         out_specs=VMEM,
         out_shape=dtype_of((1,) + row.shape),
         compiler_params=params(),
         name="whiten_row",
-    )(source_index, row, total, *edges)
+    )(picks, row, total, *edges)
 
 
 def whiten_kernel(pieces, spectra_ref, below_ref, above_ref, *refs):
@@ -312,9 +318,11 @@
 
 
 def local(spectra, source_index):
-    edges = edge_amplitudes(spectra)
-    row, total, held = extract_row(spectra, source_index)
-    rows = whiten_row(source_index, row, total, edges)
+    spectra = pltpu.with_memory_space_constraint(spectra, pltpu.HBM)
+    source_index = pltpu.with_memory_space_constraint(source_index, pltpu.HBM)
+    edges, picks = edge_amplitudes(spectra, source_index)
+    row, total, held = extract_row(spectra, picks)
+    rows = whiten_row(picks, row, total, edges)
 
     count = lax.axis_size("rx")
     bits = [1 << k for k in reversed(range(count.bit_length() - 1))]

time: 28.7 us -> 25.5 us (0.89)
  local copies, waits for them, and re-layouts: 2.19 us -> 0 us
  Pallas kernels: 11.1 us -> 10.2 us
    unnamed x4 -> x0, local copies, waits for them, and re-layouts: 2.19 us -> none
    pallas_call x3, Pallas kernels: 5.38 us -> 4.46 us  [the longest x1 3.18 us: extract_row(): pl.pallas_call(functools.partial(extract_kernel, chunks), in_specs=[VMEM,...]
  transfers between devices with their start and end apart: 5 -> 5, of which waited for: 4 -> 4; matrix products, arithmetic and copies ran while one was open for 0% -> 0% of each run, Pallas kernels for 28% -> 27%
where the time goes in v3:
time: 25.5 us; the launch traced here: 25.4 us
  Pallas kernels  10.2 us (40%)
  starting transfers between devices  8.87 us (35%)
  waiting for transfers between devices  6.26 us (25%)
    ppermute x4, waiting for transfers between devices, local(): other = lax.ppermute(rows, 'rx', [(i, i ^ bit) for i in range(count)])  6.26 us
    ppermute x4, starting transfers between devices, local(): other = lax.ppermute(rows, 'rx', [(i, i ^ bit) for i in range(count)])  5.84 us
    pallas_call x2, Pallas kernels, whiten_pieces(): pl.pallas_call(functools.partial(whiten_kernel, pieces), in_specs=[VMEM]...  3.64 us
    pallas_call x1, Pallas kernels, extract_row(): pl.pallas_call(functools.partial(extract_kernel, chunks), in_specs=[VMEM,...  3.18 us
    ppermute x1, starting transfers between devices, edge_amplitudes(): received = lax.ppermute(sent[0], 'band', [(0, 1), (1, 0)])  3.03 us
    pallas_call x1, Pallas kernels, cross_spectra(): pl.pallas_call(functools.partial(cross_kernel, offsets, chunks), in_specs...  2.08 us
    pallas_call x1, Pallas kernels, edge_amplitudes(): pl.pallas_call(edge_kernel, in_specs=[HBM, HBM], out_specs=[VMEM] * (ends...  0.97 us
  transfers between devices with their start and end apart: 5, of which 4 were waited for; matrix products, arithmetic and copies ran while one was open for 0% of the time, Pallas kernels for 27%

profile of v3, /device:TPU:0, one launch (start us, length us, event | category | flops | bytes accessed | tf_op | source)
XLA Modules:
  0.0 25.4 jit_solution(501617172376287985)
XLA Ops:
  0.0 1.0 %edge_amplitude.1 = (bf16[4,64,128]{2,1,0:T(8,128)(2,1)S(1)}, bf16[16,256]{1,0:T(8,128)(2,1)S(1)}) custom-call(s32[16]{0:T(128)} %index_ref.1, bf16[2,128,64,128]{3,2,1,0:T(8,128)(2,1)} %spectra_ref.3), custom_call_target="tpu_custom_call" | custom-call | tf_op jit(solution)/shard_map/edge_amplitude/pallas_call | solution.py:64
  1.0 3.0 %collective-permute-start = (bf16[4,64,128]{2,1,0:T(8,128)(2,1)S(1)}, bf16[4,64,128]{2,1,0:T(8,128)(2,1)S(1)}, u32[]{:S(2)}, u32[]{:S(2)}) collective-permute-start(bf16[4,64,128]{2,1,0:T(8,128)(2,1)S(1)} %get-tuple-element.17), channel_id=1, source_target_pairs={{0,1},{1,0},{2,3},{3,2},{4,5},{5,4},{6,7},{7,6},{8,9},{9,8},{10,11... | collective-permute-start | bytes 196616 | tf_op jit(solution)/shard_map/ppermute | solution.py:79
  4.0 3.2 %extract_row.1 = (f32[128,128]{1,0:T(8,128)S(1)}, f32[128,128]{1,0:T(8,128)S(1)}, bf16[2,128,64,128]{3,2,1,0:T(8,128)(2,1)S(1)}) custom-call(bf16[16,256]{1,0:T(8,128)(2,1)S(1)} %get-tuple-element.14.picks_ref, bf16[2,128,64,128]{3,2,1,0:T(8,128)(2,1)} %spectra_ref.3), custom_call_target="tpu_custom_call" | custom-call | bytes 8388608 | tf_op jit(solution)/shard_map/extract_row/pallas_call | solution.py:155
  7.2 0.0 collective-permute-done.below_ref.above_ref
  7.2 0.3 %whiten_row.1.refs_0_.mine_ref = bf16[1,128,128]{2,1,0:T(8,128)(2,1)S(1)} custom-call(bf16[16,256]{1,0:T(8,128)(2,1)S(1)} %get-tuple-element.14.picks_ref, f32[128,128]{1,0:T(8,128)S(1)} %get-tuple-element.15.row_ref, f32[128,128]{1,0:T(8,128)S(1)} %get-tuple-element.16.total_ref, bf16[4,64,128]{2,1,0:T(8,128)(2,1)S(1)} %collective-permute-done.below_ref.above_ref, ...), custom_call_target="tpu_custom_call" | custom-call | tf_op jit(solution)/shard_map/whiten_row/pallas_call | solution.py:193
  7.5 2.6 %collective-permute-start.1 = (bf16[1,128,128]{2,1,0:T(8,128)(2,1)S(1)}, bf16[1,128,128]{2,1,0:T(8,128)(2,1)S(1)}, u32[]{:S(2)}, u32[]{:S(2)}) collective-permute-start(bf16[1,128,128]{2,1,0:T(8,128)(2,1)S(1)} %whiten_row.1.refs_0_.mine_ref), channel_id=1, source_target_pairs={{0,16},{2,18},{4,20},{6,22},{8,24},{10,26},{12,28},{14,30},{16,0},... | collective-permute-start | bytes 98312 | tf_op jit(solution)/shard_map/ppermute | solution.py:333
  10.2 1.8 %whiten_windows.2 = (bf16[2,128,16,128]{3,2,1,0:T(8,128)(2,1)S(1)}, bf16[2,128,16,128]{3,2,1,0:T(8,128)(2,1)S(1)}) custom-call(bf16[2,128,64,128]{3,2,1,0:T(8,128)(2,1)S(1)} %get-tuple-element.18.spectra_ref, bf16[4,64,128]{2,1,0:T(8,128)(2,1)S(1)} %collective-permute-done.below_ref.above_ref, ...), custom_call_target="tpu_custom_call" | custom-call | flops 20971520 | bytes 4194304 | tf_op jit(solution)/shard_map/whiten_windows/pallas_call | solution.py:239
  12.0 0.4 %collective-permute-done.1.other_ref = bf16[1,128,128]{2,1,0:T(8,128)(2,1)S(1)} collective-permute-done((bf16[1,128,128]{2,1,0:T(8,128)(2,1)S(1)}, bf16[1,128,128]{2,1,0:T(8,128)(2,1)S(1)}, u32[]{:S(2)}, u32[]{:S(2)}) %collective-permute-start.1) | collective-permute-done | bytes 32800 | tf_op jit(solution)/shard_map/ppermute | solution.py:333
  12.4 1.6 %collective-permute-start.2 = (bf16[2,128,128]{2,1,0:T(8,128)(2,1)S(1)}, bf16[2,128,128]{2,1,0:T(8,128)(2,1)S(1)}, u32[]{:S(2)}, u32[]{:S(2)}) collective-permute-start(bf16[2,128,128]{2,1,0:T(8,128)(2,1)S(1)} %merge_rows.3.refs_0_.mine_ref), channel_id=1, source_target_pairs={{0,8},{2,10},{4,12},{6,14},{8,0},{10,2},{12,4},{14,6},{16,24},{18,... | collective-permute-start | bytes 196616 | tf_op jit(solution)/shard_map/ppermute | solution.py:333
  14.0 1.8 %whiten_windows.3 = (bf16[2,128,16,128]{3,2,1,0:T(8,128)(2,1)S(1)}, bf16[2,128,16,128]{3,2,1,0:T(8,128)(2,1)S(1)}) custom-call(bf16[2,128,64,128]{3,2,1,0:T(8,128)(2,1)S(1)} %get-tuple-element.18.spectra_ref, bf16[4,64,128]{2,1,0:T(8,128)(2,1)S(1)} %collective-permute-done.below_ref.above_ref, ...), custom_call_target="tpu_custom_call" | custom-call | flops 20971520 | bytes 4194304 | tf_op jit(solution)/shard_map/whiten_windows/pallas_call | solution.py:239
  15.8 0.9 %collective-permute-done.2.other_ref = bf16[2,128,128]{2,1,0:T(8,128)(2,1)S(1)} collective-permute-done((bf16[2,128,128]{2,1,0:T(8,128)(2,1)S(1)}, bf16[2,128,128]{2,1,0:T(8,128)(2,1)S(1)}, u32[]{:S(2)}, u32[]{:S(2)}) %collective-permute-start.2) | collective-permute-done | bytes 65568 | tf_op jit(solution)/shard_map/ppermute | solution.py:333
  16.7 1.6 %collective-permute-start.3 = (bf16[4,128,128]{2,1,0:T(8,128)(2,1)S(1)}, bf16[4,128,128]{2,1,0:T(8,128)(2,1)S(1)}, u32[]{:S(2)}, u32[]{:S(2)}) collective-permute-start(bf16[4,128,128]{2,1,0:T(8,128)(2,1)S(1)} %merge_rows.4.mine_ref), channel_id=1, source_target_pairs={{0,4},{2,6},{4,0},{6,2},{8,12},{10,14},{12,8},{14,10},{16,20},{18,... | collective-permute-start | bytes 393224 | tf_op jit(solution)/shard_map/ppermute | solution.py:333
  18.2 3.5 %collective-permute-done.3.other_ref = bf16[4,128,128]{2,1,0:T(8,128)(2,1)S(1)} collective-permute-done((bf16[4,128,128]{2,1,0:T(8,128)(2,1)S(1)}, bf16[4,128,128]{2,1,0:T(8,128)(2,1)S(1)}, u32[]{:S(2)}, u32[]{:S(2)}) %collective-permute-start.3) | collective-permute-done | bytes 131104 | tf_op jit(solution)/shard_map/ppermute | solution.py:333
  21.7 0.1 collective-permute-start.4
  21.8 1.5 %collective-permute-done.4.second_ref = bf16[8,128,128]{2,1,0:T(8,128)(2,1)S(1)} collective-permute-done((bf16[8,128,128]{2,1,0:T(8,128)(2,1)S(1)}, bf16[8,128,128]{2,1,0:T(8,128)(2,1)S(1)}, u32[]{:S(2)}, u32[]{:S(2)}) %collective-permute-start.4) | collective-permute-done | bytes 262176 | tf_op jit(solution)/shard_map/ppermute | solution.py:333
  23.3 2.1 %cross_spectra.1 = bf16[2,128,16,128]{3,2,1,0:T(8,128)(2,1)} custom-call(bf16[8,128,128]{2,1,0:T(8,128)(2,1)S(1)} %merge_rows.5.first_ref, bf16[8,128,128]{2,1,0:T(8,128)(2,1)S(1)} %collective-permute-done.4.second_ref, bf16[2,128,16,128]{3,2,1,0:T(8,128)(2,1)S(1)} %get-tuple-element.19.refs_0_, bf16[2,128,16,128]{3,2,1,0:T(8,128)(2,1)S(1)} %get-tuple-element.20.refs_1_, ...), custom_call_target="tpu_custom_call" | custom-call | tf_op jit(solution)/shard_map/cross_spectra/pallas_call | solution.py:305
  (3 shorter events, 0.0 us)
Async XLA Ops:
  1.0 6.2 %collective-permute-start = (bf16[4,64,128]{2,1,0:T(8,128)(2,1)S(1)}, bf16[4,64,128]{2,1,0:T(8,128)(2,1)S(1)}, u32[]{:S(2)}, u32[]{:S(2)}) collective-permute-start(bf16[4,64,128]{2,1,0:T(8,128)(2,1)S(1)} %get-tuple-element.17), channel_id=1, source_target_pairs={{0,1},{1,0},{2,3},{3,2},{4,5},{5,4},{6,7},{7,6},{8,9},{9,8},{10,11... | collective-permute-start | bytes 196616 | tf_op jit(solution)/shard_map/ppermute | solution.py:79
  7.5 4.9 %collective-permute-start.1 = (bf16[1,128,128]{2,1,0:T(8,128)(2,1)S(1)}, bf16[1,128,128]{2,1,0:T(8,128)(2,1)S(1)}, u32[]{:S(2)}, u32[]{:S(2)}) collective-permute-start(bf16[1,128,128]{2,1,0:T(8,128)(2,1)S(1)} %whiten_row.1.refs_0_.mine_ref), channel_id=1, source_target_pairs={{0,16},{2,18},{4,20},{6,22},{8,24},{10,26},{12,28},{14,30},{16,0},... | collective-permute-start | bytes 98312 | tf_op jit(solution)/shard_map/ppermute | solution.py:333
  12.4 4.3 %collective-permute-start.2 = (bf16[2,128,128]{2,1,0:T(8,128)(2,1)S(1)}, bf16[2,128,128]{2,1,0:T(8,128)(2,1)S(1)}, u32[]{:S(2)}, u32[]{:S(2)}) collective-permute-start(bf16[2,128,128]{2,1,0:T(8,128)(2,1)S(1)} %merge_rows.3.refs_0_.mine_ref), channel_id=1, source_target_pairs={{0,8},{2,10},{4,12},{6,14},{8,0},{10,2},{12,4},{14,6},{16,24},{18,... | collective-permute-start | bytes 196616 | tf_op jit(solution)/shard_map/ppermute | solution.py:333
  16.7 5.0 %collective-permute-start.3 = (bf16[4,128,128]{2,1,0:T(8,128)(2,1)S(1)}, bf16[4,128,128]{2,1,0:T(8,128)(2,1)S(1)}, u32[]{:S(2)}, u32[]{:S(2)}) collective-permute-start(bf16[4,128,128]{2,1,0:T(8,128)(2,1)S(1)} %merge_rows.4.mine_ref), channel_id=1, source_target_pairs={{0,4},{2,6},{4,0},{6,2},{8,12},{10,14},{12,8},{14,10},{16,20},{18,... | collective-permute-start | bytes 393224 | tf_op jit(solution)/shard_map/ppermute | solution.py:333
  21.7 1.6 %collective-permute-start.4 = (bf16[8,128,128]{2,1,0:T(8,128)(2,1)S(1)}, bf16[8,128,128]{2,1,0:T(8,128)(2,1)S(1)}, u32[]{:S(2)}, u32[]{:S(2)}) collective-permute-start(bf16[8,128,128]{2,1,0:T(8,128)(2,1)S(1)} %merge_rows.5.first_ref), channel_id=1, source_target_pairs={{0,2},{2,0},{4,6},{6,4},{8,10},{10,8},{12,14},{14,12},{16,18},{18,... | collective-permute-start | bytes 786440 | tf_op jit(solution)/shard_map/ppermute | solution.py:333

commit v4 on v3

--- a/solution.py
+++ b/solution.py
@@ -248,34 +248,63 @@
     )(spectra, *edges, after)
 
 
-def merge_kernel(mine_ref, other_ref, *refs):
+def merge_kernel(count, *refs):
     out_ref = refs[-1]
-    rows = mine_ref.shape[0]
-    out_ref[:rows] = mine_ref[...]
-    out_ref[rows:] = other_ref[...]
-
-
-def merge(mine, other, done):
-    return pl.pallas_call(
-        merge_kernel,
-        in_specs=[VMEM] * (2 + len(done)),
+    at = 0
+    for ref in refs[:count]:
+        out_ref[at : at + ref.shape[0]] = ref[...]
+        at += ref.shape[0]
+
+
+def merge(blocks, done):
+    return pl.pallas_call(
+        functools.partial(merge_kernel, len(blocks)),
+        in_specs=[VMEM] * (len(blocks) + len(done)),
         out_specs=VMEM,
-        out_shape=dtype_of((2 * mine.shape[0],) + mine.shape[1:]),
+        out_shape=dtype_of((sum(block.shape[0] for block in blocks),) + blocks[0].shape[1:]),
         compiler_params=params(),
         name="merge_rows",
-    )(mine, other, *done)
-
-
-def cross_kernel(offsets, chunks, first_ref, second_ref, *refs):
-    pieces, out_ref, wide_ref, buffer, sem = refs[:PIECES], *refs[PIECES:]
-    half, bins, width = first_ref.shape
+    )(*blocks, *done)
+
+
+def gather_rows(row, whiten):
+    count = lax.axis_size("rx")
+    bits = [1 << k for k in reversed(range(count.bit_length() - 1))]
+    *far, near, across, core = bits
+
+    def send(rows, bit):
+        return lax.ppermute(rows, "rx", [(i, i ^ bit) for i in range(count)])
+
+    def shifted(offsets, bit):
+        return [offset ^ bit for offset in offsets]
+
+    rows, held, pieces = row, [0], []
+    for step, bit in enumerate(far):
+        other = send(rows, bit)
+        done = whiten((0, 1), rows) if step == 0 else []
+        pieces += done
+        rows = merge([rows, other], done)
+        held = held + shifted(held, bit)
+    others = [send(rows, bit) for bit in (near, across, near ^ across)]
+    done = whiten((2, 3), rows)
+    pieces += done
+    rows = merge([rows, *others], done)
+    held = held + shifted(held, near) + shifted(held, across) + shifted(shifted(held, near), across)
+    blocks = [rows, send(rows, core)]
+    offsets = held + shifted(held, core)
+    return blocks, offsets, pieces
+
+
+def cross_kernel(offsets, chunks, *refs):
+    blocks, pieces, (out_ref, wide_ref, buffer, sem) = refs[: -4 - PIECES], refs[-4 - PIECES : -4], refs[-4:]
+    sources = len(offsets)
+    _, bins, width = blocks[0].shape
     windows = width // 2
-    sources = 2 * half
     rank = lax.axis_index("rx")
-    for p, offset in enumerate(offsets):
+    rows = [(ref, k) for ref in blocks for k in range(ref.shape[0])]
+    for (ref, k), offset in zip(rows, offsets, strict=True):
         at = pl.multiple_of((rank ^ offset) * bins, bins)
-        row = first_ref[p] if p < half else second_ref[p - half]
-        wide_ref[pl.ds(at, bins)] = row.astype(jnp.float32) * (1.0 / windows)
+        wide_ref[pl.ds(at, bins)] = ref[k].astype(jnp.float32) * (1.0 / windows)
     sign = jnp.where(lax.broadcasted_iota(jnp.int32, (sources, width), 1) < windows, -1.0, 1.0)
     size = bins // chunks
     copies = []
@@ -296,15 +325,15 @@
         copy.wait()
 
 
-def cross_spectra(first, second, offsets, pieces):
-    half, bins, width = first.shape
-    sources = 2 * half
+def cross_spectra(blocks, offsets, pieces):
+    sources = len(offsets)
+    _, bins, width = blocks[0].shape
     channels = pieces[0].shape[-1]
     chunks = min(8, bins // 8)
     shape = (2, bins, sources, channels)
     return pl.pallas_call(
         functools.partial(cross_kernel, offsets, chunks),
-        in_specs=[VMEM] * (2 + PIECES),
+        in_specs=[VMEM] * (len(blocks) + PIECES),
         out_specs=HBM,
         out_shape=dtype_of(shape),
         scratch_shapes=[
@@ -314,7 +343,7 @@
         ],
         compiler_params=params(),
         name="cross_spectra",
-    )(first, second, *pieces)
+    )(*blocks, *pieces)
 
 
 def local(spectra, source_index):
@@ -324,19 +353,10 @@
     row, total, held = extract_row(spectra, picks)
     rows = whiten_row(picks, row, total, edges)
 
-    count = lax.axis_size("rx")
-    bits = [1 << k for k in reversed(range(count.bit_length() - 1))]
-    plan = {0: (0, 1), 1: (2, 3)}
-    pieces = []
-    other = None
-    for step, bit in enumerate(bits):
-        other = lax.ppermute(rows, "rx", [(i, i ^ bit) for i in range(count)])
-        done = whiten_pieces(held, edges, plan[step], rows) if step in plan else []
-        pieces += done
-        if step < len(bits) - 1:
-            rows = merge(rows, other, done)
-    offsets = [sum(bit for k, bit in enumerate(bits) if p >> k & 1) for p in range(count)]
-    return cross_spectra(rows, other, offsets, pieces)
+    def whiten(piece, after):
+        return whiten_pieces(held, edges, piece, after)
+
+    return cross_spectra(*gather_rows(rows, whiten))
 
 
 def solution(mesh):

time: 25.5 us -> 23.5 us (0.922)
  waiting for transfers between devices: 6.26 us -> 3.91 us
  starting transfers between devices: 8.87 us -> 9.23 us
    ppermute x4 -> x5, waiting for transfers between devices: 6.26 us -> 3.91 us  [send(): return lax.ppermute(rows, 'rx', [(i, i ^ bit) for i in range(count)])]
    ppermute x4 -> x5, starting transfers between devices: 5.84 us -> 6.2 us  [send(): return lax.ppermute(rows, 'rx', [(i, i ^ bit) for i in range(count)])]
  transfers between devices with their start and end apart: 5 -> 6, of which waited for: 4 -> 5; matrix products, arithmetic and copies ran while one was open for 0% -> 0% of each run, Pallas kernels for 27% -> 29%
where the time goes in v4:
time: 23.5 us; the launch traced here: 23.4 us
  Pallas kernels  10.2 us (43%)
  starting transfers between devices  9.23 us (39%)
  waiting for transfers between devices  3.91 us (17%)
    ppermute x5, starting transfers between devices, send(): return lax.ppermute(rows, 'rx', [(i, i ^ bit) for i in range(count)])  6.2 us
    ppermute x5, waiting for transfers between devices, send(): return lax.ppermute(rows, 'rx', [(i, i ^ bit) for i in range(count)])  3.91 us
    pallas_call x2, Pallas kernels, whiten_pieces(): pl.pallas_call(functools.partial(whiten_kernel, pieces), in_specs=[VMEM]...  3.64 us
    pallas_call x1, Pallas kernels, extract_row(): pl.pallas_call(functools.partial(extract_kernel, chunks), in_specs=[VMEM,...  3.18 us
    ppermute x1, starting transfers between devices, edge_amplitudes(): received = lax.ppermute(sent[0], 'band', [(0, 1), (1, 0)])  3.03 us
    pallas_call x1, Pallas kernels, cross_spectra(): pl.pallas_call(functools.partial(cross_kernel, offsets, chunks), in_specs...  2.08 us
    pallas_call x1, Pallas kernels, edge_amplitudes(): pl.pallas_call(edge_kernel, in_specs=[HBM, HBM], out_specs=[VMEM] * (ends...  0.97 us
  transfers between devices with their start and end apart: 6, of which 5 were waited for; matrix products, arithmetic and copies ran while one was open for 0% of the time, Pallas kernels for 29%

profile of v4, /device:TPU:0, one launch (start us, length us, event | category | flops | bytes accessed | tf_op | source)
XLA Modules:
  0.0 23.4 jit_solution(14229109195607038501)
XLA Ops:
  0.0 1.0 %edge_amplitude.1 = (bf16[4,64,128]{2,1,0:T(8,128)(2,1)S(1)}, bf16[16,256]{1,0:T(8,128)(2,1)S(1)}) custom-call(s32[16]{0:T(128)} %index_ref.1, bf16[2,128,64,128]{3,2,1,0:T(8,128)(2,1)} %spectra_ref.3), custom_call_target="tpu_custom_call" | custom-call | tf_op jit(solution)/shard_map/edge_amplitude/pallas_call | solution.py:64
  1.0 3.0 %collective-permute-start = (bf16[4,64,128]{2,1,0:T(8,128)(2,1)S(1)}, bf16[4,64,128]{2,1,0:T(8,128)(2,1)S(1)}, u32[]{:S(2)}, u32[]{:S(2)}) collective-permute-start(bf16[4,64,128]{2,1,0:T(8,128)(2,1)S(1)} %get-tuple-element.17), channel_id=1, source_target_pairs={{0,1},{1,0},{2,3},{3,2},{4,5},{5,4},{6,7},{7,6},{8,9},{9,8},{10,11... | collective-permute-start | bytes 196616 | tf_op jit(solution)/shard_map/ppermute | solution.py:79
  4.0 3.2 %extract_row.1 = (f32[128,128]{1,0:T(8,128)S(1)}, f32[128,128]{1,0:T(8,128)S(1)}, bf16[2,128,64,128]{3,2,1,0:T(8,128)(2,1)S(1)}) custom-call(bf16[16,256]{1,0:T(8,128)(2,1)S(1)} %get-tuple-element.14.picks_ref, bf16[2,128,64,128]{3,2,1,0:T(8,128)(2,1)} %spectra_ref.3), custom_call_target="tpu_custom_call" | custom-call | bytes 8388608 | tf_op jit(solution)/shard_map/extract_row/pallas_call | solution.py:155
  7.2 0.0 collective-permute-done.below_ref.above_ref
  7.2 0.3 %whiten_row.1.refs_0_ = bf16[1,128,128]{2,1,0:T(8,128)(2,1)S(1)} custom-call(bf16[16,256]{1,0:T(8,128)(2,1)S(1)} %get-tuple-element.14.picks_ref, f32[128,128]{1,0:T(8,128)S(1)} %get-tuple-element.15.row_ref, f32[128,128]{1,0:T(8,128)S(1)} %get-tuple-element.16.total_ref, bf16[4,64,128]{2,1,0:T(8,128)(2,1)S(1)} %collective-permute-done.below_ref.above_ref, ...), custom_call_target="tpu_custom_call" | custom-call | tf_op jit(solution)/shard_map/whiten_row/pallas_call | solution.py:193
  7.5 2.6 %collective-permute-start.1 = (bf16[1,128,128]{2,1,0:T(8,128)(2,1)S(1)}, bf16[1,128,128]{2,1,0:T(8,128)(2,1)S(1)}, u32[]{:S(2)}, u32[]{:S(2)}) collective-permute-start(bf16[1,128,128]{2,1,0:T(8,128)(2,1)S(1)} %whiten_row.1.refs_0_), channel_id=1, source_target_pairs={{0,16},{2,18},{4,20},{6,22},{8,24},{10,26},{12,28},{14,30},{16,0},... | collective-permute-start | bytes 98312 | tf_op jit(solution)/shard_map/ppermute | solution.py:276
  10.2 1.8 %whiten_windows.2 = (bf16[2,128,16,128]{3,2,1,0:T(8,128)(2,1)S(1)}, bf16[2,128,16,128]{3,2,1,0:T(8,128)(2,1)S(1)}) custom-call(bf16[2,128,64,128]{3,2,1,0:T(8,128)(2,1)S(1)} %get-tuple-element.18.spectra_ref, bf16[4,64,128]{2,1,0:T(8,128)(2,1)S(1)} %collective-permute-done.below_ref.above_ref, ...), custom_call_target="tpu_custom_call" | custom-call | flops 20971520 | bytes 4194304 | tf_op jit(solution)/shard_map/whiten_windows/pallas_call | solution.py:239
  12.0 0.4 %collective-permute-done.1.refs_1_ = bf16[1,128,128]{2,1,0:T(8,128)(2,1)S(1)} collective-permute-done((bf16[1,128,128]{2,1,0:T(8,128)(2,1)S(1)}, bf16[1,128,128]{2,1,0:T(8,128)(2,1)S(1)}, u32[]{:S(2)}, u32[]{:S(2)}) %collective-permute-start.1) | collective-permute-done | bytes 32800 | tf_op jit(solution)/shard_map/ppermute | solution.py:276
  12.4 2.5 %collective-permute-start.4 = (bf16[2,128,128]{2,1,0:T(8,128)(2,1)S(1)}, bf16[2,128,128]{2,1,0:T(8,128)(2,1)S(1)}, u32[]{:S(2)}, u32[]{:S(2)}) collective-permute-start(bf16[2,128,128]{2,1,0:T(8,128)(2,1)S(1)} %merge_rows.2.refs_0_), channel_id=1, source_target_pairs={{0,12},{2,14},{4,8},{6,10},{8,4},{10,6},{12,0},{14,2},{16,28},{18,... | collective-permute-start | bytes 196616 | tf_op jit(solution)/shard_map/ppermute | solution.py:276
  14.9 0.5 %collective-permute-start.3 = (bf16[2,128,128]{2,1,0:T(8,128)(2,1)S(1)}, bf16[2,128,128]{2,1,0:T(8,128)(2,1)S(1)}, u32[]{:S(2)}, u32[]{:S(2)}) collective-permute-start(bf16[2,128,128]{2,1,0:T(8,128)(2,1)S(1)} %merge_rows.2.refs_0_), channel_id=1, source_target_pairs={{0,4},{2,6},{4,0},{6,2},{8,12},{10,14},{12,8},{14,10},{16,20},{18,... | collective-permute-start | bytes 196616 | tf_op jit(solution)/shard_map/ppermute | solution.py:276
  15.4 0.4 %collective-permute-start.2 = (bf16[2,128,128]{2,1,0:T(8,128)(2,1)S(1)}, bf16[2,128,128]{2,1,0:T(8,128)(2,1)S(1)}, u32[]{:S(2)}, u32[]{:S(2)}) collective-permute-start(bf16[2,128,128]{2,1,0:T(8,128)(2,1)S(1)} %merge_rows.2.refs_0_), channel_id=1, source_target_pairs={{0,8},{2,10},{4,12},{6,14},{8,0},{10,2},{12,4},{14,6},{16,24},{18,... | collective-permute-start | bytes 196616 | tf_op jit(solution)/shard_map/ppermute | solution.py:276
  15.9 1.8 %whiten_windows.3 = (bf16[2,128,16,128]{3,2,1,0:T(8,128)(2,1)S(1)}, bf16[2,128,16,128]{3,2,1,0:T(8,128)(2,1)S(1)}) custom-call(bf16[2,128,64,128]{3,2,1,0:T(8,128)(2,1)S(1)} %get-tuple-element.18.spectra_ref, bf16[4,64,128]{2,1,0:T(8,128)(2,1)S(1)} %collective-permute-done.below_ref.above_ref, ...), custom_call_target="tpu_custom_call" | custom-call | flops 20971520 | bytes 4194304 | tf_op jit(solution)/shard_map/whiten_windows/pallas_call | solution.py:239
  17.7 0.1 collective-permute-done.4.refs_3_
  17.8 1.3 %collective-permute-done.3.refs_2_ = bf16[2,128,128]{2,1,0:T(8,128)(2,1)S(1)} collective-permute-done((bf16[2,128,128]{2,1,0:T(8,128)(2,1)S(1)}, bf16[2,128,128]{2,1,0:T(8,128)(2,1)S(1)}, u32[]{:S(2)}, u32[]{:S(2)}) %collective-permute-start.3) | collective-permute-done | bytes 65568 | tf_op jit(solution)/shard_map/ppermute | solution.py:276
  19.2 0.5 %collective-permute-done.2.refs_1_ = bf16[2,128,128]{2,1,0:T(8,128)(2,1)S(1)} collective-permute-done((bf16[2,128,128]{2,1,0:T(8,128)(2,1)S(1)}, bf16[2,128,128]{2,1,0:T(8,128)(2,1)S(1)}, u32[]{:S(2)}, u32[]{:S(2)}) %collective-permute-start.2) | collective-permute-done | bytes 65568 | tf_op jit(solution)/shard_map/ppermute | solution.py:276
  19.7 0.1 collective-permute-start.5
  19.8 1.5 %collective-permute-done.5.refs_1_ = bf16[8,128,128]{2,1,0:T(8,128)(2,1)S(1)} collective-permute-done((bf16[8,128,128]{2,1,0:T(8,128)(2,1)S(1)}, bf16[8,128,128]{2,1,0:T(8,128)(2,1)S(1)}, u32[]{:S(2)}, u32[]{:S(2)}) %collective-permute-start.5) | collective-permute-done | bytes 262176 | tf_op jit(solution)/shard_map/ppermute | solution.py:276
  21.3 2.1 %cross_spectra.1 = bf16[2,128,16,128]{3,2,1,0:T(8,128)(2,1)} custom-call(bf16[8,128,128]{2,1,0:T(8,128)(2,1)S(1)} %merge_rows.3.refs_0_, bf16[8,128,128]{2,1,0:T(8,128)(2,1)S(1)} %collective-permute-done.5.refs_1_, bf16[2,128,16,128]{3,2,1,0:T(8,128)(2,1)S(1)} %get-tuple-element.19.refs_2_, bf16[2,128,16,128]{3,2,1,0:T(8,128)(2,1)S(1)} %get-tuple-element.20.refs_3_, ...), custom_call_target="tpu_custom_call" | custom-call | tf_op jit(solution)/shard_map/cross_spectra/pallas_call | solution.py:334
  (2 shorter events, 0.0 us)
Async XLA Ops:
  1.0 6.2 %collective-permute-start = (bf16[4,64,128]{2,1,0:T(8,128)(2,1)S(1)}, bf16[4,64,128]{2,1,0:T(8,128)(2,1)S(1)}, u32[]{:S(2)}, u32[]{:S(2)}) collective-permute-start(bf16[4,64,128]{2,1,0:T(8,128)(2,1)S(1)} %get-tuple-element.17), channel_id=1, source_target_pairs={{0,1},{1,0},{2,3},{3,2},{4,5},{5,4},{6,7},{7,6},{8,9},{9,8},{10,11... | collective-permute-start | bytes 196616 | tf_op jit(solution)/shard_map/ppermute | solution.py:79
  7.5 4.9 %collective-permute-start.1 = (bf16[1,128,128]{2,1,0:T(8,128)(2,1)S(1)}, bf16[1,128,128]{2,1,0:T(8,128)(2,1)S(1)}, u32[]{:S(2)}, u32[]{:S(2)}) collective-permute-start(bf16[1,128,128]{2,1,0:T(8,128)(2,1)S(1)} %whiten_row.1.refs_0_), channel_id=1, source_target_pairs={{0,16},{2,18},{4,20},{6,22},{8,24},{10,26},{12,28},{14,30},{16,0},... | collective-permute-start | bytes 98312 | tf_op jit(solution)/shard_map/ppermute | solution.py:276
  12.4 5.4 %collective-permute-start.4 = (bf16[2,128,128]{2,1,0:T(8,128)(2,1)S(1)}, bf16[2,128,128]{2,1,0:T(8,128)(2,1)S(1)}, u32[]{:S(2)}, u32[]{:S(2)}) collective-permute-start(bf16[2,128,128]{2,1,0:T(8,128)(2,1)S(1)} %merge_rows.2.refs_0_), channel_id=1, source_target_pairs={{0,12},{2,14},{4,8},{6,10},{8,4},{10,6},{12,0},{14,2},{16,28},{18,... | collective-permute-start | bytes 196616 | tf_op jit(solution)/shard_map/ppermute | solution.py:276
  14.9 4.3 %collective-permute-start.3 = (bf16[2,128,128]{2,1,0:T(8,128)(2,1)S(1)}, bf16[2,128,128]{2,1,0:T(8,128)(2,1)S(1)}, u32[]{:S(2)}, u32[]{:S(2)}) collective-permute-start(bf16[2,128,128]{2,1,0:T(8,128)(2,1)S(1)} %merge_rows.2.refs_0_), channel_id=1, source_target_pairs={{0,4},{2,6},{4,0},{6,2},{8,12},{10,14},{12,8},{14,10},{16,20},{18,... | collective-permute-start | bytes 196616 | tf_op jit(solution)/shard_map/ppermute | solution.py:276
  15.4 4.3 %collective-permute-start.2 = (bf16[2,128,128]{2,1,0:T(8,128)(2,1)S(1)}, bf16[2,128,128]{2,1,0:T(8,128)(2,1)S(1)}, u32[]{:S(2)}, u32[]{:S(2)}) collective-permute-start(bf16[2,128,128]{2,1,0:T(8,128)(2,1)S(1)} %merge_rows.2.refs_0_), channel_id=1, source_target_pairs={{0,8},{2,10},{4,12},{6,14},{8,0},{10,2},{12,4},{14,6},{16,24},{18,... | collective-permute-start | bytes 196616 | tf_op jit(solution)/shard_map/ppermute | solution.py:276
  19.7 1.6 %collective-permute-start.5 = (bf16[8,128,128]{2,1,0:T(8,128)(2,1)S(1)}, bf16[8,128,128]{2,1,0:T(8,128)(2,1)S(1)}, u32[]{:S(2)}, u32[]{:S(2)}) collective-permute-start(bf16[8,128,128]{2,1,0:T(8,128)(2,1)S(1)} %merge_rows.3.refs_0_), channel_id=1, source_target_pairs={{0,2},{2,0},{4,6},{6,4},{8,10},{10,8},{12,14},{14,12},{16,18},{18,... | collective-permute-start | bytes 786440 | tf_op jit(solution)/shard_map/ppermute | solution.py:276

commit v5 on v4

v5 whole, which is shorter than its diff:
```python
import functools

import jax
import jax.numpy as jnp
from jax import lax
from jax.experimental import pallas as pl
from jax.experimental.pallas import tpu as pltpu
from jax.sharding import PartitionSpec as P

HALF = 4
SPAN = 2 * HALF + 1
FLOOR = 0.1
TINY = 1e-37
MIB = 1024 * 1024
VMEM = pl.BlockSpec(memory_space=pltpu.VMEM)
SMEM = pl.BlockSpec(memory_space=pltpu.SMEM)
HBM = pl.BlockSpec(memory_space=pltpu.HBM)


def params(mib=24):
    return pltpu.CompilerParams(vmem_limit_bytes=mib * MIB)


def amplitude_of(power):
    return (power * lax.rsqrt(jnp.maximum(power, TINY))).astype(jnp.bfloat16)


def dtype_of(shape, dtype=jnp.bfloat16):
    return jax.ShapeDtypeStruct(shape, dtype)


def edge_kernel(index_ref, spectra_ref, *refs):
    *out_refs, picks_ref, buffer, scalars, sem, index_sem = refs
    ends = len(out_refs) // 2
    bins, channels = spectra_ref.shape[1], spectra_ref.shape[3]
    index_copy = pltpu.make_async_copy(index_ref, scalars, index_sem)
    index_copy.start()
    if ends == 1:
        starts = [jnp.where(lax.axis_index("band") == 0, bins - HALF, 0)]
    else:
        starts = [bins - HALF, 0]
    copies = []
    for k, start in enumerate(starts):
        copy = pltpu.make_async_copy(spectra_ref.at[:, pl.ds(start, HALF)], buffer.at[k], sem.at[k])
        copy.start()
        copies.append(copy)
    index_copy.wait()
    rank = lax.axis_index("rx")
    column = scalars[rank] - rank * channels
    row = lax.broadcasted_iota(jnp.int32, (256, 256), 0)
    lane = lax.broadcasted_iota(jnp.int32, (256, 256), 1)
    picks_ref[...] = (row == jnp.where(lane < channels, column, column + channels)).astype(jnp.bfloat16)
    pick = (lax.broadcasted_iota(jnp.int32, (16, 256), 1) == column).astype(jnp.bfloat16)
    for k in range(ends):
        copies[k].wait()
        real = buffer[k, 0].astype(jnp.float32)
        imag = buffer[k, 1].astype(jnp.float32)
        amplitude = amplitude_of(real * real + imag * imag)
        out_refs[k][...] = amplitude
        rows = amplitude.reshape(256, channels)
        pltpu.matmul_push_rhs(jnp.concatenate([rows, rows], 1), 0, 0, transpose=True)

        def scoped(accumulator):
            pltpu.matmul_acc_lhs(accumulator, pick, load_staged_rhs=0)
            return pltpu.matmul_pop(accumulator)

        column_of = pl.run_scoped(scoped, pltpu.ACC(0)((16, 256), jnp.float32))
        out_refs[ends + k][...] = column_of.astype(jnp.bfloat16)


def edge_amplitudes(spectra, source_index):
    count = lax.axis_size("band")
    _, _, windows, channels = spectra.shape
    ends = 1 if count == 2 else 2
    *sent, picks = pl.pallas_call(
        edge_kernel,
        in_specs=[HBM, HBM],
        out_specs=[VMEM] * (2 * ends + 1),
        out_shape=[dtype_of((HALF, windows, channels))] * ends + [dtype_of((16, HALF * windows))] * ends + [dtype_of((256, 256))],
        scratch_shapes=[
            pltpu.VMEM((ends, 2, HALF, windows, channels), spectra.dtype),
            pltpu.SMEM(source_index.shape, source_index.dtype),
            pltpu.SemaphoreType.DMA((ends,)),
            pltpu.SemaphoreType.DMA,
        ],
        compiler_params=params(),
        name="edge_amplitude",
    )(source_index, spectra)
    return sent[:ends], band_neighbours(sent[ends:]), picks


def band_neighbours(ends):
    count = lax.axis_size("band")
    if count == 2:
        received = lax.ppermute(ends[0], "band", [(0, 1), (1, 0)])
        return received, received
    below = lax.ppermute(ends[0], "band", [(i, i + 1) for i in range(count - 1)])
    above = lax.ppermute(ends[1], "band", [(i + 1, i) for i in range(count - 1)])
    return below, above


def select_column(spectra_ref, picks, start, count, spread_ref):
    windows, channels = spectra_ref.shape[2:]
    lane = lax.broadcasted_iota(jnp.int32, (windows, 2 * windows), 1)
    row = lax.broadcasted_iota(jnp.int32, (windows, 2 * windows), 0)
    masks = (lane == row, lane == row + windows)

    def scoped(*accumulators):
        for k, accumulator in enumerate(accumulators):
            both = jnp.concatenate([spectra_ref[0, start + k], spectra_ref[1, start + k]], 1)
            pltpu.matmul_acc_lhs(accumulator, both, load_staged_rhs=0 if picks[k % 2] else None)
            picks[k % 2] = False
        return [pltpu.matmul_pop(accumulator) for accumulator in accumulators]

    found = pl.run_scoped(scoped, *[pltpu.ACC(k % 2)((windows, 256), jnp.float32) for k in range(count)])
    for k, both in enumerate(found):
        total = jnp.zeros((8, 2 * windows), jnp.float32)
        for w in range(0, windows, 8):
            for part, mask in enumerate(masks):
                total = jnp.where(mask[w : w + 8], both[w : w + 8, part * channels : (part + 1) * channels], total)
        spread_ref[(start + k) * 8 : (start + k + 1) * 8] = total


def extract_kernel(chunks, picks_ref, spectra_ref, row_ref, total_ref, held_ref, spread_ref, amplitude_ref, sem):
    _, bins, windows, channels = spectra_ref.shape
    size = bins // chunks
    copies = []
    for k in range(chunks):
        part = (slice(None), pl.ds(k * size, size))
        copy = pltpu.make_async_copy(spectra_ref.at[part], held_ref.at[part], sem.at[k])
        copy.start()
        copies.append(copy)
    for unit in range(2):
        pltpu.matmul_push_rhs(picks_ref[...], 0, unit)
    staged = [True, True]
    for k in range(chunks):
        copies[k].wait()
        for start in range(k * size, (k + 1) * size, 16):
            select_column(held_ref, staged, start, 16, spread_ref)
            for f in range(start, start + 16, 8):
                rows = [spread_ref[pl.ds(f * 8 + j, 8, stride=8)] for j in range(8)]
                row_ref[f : f + 8] = sum(rows[1:], rows[0])
    values = row_ref[...]
    squares = values * values
    amplitude = amplitude_of(squares + pltpu.roll(squares, windows, 1)).astype(jnp.float32)
    amplitude_ref[0:8] = jnp.zeros((8, 2 * windows), jnp.float32)
    amplitude_ref[8 : bins + 8] = amplitude
    amplitude_ref[bins + 8 : bins + 16] = jnp.zeros((8, 2 * windows), jnp.float32)
    total = amplitude
    for k in range(1, HALF + 1):
        total = total + (amplitude_ref[8 - k : bins + 8 - k] + amplitude_ref[8 + k : bins + 8 + k])
    total_ref[...] = total


def extract_row(spectra, picks):
    _, bins, windows, _ = spectra.shape
    chunks = min(4, bins // 16)
    return pl.pallas_call(
        functools.partial(extract_kernel, chunks),
        in_specs=[VMEM, HBM],
        out_specs=[VMEM] * 3,
        out_shape=[
            dtype_of((bins, 2 * windows), jnp.float32),
            dtype_of((bins, 2 * windows), jnp.float32),
            dtype_of(spectra.shape, spectra.dtype),
        ],
        scratch_shapes=[pltpu.VMEM((8 * bins, 2 * windows), jnp.float32), pltpu.VMEM((bins + 16, 2 * windows), jnp.float32), pltpu.SemaphoreType.DMA((chunks,))],
        compiler_params=params(),
        cost_estimate=pl.CostEstimate(flops=0, bytes_accessed=4 * spectra.size, transcendentals=0),
        name="extract_row",
    )(picks, spectra)


def whiten_row_kernel(row_ref, total_ref, below_ref, above_ref, out_ref):
    bins, width = row_ref.shape
    windows = width // 2
    band, count = lax.axis_index("band"), lax.axis_size("band")
    below = below_ref[...].astype(jnp.float32)[:8] * (band > 0).astype(jnp.float32)
    above = above_ref[...].astype(jnp.float32)[:8] * (band < count - 1).astype(jnp.float32)
    sublane = lax.broadcasted_iota(jnp.int32, (8, windows), 0)
    low = jnp.zeros((8, windows), jnp.float32)
    high = jnp.zeros((8, windows), jnp.float32)
    for j in range(HALF):
        part = slice(j * windows, (j + 1) * windows)
        low = low + jnp.where(sublane <= j, below[:, part], 0.0)
        high = high + jnp.where(sublane >= 8 - HALF + j, above[:, part], 0.0)
    low = jnp.concatenate([low, low], 1)
    high = jnp.concatenate([high, high], 1)
    total = jnp.concatenate([total_ref[:8] + low, total_ref[8 : bins - 8], total_ref[bins - 8 :] + high], 0)
    out_ref[0] = (row_ref[...] / (total * (1.0 / SPAN) + FLOOR)).astype(jnp.bfloat16)


def whiten_row(row, total, columns):
    return pl.pallas_call(
        whiten_row_kernel,
        in_specs=[VMEM] * 4,
        out_specs=VMEM,
        out_shape=dtype_of((1,) + row.shape),
        compiler_params=params(),
        name="whiten_row",
    )(row, total, *columns)


def amplitude_kernel(first, spectra_ref, *refs):
    out_ref = refs[-1]
    bins = spectra_ref.shape[1]
    block = 16

    @pl.loop(0, bins // block)
    def _(b):
        at = pl.ds(b * block, block)
        for w in range(0, out_ref.shape[1], 16):
            window = slice(first + w, first + w + 16)
            real = spectra_ref[0, at, window].astype(jnp.float32)
            imag = spectra_ref[1, at, window].astype(jnp.float32)
            out_ref[at, w : w + 16] = amplitude_of(real * real + imag * imag).astype(jnp.float32)


def amplitudes(spectra, half, after):
    _, bins, windows, channels = spectra.shape
    share = spectra.size // 4
    return pl.pallas_call(
        functools.partial(amplitude_kernel, half * windows // 2),
        in_specs=[VMEM] * 2,
        out_specs=VMEM,
        out_shape=dtype_of((bins, windows // 2, channels), jnp.float32),
        compiler_params=params(),
        cost_estimate=pl.CostEstimate(flops=10 * share, bytes_accessed=4 * share, transcendentals=share),
        name="amplitude",
    )(spectra, after)


def whiten_kernel(spectra_ref, first_ref, second_ref, below_ref, above_ref, *refs):
    out_ref = refs[-1]
    _, bins, windows, _ = spectra_ref.shape
    band, count = lax.axis_index("band"), lax.axis_size("band")
    has_below = (band > 0).astype(jnp.float32)
    has_above = (band < count - 1).astype(jnp.float32)
    block = 16
    blocks = bins // block

    def one_block(b, w):
        at = b * block
        window = slice(w, w + 16)
        amplitude_ref, inner = (first_ref, w) if w < windows // 2 else (second_ref, w - windows // 2)
        one = []
        for k in range(-HALF, block + HALF):
            if isinstance(b, int) and at + k < 0:
                one.append(below_ref[HALF + k, window].astype(jnp.float32) * has_below)
            elif isinstance(b, int) and at + k >= bins:
                one.append(above_ref[at + k - bins, window].astype(jnp.float32) * has_above)
            else:
                one.append(amplitude_ref[at + k, inner : inner + 16])
        two = [one[k] + one[k + 1] for k in range(block + 2 * HALF - 1)]
        four = [two[k] + two[k + 2] for k in range(block + 2 * HALF - 3)]
        for k in range(block):
            total = (four[k] + four[k + 4]) + one[k + 8]
            scale = 1.0 / (total * (1.0 / SPAN) + FLOOR)
            for part in range(2):
                value = spectra_ref[part, at + k, window].astype(jnp.float32)
                out_ref[part, at + k, window] = (value * scale).astype(jnp.bfloat16)

    for w in range(0, windows, 16):
        one_block(0, w)
        one_block(blocks - 1, w)

        @pl.loop(1, blocks - 1)
        def _(b):
            one_block(b, w)


def whiten(spectra, halves, edges, after):
    return pl.pallas_call(
        whiten_kernel,
        in_specs=[VMEM] * (5 + len(after)),
        out_specs=VMEM,
        out_shape=dtype_of(spectra.shape),
        compiler_params=params(),
        cost_estimate=pl.CostEstimate(flops=7 * spectra.size, bytes_accessed=2 * spectra.size, transcendentals=spectra.size // 2),
        name="whiten_windows",
    )(spectra, *halves, *edges, *after)


def merge_kernel(count, *refs):
    out_ref = refs[-1]
    at = 0
    for ref in refs[:count]:
        out_ref[at : at + ref.shape[0]] = ref[...]
        at += ref.shape[0]


def merge(blocks, done):
    return pl.pallas_call(
        functools.partial(merge_kernel, len(blocks)),
        in_specs=[VMEM] * (len(blocks) + len(done)),
        out_specs=VMEM,
        out_shape=dtype_of((sum(block.shape[0] for block in blocks),) + blocks[0].shape[1:]),
        compiler_params=params(),
        name="merge_rows",
    )(*blocks, *done)


def send(rows, bit):
    count = lax.axis_size("rx")
    return lax.ppermute(rows, "rx", [(i, i ^ bit) for i in range(count)])


def shifted(offsets, bit):
    return [offset ^ bit for offset in offsets]


def gather_rows(row, spectra, ends):
    count = lax.axis_size("rx")
    *far, near, across, core = [1 << k for k in reversed(range(count.bit_length() - 1))]
    rows, held = row, [0]
    for bit in far[:-1]:
        rows = merge([rows, send(rows, bit)], [])
        held = held + shifted(held, bit)
    far = far[-1]
    from_far = send(rows, far)
    first = amplitudes(spectra, 0, rows)
    edges = band_neighbours([merge([end], [rows]) for end in ends])
    rows = merge([rows, from_far], [first])
    held = held + shifted(held, far)
    others = [send(rows, bit) for bit in (near ^ across, across, near)]
    second = amplitudes(spectra, 1, rows)
    whitened = whiten(spectra, (first, second), edges, [rows])
    rows = merge([rows, *others], [whitened])
    held = held + shifted(held, near ^ across) + shifted(held, across) + shifted(held, near)
    return [rows, send(rows, core)], held + shifted(held, core), whitened


def cross_kernel(offsets, chunks, *refs):
    *blocks, white_ref, out_ref, wide_ref, buffer, sem = refs
    sources = len(offsets)
    _, bins, width = blocks[0].shape
    windows = width // 2
    rank = lax.axis_index("rx")
    rows = [(ref, k) for ref in blocks for k in range(ref.shape[0])]
    for (ref, k), offset in zip(rows, offsets, strict=True):
        at = pl.multiple_of((rank ^ offset) * bins, bins)
        wide_ref[pl.ds(at, bins)] = ref[k].astype(jnp.float32) * (1.0 / windows)
    sign = jnp.where(lax.broadcasted_iota(jnp.int32, (sources, width), 1) < windows, -1.0, 1.0)
    size = bins // chunks
    copies = []
    for chunk in range(chunks):
        for f in range(chunk * size, (chunk + 1) * size):
            first = wide_ref[pl.ds(f, sources, stride=bins)]
            second = pltpu.roll(first, windows, 1) * sign
            left = jnp.concatenate([first, second], 0).astype(jnp.bfloat16)
            right = jnp.concatenate([white_ref[0, f], white_ref[1, f]], 0)
            product = jnp.dot(left, right, preferred_element_type=jnp.float32).astype(jnp.bfloat16)
            buffer[0, f] = product[:sources]
            buffer[1, f] = product[sources:]
        part = (slice(None), pl.ds(chunk * size, size))
        copy = pltpu.make_async_copy(buffer.at[part], out_ref.at[part], sem.at[chunk])
        copy.start()
        copies.append(copy)
    for copy in copies:
        copy.wait()


def cross_spectra(blocks, offsets, whitened):
    sources = len(offsets)
    _, bins, width = blocks[0].shape
    channels = whitened.shape[-1]
    chunks = min(8, bins // 8)
    shape = (2, bins, sources, channels)
    return pl.pallas_call(
        functools.partial(cross_kernel, offsets, chunks),
        in_specs=[VMEM] * (len(blocks) + 1),
        out_specs=HBM,
        out_shape=dtype_of(shape),
        scratch_shapes=[
            pltpu.VMEM((sources * bins, width), jnp.float32),
            pltpu.VMEM(shape, jnp.bfloat16),
            pltpu.SemaphoreType.DMA((chunks,)),
        ],
        compiler_params=params(),
        name="cross_spectra",
    )(*blocks, whitened)


def local(spectra, source_index):
    ends, columns, picks = edge_amplitudes(
        pltpu.with_memory_space_constraint(spectra, pltpu.HBM),
        pltpu.with_memory_space_constraint(source_index, pltpu.HBM),
    )
    row, total, held = extract_row(spectra, picks)
    return cross_spectra(*gather_rows(whiten_row(row, total, columns), held, ends))


def solution(mesh):
    def placed(spectra, source_index):
        with jax.sharding.use_abstract_mesh(mesh.abstract_mesh):
            return body(spectra, source_index)

    body = jax.shard_map(
        local,
        mesh=mesh,
        in_specs=(P(None, "band", None, "rx"), P()),
        out_specs=P(None, "band", None, "rx"),
        check_vma=False,
    )
    return placed
```

time: 23.5 us -> 22.7 us (0.966)
  starting transfers between devices: 9.23 us -> 10.8 us
  waiting for transfers between devices: 3.91 us -> 2.62 us
  Pallas kernels: 10.2 us -> 9.08 us
    ppermute x1 -> x2, starting transfers between devices: 3.03 us -> 4.55 us  [band_neighbours(): received = lax.ppermute(ends[0], 'band', [(0, 1), (1, 0)])]
    ppermute x5, waiting for transfers between devices: 3.91 us -> 2.61 us  [send(): return lax.ppermute(rows, 'rx', [(i, i ^ bit) for i in range(count)])]
    pallas_call x1, Pallas kernels: 3.18 us -> 2.12 us  [extract_row(): pl.pallas_call(functools.partial(extract_kernel, chunks), in_specs=[VMEM,...]
    pallas_call x4 -> x5, Pallas kernels: 4.93 us -> 4.85 us  [the longest x1 1.97 us: whiten(): pl.pallas_call(whiten_kernel, in_specs=[VMEM] * (5 + len(after)), out_spe...]
  transfers between devices with their start and end apart: 6 -> 7, of which waited for: 5 -> 3; matrix products, arithmetic and copies ran while one was open for 0% -> 0% of each run, Pallas kernels for 29% -> 25%
where the time goes in v5:
time: 22.7 us; the launch traced here: 22.6 us
  starting transfers between devices  10.8 us (48%)
  Pallas kernels  9.08 us (40%)
  waiting for transfers between devices  2.62 us (12%)
    ppermute x5, starting transfers between devices, send(): return lax.ppermute(rows, 'rx', [(i, i ^ bit) for i in range(count)])  6.23 us
    ppermute x2, starting transfers between devices, band_neighbours(): received = lax.ppermute(ends[0], 'band', [(0, 1), (1, 0)])  4.55 us
    ppermute x5, waiting for transfers between devices, send(): return lax.ppermute(rows, 'rx', [(i, i ^ bit) for i in range(count)])  2.61 us
    pallas_call x1, Pallas kernels, extract_row(): pl.pallas_call(functools.partial(extract_kernel, chunks), in_specs=[VMEM,...  2.12 us
    pallas_call x1, Pallas kernels, cross_spectra(): pl.pallas_call(functools.partial(cross_kernel, offsets, chunks), in_specs...  2.08 us
    pallas_call x1, Pallas kernels, whiten(): pl.pallas_call(whiten_kernel, in_specs=[VMEM] * (5 + len(after)), out_spe...  1.97 us
    pallas_call x2, Pallas kernels, amplitudes(): pl.pallas_call(functools.partial(amplitude_kernel, half * windows // 2),...  1.45 us
    pallas_call x1, Pallas kernels, edge_amplitudes(): pl.pallas_call(edge_kernel, in_specs=[HBM, HBM], out_specs=[VMEM] * (2 *...  1.27 us
  transfers between devices with their start and end apart: 7, of which 3 were waited for; matrix products, arithmetic and copies ran while one was open for 0% of the time, Pallas kernels for 25%

profile of v5, /device:TPU:0, one launch (start us, length us, event | category | flops | bytes accessed | tf_op | source)
XLA Modules:
  0.0 22.6 jit_solution(15177952562894847245)
XLA Ops:
  0.0 0.0 copy-start
  0.0 1.3 %edge_amplitude.1 = (bf16[4,64,128]{2,1,0:T(8,128)(2,1)S(1)}, bf16[16,256]{1,0:T(8,128)(2,1)S(1)}, bf16[256,256]{1,0:T(8,128)(2,1)S(1)}) custom-call(s32[16]{0:T(128)} %index_ref.1, bf16[2,128,64,128]{3,2,1,0:T(8,128)(2,1)} %spectra_ref.3), custom_call_target="tpu_custom_call" | custom-call | tf_op jit(solution)/shard_map/edge_amplitude/pallas_call | solution.py:75
  1.3 3.0 %collective-permute-start = (bf16[16,256]{1,0:T(8,128)(2,1)S(1)}, bf16[16,256]{1,0:T(8,128)(2,1)S(1)}, u32[]{:S(2)}, u32[]{:S(2)}) collective-permute-start(bf16[16,256]{1,0:T(8,128)(2,1)S(1)} %get-tuple-element.14), channel_id=1, source_target_pairs={{0,1},{1,0},{2,3},{3,2},{4,5},{5,4},{6,7},{7,6},{8,9},{9,8},{10,11... | collective-permute-start | bytes 24584 | tf_op jit(solution)/shard_map/ppermute | solution.py:95
  4.3 0.0 copy-done
  4.3 2.1 %extract_row.1 = (f32[128,128]{1,0:T(8,128)S(1)}, f32[128,128]{1,0:T(8,128)S(1)}, bf16[2,128,64,128]{3,2,1,0:T(8,128)(2,1)S(1)}) custom-call(bf16[256,256]{1,0:T(8,128)(2,1)S(1)} %get-tuple-element.11.picks_ref, bf16[2,128,64,128]{3,2,1,0:T(8,128)(2,1)S(1)} %copy-done), custom_call_target="tpu_custom_call" | custom-call | bytes 8388608 | tf_op jit(solution)/shard_map/extract_row/pallas_call | solution.py:158
  6.4 0.0 collective-permute-done.below_ref.above_ref
  6.5 0.2 whiten_row.1.refs_0_.refs_1_
  6.6 2.6 %collective-permute-start.1 = (bf16[1,128,128]{2,1,0:T(8,128)(2,1)S(1)}, bf16[1,128,128]{2,1,0:T(8,128)(2,1)S(1)}, u32[]{:S(2)}, u32[]{:S(2)}) collective-permute-start(bf16[1,128,128]{2,1,0:T(8,128)(2,1)S(1)} %whiten_row.1.refs_0_.refs_1_), channel_id=1, source_target_pairs={{0,16},{2,18},{4,20},{6,22},{8,24},{10,26},{12,28},{14,30},{16,0},... | collective-permute-start | bytes 98312 | tf_op jit(solution)/shard_map/ppermute | solution.py:305
  9.2 1.5 %collective-permute-start.5 = (bf16[4,64,128]{2,1,0:T(8,128)(2,1)S(1)}, bf16[4,64,128]{2,1,0:T(8,128)(2,1)S(1)}, u32[]{:S(2)}, u32[]{:S(2)}) collective-permute-start(bf16[4,64,128]{2,1,0:T(8,128)(2,1)S(1)} %merge_rows.4), channel_id=1, source_target_pairs={{0,1},{1,0},{2,3},{3,2},{4,5},{5,4},{6,7},{7,6},{8,9},{9,8},{10,11... | collective-permute-start | bytes 196616 | tf_op jit(solution)/shard_map/ppermute | solution.py:95
  10.8 0.7 %amplitude.2.refs_2_.first_ref = f32[128,32,128]{2,1,0:T(8,128)S(1)} custom-call(bf16[2,128,64,128]{3,2,1,0:T(8,128)(2,1)S(1)} %get-tuple-element.15.spectra_ref, bf16[1,128,128]{2,1,0:T(8,128)(2,1)S(1)} %whiten_row.1.refs_0_.refs_1_), custom_call_target="tpu_custom_call" | custom-call | flops 5242880 | bytes 2097152 | tf_op jit(solution)/shard_map/amplitude/pallas_call | solution.py:222
  11.5 0.0 collective-permute-done.1.refs_1_
  11.5 2.6 %collective-permute-start.2 = (bf16[2,128,128]{2,1,0:T(8,128)(2,1)S(1)}, bf16[2,128,128]{2,1,0:T(8,128)(2,1)S(1)}, u32[]{:S(2)}, u32[]{:S(2)}) collective-permute-start(bf16[2,128,128]{2,1,0:T(8,128)(2,1)S(1)} %merge_rows.3.refs_0_), channel_id=1, source_target_pairs={{0,12},{2,14},{4,8},{6,10},{8,4},{10,6},{12,0},{14,2},{16,28},{18,... | collective-permute-start | bytes 196616 | tf_op jit(solution)/shard_map/ppermute | solution.py:305
  14.1 0.5 %collective-permute-start.3 = (bf16[2,128,128]{2,1,0:T(8,128)(2,1)S(1)}, bf16[2,128,128]{2,1,0:T(8,128)(2,1)S(1)}, u32[]{:S(2)}, u32[]{:S(2)}) collective-permute-start(bf16[2,128,128]{2,1,0:T(8,128)(2,1)S(1)} %merge_rows.3.refs_0_), channel_id=1, source_target_pairs={{0,4},{2,6},{4,0},{6,2},{8,12},{10,14},{12,8},{14,10},{16,20},{18,... | collective-permute-start | bytes 196616 | tf_op jit(solution)/shard_map/ppermute | solution.py:305
  14.6 0.4 %collective-permute-start.4 = (bf16[2,128,128]{2,1,0:T(8,128)(2,1)S(1)}, bf16[2,128,128]{2,1,0:T(8,128)(2,1)S(1)}, u32[]{:S(2)}, u32[]{:S(2)}) collective-permute-start(bf16[2,128,128]{2,1,0:T(8,128)(2,1)S(1)} %merge_rows.3.refs_0_), channel_id=1, source_target_pairs={{0,8},{2,10},{4,12},{6,14},{8,0},{10,2},{12,4},{14,6},{16,24},{18,... | collective-permute-start | bytes 196616 | tf_op jit(solution)/shard_map/ppermute | solution.py:305
  15.1 0.7 %amplitude.3.second_ref = f32[128,32,128]{2,1,0:T(8,128)S(1)} custom-call(bf16[2,128,64,128]{3,2,1,0:T(8,128)(2,1)S(1)} %get-tuple-element.15.spectra_ref, bf16[2,128,128]{2,1,0:T(8,128)(2,1)S(1)} %merge_rows.3.refs_0_), custom_call_target="tpu_custom_call" | custom-call | flops 5242880 | bytes 2097152 | tf_op jit(solution)/shard_map/amplitude/pallas_call | solution.py:222
  15.8 0.0 collective-permute-done.5.below_ref.above_ref
  15.8 2.0 %whiten_windows.1.refs_4_.refs_2_ = bf16[2,128,64,128]{3,2,1,0:T(8,128)(2,1)S(1)} custom-call(bf16[2,128,64,128]{3,2,1,0:T(8,128)(2,1)S(1)} %get-tuple-element.15.spectra_ref, f32[128,32,128]{2,1,0:T(8,128)S(1)} %amplitude.2.refs_2_.first_ref, f32[128,32,128]{2,1,0:T(8,128)S(1)} %amplitude.3.second_ref, ...), custom_call_target="tpu_custom_call" | custom-call | flops 14680064 | bytes 4194304 | tf_op jit(solution)/shard_map/whiten_windows/pallas_call | solution.py:273
  17.8 0.0 collective-permute-done.2.refs_1_
  17.8 0.6 %collective-permute-done.3.refs_2_ = bf16[2,128,128]{2,1,0:T(8,128)(2,1)S(1)} collective-permute-done((bf16[2,128,128]{2,1,0:T(8,128)(2,1)S(1)}, bf16[2,128,128]{2,1,0:T(8,128)(2,1)S(1)}, u32[]{:S(2)}, u32[]{:S(2)}) %collective-permute-start.3) | collective-permute-done | bytes 65568 | tf_op jit(solution)/shard_map/ppermute | solution.py:305
  18.3 0.5 %collective-permute-done.4.refs_3_ = bf16[2,128,128]{2,1,0:T(8,128)(2,1)S(1)} collective-permute-done((bf16[2,128,128]{2,1,0:T(8,128)(2,1)S(1)}, bf16[2,128,128]{2,1,0:T(8,128)(2,1)S(1)}, u32[]{:S(2)}, u32[]{:S(2)}) %collective-permute-start.4) | collective-permute-done | bytes 65568 | tf_op jit(solution)/shard_map/ppermute | solution.py:305
  18.9 0.1 collective-permute-start.6
  19.0 1.5 %collective-permute-done.6.refs_1_ = bf16[8,128,128]{2,1,0:T(8,128)(2,1)S(1)} collective-permute-done((bf16[8,128,128]{2,1,0:T(8,128)(2,1)S(1)}, bf16[8,128,128]{2,1,0:T(8,128)(2,1)S(1)}, u32[]{:S(2)}, u32[]{:S(2)}) %collective-permute-start.6) | collective-permute-done | bytes 262176 | tf_op jit(solution)/shard_map/ppermute | solution.py:305
  20.5 2.1 %cross_spectra.1 = bf16[2,128,16,128]{3,2,1,0:T(8,128)(2,1)} custom-call(bf16[8,128,128]{2,1,0:T(8,128)(2,1)S(1)} %merge_rows.5.refs_0_, bf16[8,128,128]{2,1,0:T(8,128)(2,1)S(1)} %collective-permute-done.6.refs_1_, bf16[2,128,64,128]{3,2,1,0:T(8,128)(2,1)S(1)} %whiten_windows.1.refs_4_.refs_2_), custom_call_target="tpu_custom_call" | custom-call | tf_op jit(solution)/shard_map/cross_spectra/pallas_call | solution.py:369
  (3 shorter events, 0.0 us)
Async XLA Ops:
  0.0 4.3 %copy-start = (bf16[2,128,64,128]{3,2,1,0:T(8,128)(2,1)S(1)}, bf16[2,128,64,128]{3,2,1,0:T(8,128)(2,1)}, u32[]{:S(2)}) copy-start(bf16[2,128,64,128]{3,2,1,0:T(8,128)(2,1)} %spectra_ref.3) | copy-start | bytes 12582916
  1.3 5.2 %collective-permute-start = (bf16[16,256]{1,0:T(8,128)(2,1)S(1)}, bf16[16,256]{1,0:T(8,128)(2,1)S(1)}, u32[]{:S(2)}, u32[]{:S(2)}) collective-permute-start(bf16[16,256]{1,0:T(8,128)(2,1)S(1)} %get-tuple-element.14), channel_id=1, source_target_pairs={{0,1},{1,0},{2,3},{3,2},{4,5},{5,4},{6,7},{7,6},{8,9},{9,8},{10,11... | collective-permute-start | bytes 24584 | tf_op jit(solution)/shard_map/ppermute | solution.py:95
  6.6 4.9 %collective-permute-start.1 = (bf16[1,128,128]{2,1,0:T(8,128)(2,1)S(1)}, bf16[1,128,128]{2,1,0:T(8,128)(2,1)S(1)}, u32[]{:S(2)}, u32[]{:S(2)}) collective-permute-start(bf16[1,128,128]{2,1,0:T(8,128)(2,1)S(1)} %whiten_row.1.refs_0_.refs_1_), channel_id=1, source_target_pairs={{0,16},{2,18},{4,20},{6,22},{8,24},{10,26},{12,28},{14,30},{16,0},... | collective-permute-start | bytes 98312 | tf_op jit(solution)/shard_map/ppermute | solution.py:305
  9.2 6.6 %collective-permute-start.5 = (bf16[4,64,128]{2,1,0:T(8,128)(2,1)S(1)}, bf16[4,64,128]{2,1,0:T(8,128)(2,1)S(1)}, u32[]{:S(2)}, u32[]{:S(2)}) collective-permute-start(bf16[4,64,128]{2,1,0:T(8,128)(2,1)S(1)} %merge_rows.4), channel_id=1, source_target_pairs={{0,1},{1,0},{2,3},{3,2},{4,5},{5,4},{6,7},{7,6},{8,9},{9,8},{10,11... | collective-permute-start | bytes 196616 | tf_op jit(solution)/shard_map/ppermute | solution.py:95
  11.5 6.3 %collective-permute-start.2 = (bf16[2,128,128]{2,1,0:T(8,128)(2,1)S(1)}, bf16[2,128,128]{2,1,0:T(8,128)(2,1)S(1)}, u32[]{:S(2)}, u32[]{:S(2)}) collective-permute-start(bf16[2,128,128]{2,1,0:T(8,128)(2,1)S(1)} %merge_rows.3.refs_0_), channel_id=1, source_target_pairs={{0,12},{2,14},{4,8},{6,10},{8,4},{10,6},{12,0},{14,2},{16,28},{18,... | collective-permute-start | bytes 196616 | tf_op jit(solution)/shard_map/ppermute | solution.py:305
  14.1 4.3 %collective-permute-start.3 = (bf16[2,128,128]{2,1,0:T(8,128)(2,1)S(1)}, bf16[2,128,128]{2,1,0:T(8,128)(2,1)S(1)}, u32[]{:S(2)}, u32[]{:S(2)}) collective-permute-start(bf16[2,128,128]{2,1,0:T(8,128)(2,1)S(1)} %merge_rows.3.refs_0_), channel_id=1, source_target_pairs={{0,4},{2,6},{4,0},{6,2},{8,12},{10,14},{12,8},{14,10},{16,20},{18,... | collective-permute-start | bytes 196616 | tf_op jit(solution)/shard_map/ppermute | solution.py:305
  14.6 4.3 %collective-permute-start.4 = (bf16[2,128,128]{2,1,0:T(8,128)(2,1)S(1)}, bf16[2,128,128]{2,1,0:T(8,128)(2,1)S(1)}, u32[]{:S(2)}, u32[]{:S(2)}) collective-permute-start(bf16[2,128,128]{2,1,0:T(8,128)(2,1)S(1)} %merge_rows.3.refs_0_), channel_id=1, source_target_pairs={{0,8},{2,10},{4,12},{6,14},{8,0},{10,2},{12,4},{14,6},{16,24},{18,... | collective-permute-start | bytes 196616 | tf_op jit(solution)/shard_map/ppermute | solution.py:305
  18.9 1.6 %collective-permute-start.6 = (bf16[8,128,128]{2,1,0:T(8,128)(2,1)S(1)}, bf16[8,128,128]{2,1,0:T(8,128)(2,1)S(1)}, u32[]{:S(2)}, u32[]{:S(2)}) collective-permute-start(bf16[8,128,128]{2,1,0:T(8,128)(2,1)S(1)} %merge_rows.5.refs_0_), channel_id=1, source_target_pairs={{0,2},{2,0},{4,6},{6,4},{8,10},{10,8},{12,14},{14,12},{16,18},{18,... | collective-permute-start | bytes 786440 | tf_op jit(solution)/shard_map/ppermute | solution.py:305

commit v6 on v5

--- a/solution.py
+++ b/solution.py
@@ -29,10 +29,16 @@
     return jax.ShapeDtypeStruct(shape, dtype)
 
 
+def window_masks(windows):
+    lane = lax.broadcasted_iota(jnp.int32, (windows, 2 * windows), 1)
+    row = lax.broadcasted_iota(jnp.int32, (windows, 2 * windows), 0)
+    return lane == row, lane == row + windows
+
+
 def edge_kernel(index_ref, spectra_ref, *refs):
-    *out_refs, picks_ref, buffer, scalars, sem, index_sem = refs
+    *out_refs, column_ref, scalars, sem, index_sem = refs
     ends = len(out_refs) // 2
-    bins, channels = spectra_ref.shape[1], spectra_ref.shape[3]
+    bins, windows, channels = spectra_ref.shape[1:]
     index_copy = pltpu.make_async_copy(index_ref, scalars, index_sem)
     index_copy.start()
     if ends == 1:
@@ -41,52 +47,70 @@
         starts = [bins - HALF, 0]
     copies = []
     for k, start in enumerate(starts):
-        copy = pltpu.make_async_copy(spectra_ref.at[:, pl.ds(start, HALF)], buffer.at[k], sem.at[k])
-        copy.start()
-        copies.append(copy)
+        for part in range(2):
+            for j in range(HALF):
+                copy = pltpu.make_async_copy(spectra_ref.at[part, start + j], out_refs[k].at[part, j], sem.at[len(copies)])
+                copy.start()
+                copies.append(copy)
     index_copy.wait()
     rank = lax.axis_index("rx")
-    column = scalars[rank] - rank * channels
-    row = lax.broadcasted_iota(jnp.int32, (256, 256), 0)
-    lane = lax.broadcasted_iota(jnp.int32, (256, 256), 1)
-    picks_ref[...] = (row == jnp.where(lane < channels, column, column + channels)).astype(jnp.bfloat16)
-    pick = (lax.broadcasted_iota(jnp.int32, (16, 256), 1) == column).astype(jnp.bfloat16)
+    column = jnp.full(column_ref.shape, scalars[rank] - rank * channels, jnp.int32)
+    column_ref[...] = column
+    masks = window_masks(windows)
     for k in range(ends):
-        copies[k].wait()
-        real = buffer[k, 0].astype(jnp.float32)
-        imag = buffer[k, 1].astype(jnp.float32)
-        amplitude = amplitude_of(real * real + imag * imag)
-        out_refs[k][...] = amplitude
-        rows = amplitude.reshape(256, channels)
-        pltpu.matmul_push_rhs(jnp.concatenate([rows, rows], 1), 0, 0, transpose=True)
-
-        def scoped(accumulator):
-            pltpu.matmul_acc_lhs(accumulator, pick, load_staged_rhs=0)
-            return pltpu.matmul_pop(accumulator)
-
-        column_of = pl.run_scoped(scoped, pltpu.ACC(0)((16, 256), jnp.float32))
-        out_refs[ends + k][...] = column_of.astype(jnp.bfloat16)
+        for copy in copies[2 * HALF * k : 2 * HALF * (k + 1)]:
+            copy.wait()
+        real = out_refs[k][0].astype(jnp.float32)
+        imag = out_refs[k][1].astype(jnp.float32)
+        amplitude = amplitude_of(real * real + imag * imag).astype(jnp.float32)
+        pairs = []
+        for first in range(0, HALF, 2):
+            total = jnp.zeros((8, 2 * windows), jnp.float32)
+            for w in range(0, windows, 8):
+                for part, mask in enumerate(masks):
+                    value = jnp.take_along_axis(amplitude[first + part, w : w + 8], column, axis=1, mode="promise_in_bounds")
+                    total = jnp.where(mask[w : w + 8], value, total)
+            pairs.append(total)
+        total = jnp.concatenate(pairs, 1)
+        out_refs[ends + k][...] = jnp.concatenate([total, total], 0).astype(jnp.bfloat16)
 
 
 def edge_amplitudes(spectra, source_index):
     count = lax.axis_size("band")
     _, _, windows, channels = spectra.shape
     ends = 1 if count == 2 else 2
-    *sent, picks = pl.pallas_call(
+    *sent, column = pl.pallas_call(
         edge_kernel,
         in_specs=[HBM, HBM],
         out_specs=[VMEM] * (2 * ends + 1),
-        out_shape=[dtype_of((HALF, windows, channels))] * ends + [dtype_of((16, HALF * windows))] * ends + [dtype_of((256, 256))],
+        out_shape=[dtype_of((2, HALF, windows, channels))] * ends + [dtype_of((16, HALF * windows))] * ends
+        + [dtype_of((8, channels), jnp.int32)],
         scratch_shapes=[
-            pltpu.VMEM((ends, 2, HALF, windows, channels), spectra.dtype),
             pltpu.SMEM(source_index.shape, source_index.dtype),
-            pltpu.SemaphoreType.DMA((ends,)),
+            pltpu.SemaphoreType.DMA((2 * HALF * ends,)),
             pltpu.SemaphoreType.DMA,
         ],
         compiler_params=params(),
         name="edge_amplitude",
     )(source_index, spectra)
-    return sent[:ends], band_neighbours(sent[ends:]), picks
+    return sent[:ends], band_neighbours(sent[ends:]), column
+
+
+def end_kernel(end_ref, after_ref, out_ref):
+    real = end_ref[0].astype(jnp.float32)
+    imag = end_ref[1].astype(jnp.float32)
+    out_ref[...] = amplitude_of(real * real + imag * imag)
+
+
+def end_amplitudes(end, after):
+    return pl.pallas_call(
+        end_kernel,
+        in_specs=[VMEM] * 2,
+        out_specs=VMEM,
+        out_shape=dtype_of(end.shape[1:]),
+        compiler_params=params(),
+        name="end_amplitude",
+    )(end, after)
 
 
 def band_neighbours(ends):
@@ -99,45 +123,48 @@
     return below, above
 
 
-def select_column(spectra_ref, picks, start, count, spread_ref):
+def select_column(spectra_ref, column, staged, start, count, spread_ref):
     windows, channels = spectra_ref.shape[2:]
-    lane = lax.broadcasted_iota(jnp.int32, (windows, 2 * windows), 1)
-    row = lax.broadcasted_iota(jnp.int32, (windows, 2 * windows), 0)
-    masks = (lane == row, lane == row + windows)
+    masks = window_masks(windows)
+    halves = count // 2
 
     def scoped(*accumulators):
         for k, accumulator in enumerate(accumulators):
             both = jnp.concatenate([spectra_ref[0, start + k], spectra_ref[1, start + k]], 1)
-            pltpu.matmul_acc_lhs(accumulator, both, load_staged_rhs=0 if picks[k % 2] else None)
-            picks[k % 2] = False
+            pltpu.matmul_acc_lhs(accumulator, both, load_staged_rhs=0 if staged[k % 2] else None)
+            staged[k % 2] = False
         return [pltpu.matmul_pop(accumulator) for accumulator in accumulators]
 
-    found = pl.run_scoped(scoped, *[pltpu.ACC(k % 2)((windows, 256), jnp.float32) for k in range(count)])
-    for k, both in enumerate(found):
+    found = pl.run_scoped(scoped, *[pltpu.ACC(k % 2)((windows, 256), jnp.float32) for k in range(halves)])
+    for k in range(count):
         total = jnp.zeros((8, 2 * windows), jnp.float32)
+        if k >= halves:
+            values = [spectra_ref[part, start + k].astype(jnp.float32) for part in range(2)]
         for w in range(0, windows, 8):
             for part, mask in enumerate(masks):
-                total = jnp.where(mask[w : w + 8], both[w : w + 8, part * channels : (part + 1) * channels], total)
+                if k < halves:
+                    value = found[k][w : w + 8, part * channels : (part + 1) * channels]
+                else:
+                    value = jnp.take_along_axis(values[part][w : w + 8], column, axis=1, mode="promise_in_bounds")
+                total = jnp.where(mask[w : w + 8], value, total)
         spread_ref[(start + k) * 8 : (start + k + 1) * 8] = total
 
 
-def extract_kernel(chunks, picks_ref, spectra_ref, row_ref, total_ref, held_ref, spread_ref, amplitude_ref, sem):
+def extract_kernel(chunks, column_ref, spectra_ref, row_ref, total_ref, spread_ref, amplitude_ref):
     _, bins, windows, channels = spectra_ref.shape
     size = bins // chunks
-    copies = []
+    column = column_ref[...]
+    wide = jnp.concatenate([column] * (256 // 8), 0)
+    row = lax.broadcasted_iota(jnp.int32, (256, channels), 0)
+    picks = jnp.concatenate([(row == wide + part * channels).astype(jnp.bfloat16) for part in range(2)], 1)
+    for unit in range(2):
+        pltpu.matmul_push_rhs(picks, 0, unit)
+    staged = [True, True]
+    group = min(64, size)
     for k in range(chunks):
-        part = (slice(None), pl.ds(k * size, size))
-        copy = pltpu.make_async_copy(spectra_ref.at[part], held_ref.at[part], sem.at[k])
-        copy.start()
-        copies.append(copy)
-    for unit in range(2):
-        pltpu.matmul_push_rhs(picks_ref[...], 0, unit)
-    staged = [True, True]
-    for k in range(chunks):
-        copies[k].wait()
-        for start in range(k * size, (k + 1) * size, 16):
-            select_column(held_ref, staged, start, 16, spread_ref)
-            for f in range(start, start + 16, 8):
+        for start in range(k * size, (k + 1) * size, group):
+            select_column(spectra_ref, column, staged, start, group, spread_ref)
+            for f in range(start, start + group, 8):
                 rows = [spread_ref[pl.ds(f * 8 + j, 8, stride=8)] for j in range(8)]
                 row_ref[f : f + 8] = sum(rows[1:], rows[0])
     values = row_ref[...]
@@ -152,31 +179,30 @@
     total_ref[...] = total
 
 
-def extract_row(spectra, picks):
+def extract_row(spectra, column):
     _, bins, windows, _ = spectra.shape
-    chunks = min(4, bins // 16)
+    chunks = max(bins // 64, 1)
     return pl.pallas_call(
         functools.partial(extract_kernel, chunks),
-        in_specs=[VMEM, HBM],
-        out_specs=[VMEM] * 3,
+        in_specs=[VMEM] * 2,
+        out_specs=[VMEM] * 2,
         out_shape=[
             dtype_of((bins, 2 * windows), jnp.float32),
             dtype_of((bins, 2 * windows), jnp.float32),
-            dtype_of(spectra.shape, spectra.dtype),
         ],
-        scratch_shapes=[pltpu.VMEM((8 * bins, 2 * windows), jnp.float32), pltpu.VMEM((bins + 16, 2 * windows), jnp.float32), pltpu.SemaphoreType.DMA((chunks,))],
+        scratch_shapes=[pltpu.VMEM((8 * bins, 2 * windows), jnp.float32), pltpu.VMEM((bins + 16, 2 * windows), jnp.float32)],
         compiler_params=params(),
         cost_estimate=pl.CostEstimate(flops=0, bytes_accessed=4 * spectra.size, transcendentals=0),
         name="extract_row",
-    )(picks, spectra)
-
-
-def whiten_row_kernel(row_ref, total_ref, below_ref, above_ref, out_ref):
+    )(column, spectra)
+
+
+def whiten_row_kernel(row_ref, total_ref, below_ref, above_ref, after_ref, out_ref):
     bins, width = row_ref.shape
     windows = width // 2
     band, count = lax.axis_index("band"), lax.axis_size("band")
-    below = below_ref[...].astype(jnp.float32)[:8] * (band > 0).astype(jnp.float32)
-    above = above_ref[...].astype(jnp.float32)[:8] * (band < count - 1).astype(jnp.float32)
+    below = jnp.sum(below_ref[...].astype(jnp.float32)[:8], 0, keepdims=True) * (band > 0).astype(jnp.float32)
+    above = jnp.sum(above_ref[...].astype(jnp.float32)[:8], 0, keepdims=True) * (band < count - 1).astype(jnp.float32)
     sublane = lax.broadcasted_iota(jnp.int32, (8, windows), 0)
     low = jnp.zeros((8, windows), jnp.float32)
     high = jnp.zeros((8, windows), jnp.float32)
@@ -190,15 +216,15 @@
     out_ref[0] = (row_ref[...] / (total * (1.0 / SPAN) + FLOOR)).astype(jnp.bfloat16)
 
 
-def whiten_row(row, total, columns):
+def whiten_row(row, total, columns, after):
     return pl.pallas_call(
         whiten_row_kernel,
-        in_specs=[VMEM] * 4,
+        in_specs=[VMEM] * 5,
         out_specs=VMEM,
         out_shape=dtype_of((1,) + row.shape),
         compiler_params=params(),
         name="whiten_row",
-    )(row, total, *columns)
+    )(row, total, *columns, after)
 
 
 def amplitude_kernel(first, spectra_ref, *refs):
@@ -309,7 +335,7 @@
     return [offset ^ bit for offset in offsets]
 
 
-def gather_rows(row, spectra, ends):
+def gather_rows(row, spectra, first, ends):
     count = lax.axis_size("rx")
     *far, near, across, core = [1 << k for k in reversed(range(count.bit_length() - 1))]
     rows, held = row, [0]
@@ -318,9 +344,8 @@
         held = held + shifted(held, bit)
     far = far[-1]
     from_far = send(rows, far)
-    first = amplitudes(spectra, 0, rows)
-    edges = band_neighbours([merge([end], [rows]) for end in ends])
-    rows = merge([rows, from_far], [first])
+    edges = band_neighbours([end_amplitudes(end, rows) for end in ends])
+    rows = merge([rows, from_far], [])
     held = held + shifted(held, far)
     others = [send(rows, bit) for bit in (near ^ across, across, near)]
     second = amplitudes(spectra, 1, rows)
@@ -382,12 +407,13 @@
 
 
 def local(spectra, source_index):
-    ends, columns, picks = edge_amplitudes(
+    ends, columns, column = edge_amplitudes(
         pltpu.with_memory_space_constraint(spectra, pltpu.HBM),
         pltpu.with_memory_space_constraint(source_index, pltpu.HBM),
     )
-    row, total, held = extract_row(spectra, picks)
-    return cross_spectra(*gather_rows(whiten_row(row, total, columns), held, ends))
+    row, total = extract_row(spectra, column)
+    first = amplitudes(spectra, 0, row)
+    return cross_spectra(*gather_rows(whiten_row(row, total, columns, first), spectra, first, ends))
 
 
 def solution(mesh):

time: 22.7 us -> 22.5 us (level)
  Pallas kernels: 9.08 us -> 7.8 us
  waiting for transfers between devices: 2.62 us -> 3.21 us
  starting transfers between devices: 10.8 us -> 11.3 us
    pallas_call x2 -> x3, Pallas kernels: 2.28 us -> 1.11 us  [the longest x1 0.9 us: extract_row(): pl.pallas_call(functools.partial(extract_kernel, chunks), in_specs=[VMEM]...]
    ppermute x5, waiting for transfers between devices: 2.61 us -> 3.2 us  [send(): return lax.ppermute(rows, 'rx', [(i, i ^ bit) for i in range(count)])]
    ppermute x5, starting transfers between devices: 6.23 us -> 6.65 us  [send(): return lax.ppermute(rows, 'rx', [(i, i ^ bit) for i in range(count)])]
  transfers between devices with their start and end apart: 7 -> 7, of which waited for: 3 -> 4; matrix products, arithmetic and copies ran while one was open for 0% -> 0% of each run, Pallas kernels for 25% -> 20%
where the time goes in v6:
time: 22.5 us; the launch traced here: 22.4 us
  starting transfers between devices  11.3 us (50%)
  Pallas kernels  7.8 us (35%)
  waiting for transfers between devices  3.21 us (14%)
    ppermute x5, starting transfers between devices, send(): return lax.ppermute(rows, 'rx', [(i, i ^ bit) for i in range(count)])  6.65 us
    ppermute x2, starting transfers between devices, band_neighbours(): received = lax.ppermute(ends[0], 'band', [(0, 1), (1, 0)])  4.62 us
    ppermute x5, waiting for transfers between devices, send(): return lax.ppermute(rows, 'rx', [(i, i ^ bit) for i in range(count)])  3.2 us
    pallas_call x1, Pallas kernels, cross_spectra(): pl.pallas_call(functools.partial(cross_kernel, offsets, chunks), in_specs...  2.08 us
    pallas_call x1, Pallas kernels, whiten(): pl.pallas_call(whiten_kernel, in_specs=[VMEM] * (5 + len(after)), out_spe...  1.97 us
    pallas_call x2, Pallas kernels, amplitudes(): pl.pallas_call(functools.partial(amplitude_kernel, half * windows // 2),...  1.45 us
    pallas_call x1, Pallas kernels, edge_amplitudes(): pl.pallas_call(edge_kernel, in_specs=[HBM, HBM], out_specs=[VMEM] * (2 *...  1.17 us
    pallas_call x1, Pallas kernels, extract_row(): pl.pallas_call(functools.partial(extract_kernel, chunks), in_specs=[VMEM]...  0.9 us
  transfers between devices with their start and end apart: 7, of which 4 were waited for; matrix products, arithmetic and copies ran while one was open for 0% of the time, Pallas kernels for 20%

profile of v6, /device:TPU:0, one launch (start us, length us, event | category | flops | bytes accessed | tf_op | source)
XLA Modules:
  0.0 22.4 jit_solution(16641222722568989804)
XLA Ops:
  0.0 0.0 copy-start
  0.0 1.2 %edge_amplitude.1 = (bf16[2,4,64,128]{3,2,1,0:T(8,128)(2,1)S(1)}, bf16[16,256]{1,0:T(8,128)(2,1)S(1)}, s32[8,128]{1,0:T(8,128)S(1)}) custom-call(s32[16]{0:T(128)} %index_ref.1, bf16[2,128,64,128]{3,2,1,0:T(8,128)(2,1)} %spectra_ref.9), custom_call_target="tpu_custom_call" | custom-call | tf_op jit(solution)/shard_map/edge_amplitude/pallas_call | solution.py:82
  1.2 3.0 %collective-permute-start = (bf16[16,256]{1,0:T(8,128)(2,1)S(1)}, bf16[16,256]{1,0:T(8,128)(2,1)S(1)}, u32[]{:S(2)}, u32[]{:S(2)}) collective-permute-start(bf16[16,256]{1,0:T(8,128)(2,1)S(1)} %get-tuple-element.13), channel_id=1, source_target_pairs={{0,1},{1,0},{2,3},{3,2},{4,5},{5,4},{6,7},{7,6},{8,9},{9,8},{10,11... | collective-permute-start | bytes 24584 | tf_op jit(solution)/shard_map/ppermute | solution.py:119
  4.2 0.0 copy-done
  4.2 0.9 %extract_row.1 = (f32[128,128]{1,0:T(8,128)S(1)}, f32[128,128]{1,0:T(8,128)S(1)}) custom-call(s32[8,128]{1,0:T(8,128)S(1)} %get-tuple-element.10.column_ref, bf16[2,128,64,128]{3,2,1,0:T(8,128)(2,1)S(1)} %copy-done), custom_call_target="tpu_custom_call" | custom-call | bytes 8388608 | tf_op jit(solution)/shard_map/extract_row/pallas_call | solution.py:185
  5.1 0.7 %amplitude.2.after_ref.first_ref = f32[128,32,128]{2,1,0:T(8,128)S(1)} custom-call(bf16[2,128,64,128]{3,2,1,0:T(8,128)(2,1)S(1)} %copy-done, f32[128,128]{1,0:T(8,128)S(1)} %get-tuple-element.11.refs_0_.row_ref), custom_call_target="tpu_custom_call" | custom-call | flops 5242880 | bytes 2097152 | tf_op jit(solution)/shard_map/amplitude/pallas_call | solution.py:248
  5.9 0.0 collective-permute-done.below_ref.above_ref
  5.9 0.2 whiten_row.1.refs_0_.after_ref
  6.0 3.1 %collective-permute-start.1 = (bf16[1,128,128]{2,1,0:T(8,128)(2,1)S(1)}, bf16[1,128,128]{2,1,0:T(8,128)(2,1)S(1)}, u32[]{:S(2)}, u32[]{:S(2)}) collective-permute-start(bf16[1,128,128]{2,1,0:T(8,128)(2,1)S(1)} %whiten_row.1.refs_0_.after_ref), channel_id=1, source_target_pairs={{0,16},{2,18},{4,20},{6,22},{8,24},{10,26},{12,28},{14,30},{16,0},... | collective-permute-start | bytes 98312 | tf_op jit(solution)/shard_map/ppermute | solution.py:331
  9.2 1.6 %collective-permute-start.5 = (bf16[4,64,128]{2,1,0:T(8,128)(2,1)S(1)}, bf16[4,64,128]{2,1,0:T(8,128)(2,1)S(1)}, u32[]{:S(2)}, u32[]{:S(2)}) collective-permute-start(bf16[4,64,128]{2,1,0:T(8,128)(2,1)S(1)} %end_amplitude.1), channel_id=1, source_target_pairs={{0,1},{1,0},{2,3},{3,2},{4,5},{5,4},{6,7},{7,6},{8,9},{9,8},{10,11... | collective-permute-start | bytes 196616 | tf_op jit(solution)/shard_map/ppermute | solution.py:119
  10.8 0.3 %collective-permute-done.1.refs_1_ = bf16[1,128,128]{2,1,0:T(8,128)(2,1)S(1)} collective-permute-done((bf16[1,128,128]{2,1,0:T(8,128)(2,1)S(1)}, bf16[1,128,128]{2,1,0:T(8,128)(2,1)S(1)}, u32[]{:S(2)}, u32[]{:S(2)}) %collective-permute-start.1) | collective-permute-done | bytes 32800 | tf_op jit(solution)/shard_map/ppermute | solution.py:331
  11.0 2.8 %collective-permute-start.2 = (bf16[2,128,128]{2,1,0:T(8,128)(2,1)S(1)}, bf16[2,128,128]{2,1,0:T(8,128)(2,1)S(1)}, u32[]{:S(2)}, u32[]{:S(2)}) collective-permute-start(bf16[2,128,128]{2,1,0:T(8,128)(2,1)S(1)} %merge_rows.2.refs_0_), channel_id=1, source_target_pairs={{0,12},{2,14},{4,8},{6,10},{8,4},{10,6},{12,0},{14,2},{16,28},{18,... | collective-permute-start | bytes 196616 | tf_op jit(solution)/shard_map/ppermute | solution.py:331
  13.9 0.5 %collective-permute-start.3 = (bf16[2,128,128]{2,1,0:T(8,128)(2,1)S(1)}, bf16[2,128,128]{2,1,0:T(8,128)(2,1)S(1)}, u32[]{:S(2)}, u32[]{:S(2)}) collective-permute-start(bf16[2,128,128]{2,1,0:T(8,128)(2,1)S(1)} %merge_rows.2.refs_0_), channel_id=1, source_target_pairs={{0,4},{2,6},{4,0},{6,2},{8,12},{10,14},{12,8},{14,10},{16,20},{18,... | collective-permute-start | bytes 196616 | tf_op jit(solution)/shard_map/ppermute | solution.py:331
  14.4 0.1 collective-permute-start.4
  14.5 0.7 %amplitude.3.second_ref = f32[128,32,128]{2,1,0:T(8,128)S(1)} custom-call(bf16[2,128,64,128]{3,2,1,0:T(8,128)(2,1)S(1)} %copy-done, bf16[2,128,128]{2,1,0:T(8,128)(2,1)S(1)} %merge_rows.2.refs_0_), custom_call_target="tpu_custom_call" | custom-call | flops 5242880 | bytes 2097152 | tf_op jit(solution)/shard_map/amplitude/pallas_call | solution.py:248
  15.3 0.0 collective-permute-done.5.below_ref.above_ref
  15.3 2.0 %whiten_windows.1.refs_4_.refs_2_ = bf16[2,128,64,128]{3,2,1,0:T(8,128)(2,1)S(1)} custom-call(bf16[2,128,64,128]{3,2,1,0:T(8,128)(2,1)S(1)} %copy-done, f32[128,32,128]{2,1,0:T(8,128)S(1)} %amplitude.2.after_ref.first_ref, f32[128,32,128]{2,1,0:T(8,128)S(1)} %amplitude.3.second_ref, bf16[4,64,128]{2,1,0:T(8,128)(2,1)S(1)} %collective-permute-done.5.below_ref.above_ref, ...), custom_call_target="tpu_custom_call" | custom-call | flops 14680064 | bytes 4194304 | tf_op jit(solution)/shard_map/whiten_windows/pallas_call | solution.py:299
  17.2 0.0 collective-permute-done.2.refs_1_
  17.2 0.9 %collective-permute-done.3.refs_2_ = bf16[2,128,128]{2,1,0:T(8,128)(2,1)S(1)} collective-permute-done((bf16[2,128,128]{2,1,0:T(8,128)(2,1)S(1)}, bf16[2,128,128]{2,1,0:T(8,128)(2,1)S(1)}, u32[]{:S(2)}, u32[]{:S(2)}) %collective-permute-start.3) | collective-permute-done | bytes 65568 | tf_op jit(solution)/shard_map/ppermute | solution.py:331
  18.1 0.5 %collective-permute-done.4.refs_3_ = bf16[2,128,128]{2,1,0:T(8,128)(2,1)S(1)} collective-permute-done((bf16[2,128,128]{2,1,0:T(8,128)(2,1)S(1)}, bf16[2,128,128]{2,1,0:T(8,128)(2,1)S(1)}, u32[]{:S(2)}, u32[]{:S(2)}) %collective-permute-start.4) | collective-permute-done | bytes 65568 | tf_op jit(solution)/shard_map/ppermute | solution.py:331
  18.7 0.1 collective-permute-start.6
  18.8 1.5 %collective-permute-done.6.refs_1_ = bf16[8,128,128]{2,1,0:T(8,128)(2,1)S(1)} collective-permute-done((bf16[8,128,128]{2,1,0:T(8,128)(2,1)S(1)}, bf16[8,128,128]{2,1,0:T(8,128)(2,1)S(1)}, u32[]{:S(2)}, u32[]{:S(2)}) %collective-permute-start.6) | collective-permute-done | bytes 262176 | tf_op jit(solution)/shard_map/ppermute | solution.py:331
  20.3 2.1 %cross_spectra.1 = bf16[2,128,16,128]{3,2,1,0:T(8,128)(2,1)} custom-call(bf16[8,128,128]{2,1,0:T(8,128)(2,1)S(1)} %merge_rows.3.refs_0_, bf16[8,128,128]{2,1,0:T(8,128)(2,1)S(1)} %collective-permute-done.6.refs_1_, bf16[2,128,64,128]{3,2,1,0:T(8,128)(2,1)S(1)} %whiten_windows.1.refs_4_.refs_2_), custom_call_target="tpu_custom_call" | custom-call | tf_op jit(solution)/shard_map/cross_spectra/pallas_call | solution.py:394
  (3 shorter events, 0.1 us)
Async XLA Ops:
  0.0 4.2 %copy-start = (bf16[2,128,64,128]{3,2,1,0:T(8,128)(2,1)S(1)}, bf16[2,128,64,128]{3,2,1,0:T(8,128)(2,1)}, u32[]{:S(2)}) copy-start(bf16[2,128,64,128]{3,2,1,0:T(8,128)(2,1)} %spectra_ref.9) | copy-start | bytes 12582916
  1.2 4.7 %collective-permute-start = (bf16[16,256]{1,0:T(8,128)(2,1)S(1)}, bf16[16,256]{1,0:T(8,128)(2,1)S(1)}, u32[]{:S(2)}, u32[]{:S(2)}) collective-permute-start(bf16[16,256]{1,0:T(8,128)(2,1)S(1)} %get-tuple-element.13), channel_id=1, source_target_pairs={{0,1},{1,0},{2,3},{3,2},{4,5},{5,4},{6,7},{7,6},{8,9},{9,8},{10,11... | collective-permute-start | bytes 24584 | tf_op jit(solution)/shard_map/ppermute | solution.py:119
  6.0 5.0 %collective-permute-start.1 = (bf16[1,128,128]{2,1,0:T(8,128)(2,1)S(1)}, bf16[1,128,128]{2,1,0:T(8,128)(2,1)S(1)}, u32[]{:S(2)}, u32[]{:S(2)}) collective-permute-start(bf16[1,128,128]{2,1,0:T(8,128)(2,1)S(1)} %whiten_row.1.refs_0_.after_ref), channel_id=1, source_target_pairs={{0,16},{2,18},{4,20},{6,22},{8,24},{10,26},{12,28},{14,30},{16,0},... | collective-permute-start | bytes 98312 | tf_op jit(solution)/shard_map/ppermute | solution.py:331
  9.2 6.1 %collective-permute-start.5 = (bf16[4,64,128]{2,1,0:T(8,128)(2,1)S(1)}, bf16[4,64,128]{2,1,0:T(8,128)(2,1)S(1)}, u32[]{:S(2)}, u32[]{:S(2)}) collective-permute-start(bf16[4,64,128]{2,1,0:T(8,128)(2,1)S(1)} %end_amplitude.1), channel_id=1, source_target_pairs={{0,1},{1,0},{2,3},{3,2},{4,5},{5,4},{6,7},{7,6},{8,9},{9,8},{10,11... | collective-permute-start | bytes 196616 | tf_op jit(solution)/shard_map/ppermute | solution.py:119
  11.0 6.2 %collective-permute-start.2 = (bf16[2,128,128]{2,1,0:T(8,128)(2,1)S(1)}, bf16[2,128,128]{2,1,0:T(8,128)(2,1)S(1)}, u32[]{:S(2)}, u32[]{:S(2)}) collective-permute-start(bf16[2,128,128]{2,1,0:T(8,128)(2,1)S(1)} %merge_rows.2.refs_0_), channel_id=1, source_target_pairs={{0,12},{2,14},{4,8},{6,10},{8,4},{10,6},{12,0},{14,2},{16,28},{18,... | collective-permute-start | bytes 196616 | tf_op jit(solution)/shard_map/ppermute | solution.py:331
  13.9 4.3 %collective-permute-start.3 = (bf16[2,128,128]{2,1,0:T(8,128)(2,1)S(1)}, bf16[2,128,128]{2,1,0:T(8,128)(2,1)S(1)}, u32[]{:S(2)}, u32[]{:S(2)}) collective-permute-start(bf16[2,128,128]{2,1,0:T(8,128)(2,1)S(1)} %merge_rows.2.refs_0_), channel_id=1, source_target_pairs={{0,4},{2,6},{4,0},{6,2},{8,12},{10,14},{12,8},{14,10},{16,20},{18,... | collective-permute-start | bytes 196616 | tf_op jit(solution)/shard_map/ppermute | solution.py:331
  14.4 4.3 %collective-permute-start.4 = (bf16[2,128,128]{2,1,0:T(8,128)(2,1)S(1)}, bf16[2,128,128]{2,1,0:T(8,128)(2,1)S(1)}, u32[]{:S(2)}, u32[]{:S(2)}) collective-permute-start(bf16[2,128,128]{2,1,0:T(8,128)(2,1)S(1)} %merge_rows.2.refs_0_), channel_id=1, source_target_pairs={{0,8},{2,10},{4,12},{6,14},{8,0},{10,2},{12,4},{14,6},{16,24},{18,... | collective-permute-start | bytes 196616 | tf_op jit(solution)/shard_map/ppermute | solution.py:331
  18.7 1.6 %collective-permute-start.6 = (bf16[8,128,128]{2,1,0:T(8,128)(2,1)S(1)}, bf16[8,128,128]{2,1,0:T(8,128)(2,1)S(1)}, u32[]{:S(2)}, u32[]{:S(2)}) collective-permute-start(bf16[8,128,128]{2,1,0:T(8,128)(2,1)S(1)} %merge_rows.3.refs_0_), channel_id=1, source_target_pairs={{0,2},{2,0},{4,6},{6,4},{8,10},{10,8},{12,14},{14,12},{16,18},{18,... | collective-permute-start | bytes 786440 | tf_op jit(solution)/shard_map/ppermute | solution.py:331

commit v7 on v6

--- a/solution.py
+++ b/solution.py
@@ -355,32 +355,34 @@
     return [rows, send(rows, core)], held + shifted(held, core), whitened
 
 
-def cross_kernel(offsets, chunks, *refs):
+def cross_kernel(offsets, ends, *refs):
     *blocks, white_ref, out_ref, wide_ref, buffer, sem = refs
     sources = len(offsets)
     _, bins, width = blocks[0].shape
     windows = width // 2
     rank = lax.axis_index("rx")
     rows = [(ref, k) for ref in blocks for k in range(ref.shape[0])]
+    pitch = wide_ref.shape[0] // sources
     for (ref, k), offset in zip(rows, offsets, strict=True):
-        at = pl.multiple_of((rank ^ offset) * bins, bins)
+        at = pl.multiple_of((rank ^ offset) * pitch, 8)
         wide_ref[pl.ds(at, bins)] = ref[k].astype(jnp.float32) * (1.0 / windows)
     sign = jnp.where(lax.broadcasted_iota(jnp.int32, (sources, width), 1) < windows, -1.0, 1.0)
-    size = bins // chunks
     copies = []
-    for chunk in range(chunks):
-        for f in range(chunk * size, (chunk + 1) * size):
-            first = wide_ref[pl.ds(f, sources, stride=bins)]
+    start = 0
+    for end in ends:
+        for f in range(start, end):
+            first = wide_ref[pl.ds(f, sources, stride=pitch)]
             second = pltpu.roll(first, windows, 1) * sign
             left = jnp.concatenate([first, second], 0).astype(jnp.bfloat16)
             right = jnp.concatenate([white_ref[0, f], white_ref[1, f]], 0)
             product = jnp.dot(left, right, preferred_element_type=jnp.float32).astype(jnp.bfloat16)
             buffer[0, f] = product[:sources]
             buffer[1, f] = product[sources:]
-        part = (slice(None), pl.ds(chunk * size, size))
-        copy = pltpu.make_async_copy(buffer.at[part], out_ref.at[part], sem.at[chunk])
+        part = (slice(None), pl.ds(start, end - start))
+        copy = pltpu.make_async_copy(buffer.at[part], out_ref.at[part], sem.at[len(copies)])
         copy.start()
         copies.append(copy)
+        start = end
     for copy in copies:
         copy.wait()
 
@@ -389,17 +391,17 @@
     sources = len(offsets)
     _, bins, width = blocks[0].shape
     channels = whitened.shape[-1]
-    chunks = min(8, bins // 8)
+    ends = [k * bins // 32 for k in (8, 16, 24, 30, 32)]
     shape = (2, bins, sources, channels)
     return pl.pallas_call(
-        functools.partial(cross_kernel, offsets, chunks),
+        functools.partial(cross_kernel, offsets, ends),
         in_specs=[VMEM] * (len(blocks) + 1),
         out_specs=HBM,
         out_shape=dtype_of(shape),
         scratch_shapes=[
-            pltpu.VMEM((sources * bins, width), jnp.float32),
+            pltpu.VMEM((sources * (bins + 8), width), jnp.float32),
             pltpu.VMEM(shape, jnp.bfloat16),
-            pltpu.SemaphoreType.DMA((chunks,)),
+            pltpu.SemaphoreType.DMA((len(ends),)),
         ],
         compiler_params=params(),
         name="cross_spectra",

time: 22.5 us -> 22.4 us (level)
  no operation moved by 1% of the time
where the time goes in v7:
time: 22.4 us; the launch traced here: 22.3 us
  starting transfers between devices  11.3 us (50%)
  Pallas kernels  7.74 us (35%)
  waiting for transfers between devices  3.21 us (14%)
    ppermute x5, starting transfers between devices, send(): return lax.ppermute(rows, 'rx', [(i, i ^ bit) for i in range(count)])  6.65 us
    ppermute x2, starting transfers between devices, band_neighbours(): received = lax.ppermute(ends[0], 'band', [(0, 1), (1, 0)])  4.62 us
    ppermute x5, waiting for transfers between devices, send(): return lax.ppermute(rows, 'rx', [(i, i ^ bit) for i in range(count)])  3.2 us
    pallas_call x1, Pallas kernels, cross_spectra(): pl.pallas_call(functools.partial(cross_kernel, offsets, ends), in_specs=[...  2.02 us
    pallas_call x1, Pallas kernels, whiten(): pl.pallas_call(whiten_kernel, in_specs=[VMEM] * (5 + len(after)), out_spe...  1.97 us
    pallas_call x2, Pallas kernels, amplitudes(): pl.pallas_call(functools.partial(amplitude_kernel, half * windows // 2),...  1.45 us
    pallas_call x1, Pallas kernels, edge_amplitudes(): pl.pallas_call(edge_kernel, in_specs=[HBM, HBM], out_specs=[VMEM] * (2 *...  1.17 us
    pallas_call x1, Pallas kernels, extract_row(): pl.pallas_call(functools.partial(extract_kernel, chunks), in_specs=[VMEM]...  0.9 us
  transfers between devices with their start and end apart: 7, of which 4 were waited for; matrix products, arithmetic and copies ran while one was open for 0% of the time, Pallas kernels for 20%

profile of v7, /device:TPU:0, one launch (start us, length us, event | category | flops | bytes accessed | tf_op | source)
XLA Modules:
  0.0 22.3 jit_solution(6334476250555918541)
XLA Ops:
  0.0 0.0 copy-start
  0.0 1.2 %edge_amplitude.1 = (bf16[2,4,64,128]{3,2,1,0:T(8,128)(2,1)S(1)}, bf16[16,256]{1,0:T(8,128)(2,1)S(1)}, s32[8,128]{1,0:T(8,128)S(1)}) custom-call(s32[16]{0:T(128)} %index_ref.1, bf16[2,128,64,128]{3,2,1,0:T(8,128)(2,1)} %spectra_ref.9), custom_call_target="tpu_custom_call" | custom-call | tf_op jit(solution)/shard_map/edge_amplitude/pallas_call | solution.py:82
  1.2 3.0 %collective-permute-start = (bf16[16,256]{1,0:T(8,128)(2,1)S(1)}, bf16[16,256]{1,0:T(8,128)(2,1)S(1)}, u32[]{:S(2)}, u32[]{:S(2)}) collective-permute-start(bf16[16,256]{1,0:T(8,128)(2,1)S(1)} %get-tuple-element.13), channel_id=1, source_target_pairs={{0,1},{1,0},{2,3},{3,2},{4,5},{5,4},{6,7},{7,6},{8,9},{9,8},{10,11... | collective-permute-start | bytes 24584 | tf_op jit(solution)/shard_map/ppermute | solution.py:119
  4.2 0.0 copy-done
  4.2 0.9 %extract_row.1 = (f32[128,128]{1,0:T(8,128)S(1)}, f32[128,128]{1,0:T(8,128)S(1)}) custom-call(s32[8,128]{1,0:T(8,128)S(1)} %get-tuple-element.10.column_ref, bf16[2,128,64,128]{3,2,1,0:T(8,128)(2,1)S(1)} %copy-done), custom_call_target="tpu_custom_call" | custom-call | bytes 8388608 | tf_op jit(solution)/shard_map/extract_row/pallas_call | solution.py:185
  5.1 0.7 %amplitude.2.after_ref.first_ref = f32[128,32,128]{2,1,0:T(8,128)S(1)} custom-call(bf16[2,128,64,128]{3,2,1,0:T(8,128)(2,1)S(1)} %copy-done, f32[128,128]{1,0:T(8,128)S(1)} %get-tuple-element.11.refs_0_.row_ref), custom_call_target="tpu_custom_call" | custom-call | flops 5242880 | bytes 2097152 | tf_op jit(solution)/shard_map/amplitude/pallas_call | solution.py:248
  5.9 0.0 collective-permute-done.below_ref.above_ref
  5.9 0.2 whiten_row.1.refs_0_.after_ref
  6.0 3.1 %collective-permute-start.1 = (bf16[1,128,128]{2,1,0:T(8,128)(2,1)S(1)}, bf16[1,128,128]{2,1,0:T(8,128)(2,1)S(1)}, u32[]{:S(2)}, u32[]{:S(2)}) collective-permute-start(bf16[1,128,128]{2,1,0:T(8,128)(2,1)S(1)} %whiten_row.1.refs_0_.after_ref), channel_id=1, source_target_pairs={{0,16},{2,18},{4,20},{6,22},{8,24},{10,26},{12,28},{14,30},{16,0},... | collective-permute-start | bytes 98312 | tf_op jit(solution)/shard_map/ppermute | solution.py:331
  9.2 1.6 %collective-permute-start.5 = (bf16[4,64,128]{2,1,0:T(8,128)(2,1)S(1)}, bf16[4,64,128]{2,1,0:T(8,128)(2,1)S(1)}, u32[]{:S(2)}, u32[]{:S(2)}) collective-permute-start(bf16[4,64,128]{2,1,0:T(8,128)(2,1)S(1)} %end_amplitude.1), channel_id=1, source_target_pairs={{0,1},{1,0},{2,3},{3,2},{4,5},{5,4},{6,7},{7,6},{8,9},{9,8},{10,11... | collective-permute-start | bytes 196616 | tf_op jit(solution)/shard_map/ppermute | solution.py:119
  10.8 0.3 %collective-permute-done.1.refs_1_ = bf16[1,128,128]{2,1,0:T(8,128)(2,1)S(1)} collective-permute-done((bf16[1,128,128]{2,1,0:T(8,128)(2,1)S(1)}, bf16[1,128,128]{2,1,0:T(8,128)(2,1)S(1)}, u32[]{:S(2)}, u32[]{:S(2)}) %collective-permute-start.1) | collective-permute-done | bytes 32800 | tf_op jit(solution)/shard_map/ppermute | solution.py:331
  11.0 2.8 %collective-permute-start.2 = (bf16[2,128,128]{2,1,0:T(8,128)(2,1)S(1)}, bf16[2,128,128]{2,1,0:T(8,128)(2,1)S(1)}, u32[]{:S(2)}, u32[]{:S(2)}) collective-permute-start(bf16[2,128,128]{2,1,0:T(8,128)(2,1)S(1)} %merge_rows.2.refs_0_), channel_id=1, source_target_pairs={{0,12},{2,14},{4,8},{6,10},{8,4},{10,6},{12,0},{14,2},{16,28},{18,... | collective-permute-start | bytes 196616 | tf_op jit(solution)/shard_map/ppermute | solution.py:331
  13.9 0.5 %collective-permute-start.3 = (bf16[2,128,128]{2,1,0:T(8,128)(2,1)S(1)}, bf16[2,128,128]{2,1,0:T(8,128)(2,1)S(1)}, u32[]{:S(2)}, u32[]{:S(2)}) collective-permute-start(bf16[2,128,128]{2,1,0:T(8,128)(2,1)S(1)} %merge_rows.2.refs_0_), channel_id=1, source_target_pairs={{0,4},{2,6},{4,0},{6,2},{8,12},{10,14},{12,8},{14,10},{16,20},{18,... | collective-permute-start | bytes 196616 | tf_op jit(solution)/shard_map/ppermute | solution.py:331
  14.4 0.1 collective-permute-start.4
  14.5 0.7 %amplitude.3.second_ref = f32[128,32,128]{2,1,0:T(8,128)S(1)} custom-call(bf16[2,128,64,128]{3,2,1,0:T(8,128)(2,1)S(1)} %copy-done, bf16[2,128,128]{2,1,0:T(8,128)(2,1)S(1)} %merge_rows.2.refs_0_), custom_call_target="tpu_custom_call" | custom-call | flops 5242880 | bytes 2097152 | tf_op jit(solution)/shard_map/amplitude/pallas_call | solution.py:248
  15.3 0.0 collective-permute-done.5.below_ref.above_ref
  15.3 2.0 %whiten_windows.1.refs_4_.refs_2_ = bf16[2,128,64,128]{3,2,1,0:T(8,128)(2,1)S(1)} custom-call(bf16[2,128,64,128]{3,2,1,0:T(8,128)(2,1)S(1)} %copy-done, f32[128,32,128]{2,1,0:T(8,128)S(1)} %amplitude.2.after_ref.first_ref, f32[128,32,128]{2,1,0:T(8,128)S(1)} %amplitude.3.second_ref, bf16[4,64,128]{2,1,0:T(8,128)(2,1)S(1)} %collective-permute-done.5.below_ref.above_ref, ...), custom_call_target="tpu_custom_call" | custom-call | flops 14680064 | bytes 4194304 | tf_op jit(solution)/shard_map/whiten_windows/pallas_call | solution.py:299
  17.2 0.0 collective-permute-done.2.refs_1_
  17.2 0.9 %collective-permute-done.3.refs_2_ = bf16[2,128,128]{2,1,0:T(8,128)(2,1)S(1)} collective-permute-done((bf16[2,128,128]{2,1,0:T(8,128)(2,1)S(1)}, bf16[2,128,128]{2,1,0:T(8,128)(2,1)S(1)}, u32[]{:S(2)}, u32[]{:S(2)}) %collective-permute-start.3) | collective-permute-done | bytes 65568 | tf_op jit(solution)/shard_map/ppermute | solution.py:331
  18.1 0.5 %collective-permute-done.4.refs_3_ = bf16[2,128,128]{2,1,0:T(8,128)(2,1)S(1)} collective-permute-done((bf16[2,128,128]{2,1,0:T(8,128)(2,1)S(1)}, bf16[2,128,128]{2,1,0:T(8,128)(2,1)S(1)}, u32[]{:S(2)}, u32[]{:S(2)}) %collective-permute-start.4) | collective-permute-done | bytes 65568 | tf_op jit(solution)/shard_map/ppermute | solution.py:331
  18.7 0.1 collective-permute-start.6
  18.8 1.5 %collective-permute-done.6.refs_1_ = bf16[8,128,128]{2,1,0:T(8,128)(2,1)S(1)} collective-permute-done((bf16[8,128,128]{2,1,0:T(8,128)(2,1)S(1)}, bf16[8,128,128]{2,1,0:T(8,128)(2,1)S(1)}, u32[]{:S(2)}, u32[]{:S(2)}) %collective-permute-start.6) | collective-permute-done | bytes 262176 | tf_op jit(solution)/shard_map/ppermute | solution.py:331
  20.3 2.0 %cross_spectra.1 = bf16[2,128,16,128]{3,2,1,0:T(8,128)(2,1)} custom-call(bf16[8,128,128]{2,1,0:T(8,128)(2,1)S(1)} %merge_rows.3.refs_0_, bf16[8,128,128]{2,1,0:T(8,128)(2,1)S(1)} %collective-permute-done.6.refs_1_, bf16[2,128,64,128]{3,2,1,0:T(8,128)(2,1)S(1)} %whiten_windows.1.refs_4_.refs_2_), custom_call_target="tpu_custom_call" | custom-call | tf_op jit(solution)/shard_map/cross_spectra/pallas_call | solution.py:396
  (3 shorter events, 0.1 us)
Async XLA Ops:
  0.0 4.2 %copy-start = (bf16[2,128,64,128]{3,2,1,0:T(8,128)(2,1)S(1)}, bf16[2,128,64,128]{3,2,1,0:T(8,128)(2,1)}, u32[]{:S(2)}) copy-start(bf16[2,128,64,128]{3,2,1,0:T(8,128)(2,1)} %spectra_ref.9) | copy-start | bytes 12582916
  1.2 4.7 %collective-permute-start = (bf16[16,256]{1,0:T(8,128)(2,1)S(1)}, bf16[16,256]{1,0:T(8,128)(2,1)S(1)}, u32[]{:S(2)}, u32[]{:S(2)}) collective-permute-start(bf16[16,256]{1,0:T(8,128)(2,1)S(1)} %get-tuple-element.13), channel_id=1, source_target_pairs={{0,1},{1,0},{2,3},{3,2},{4,5},{5,4},{6,7},{7,6},{8,9},{9,8},{10,11... | collective-permute-start | bytes 24584 | tf_op jit(solution)/shard_map/ppermute | solution.py:119
  6.0 5.0 %collective-permute-start.1 = (bf16[1,128,128]{2,1,0:T(8,128)(2,1)S(1)}, bf16[1,128,128]{2,1,0:T(8,128)(2,1)S(1)}, u32[]{:S(2)}, u32[]{:S(2)}) collective-permute-start(bf16[1,128,128]{2,1,0:T(8,128)(2,1)S(1)} %whiten_row.1.refs_0_.after_ref), channel_id=1, source_target_pairs={{0,16},{2,18},{4,20},{6,22},{8,24},{10,26},{12,28},{14,30},{16,0},... | collective-permute-start | bytes 98312 | tf_op jit(solution)/shard_map/ppermute | solution.py:331
  9.2 6.1 %collective-permute-start.5 = (bf16[4,64,128]{2,1,0:T(8,128)(2,1)S(1)}, bf16[4,64,128]{2,1,0:T(8,128)(2,1)S(1)}, u32[]{:S(2)}, u32[]{:S(2)}) collective-permute-start(bf16[4,64,128]{2,1,0:T(8,128)(2,1)S(1)} %end_amplitude.1), channel_id=1, source_target_pairs={{0,1},{1,0},{2,3},{3,2},{4,5},{5,4},{6,7},{7,6},{8,9},{9,8},{10,11... | collective-permute-start | bytes 196616 | tf_op jit(solution)/shard_map/ppermute | solution.py:119
  11.0 6.2 %collective-permute-start.2 = (bf16[2,128,128]{2,1,0:T(8,128)(2,1)S(1)}, bf16[2,128,128]{2,1,0:T(8,128)(2,1)S(1)}, u32[]{:S(2)}, u32[]{:S(2)}) collective-permute-start(bf16[2,128,128]{2,1,0:T(8,128)(2,1)S(1)} %merge_rows.2.refs_0_), channel_id=1, source_target_pairs={{0,12},{2,14},{4,8},{6,10},{8,4},{10,6},{12,0},{14,2},{16,28},{18,... | collective-permute-start | bytes 196616 | tf_op jit(solution)/shard_map/ppermute | solution.py:331
  13.9 4.3 %collective-permute-start.3 = (bf16[2,128,128]{2,1,0:T(8,128)(2,1)S(1)}, bf16[2,128,128]{2,1,0:T(8,128)(2,1)S(1)}, u32[]{:S(2)}, u32[]{:S(2)}) collective-permute-start(bf16[2,128,128]{2,1,0:T(8,128)(2,1)S(1)} %merge_rows.2.refs_0_), channel_id=1, source_target_pairs={{0,4},{2,6},{4,0},{6,2},{8,12},{10,14},{12,8},{14,10},{16,20},{18,... | collective-permute-start | bytes 196616 | tf_op jit(solution)/shard_map/ppermute | solution.py:331
  14.4 4.3 %collective-permute-start.4 = (bf16[2,128,128]{2,1,0:T(8,128)(2,1)S(1)}, bf16[2,128,128]{2,1,0:T(8,128)(2,1)S(1)}, u32[]{:S(2)}, u32[]{:S(2)}) collective-permute-start(bf16[2,128,128]{2,1,0:T(8,128)(2,1)S(1)} %merge_rows.2.refs_0_), channel_id=1, source_target_pairs={{0,8},{2,10},{4,12},{6,14},{8,0},{10,2},{12,4},{14,6},{16,24},{18,... | collective-permute-start | bytes 196616 | tf_op jit(solution)/shard_map/ppermute | solution.py:331
  18.7 1.6 %collective-permute-start.6 = (bf16[8,128,128]{2,1,0:T(8,128)(2,1)S(1)}, bf16[8,128,128]{2,1,0:T(8,128)(2,1)S(1)}, u32[]{:S(2)}, u32[]{:S(2)}) collective-permute-start(bf16[8,128,128]{2,1,0:T(8,128)(2,1)S(1)} %merge_rows.3.refs_0_), channel_id=1, source_target_pairs={{0,2},{2,0},{4,6},{6,4},{8,10},{10,8},{12,14},{14,12},{16,18},{18,... | collective-permute-start | bytes 786440 | tf_op jit(solution)/shard_map/ppermute | solution.py:331

commit v8 on v7

--- a/solution.py
+++ b/solution.py
@@ -367,15 +367,36 @@
         at = pl.multiple_of((rank ^ offset) * pitch, 8)
         wide_ref[pl.ds(at, bins)] = ref[k].astype(jnp.float32) * (1.0 / windows)
     sign = jnp.where(lax.broadcasted_iota(jnp.int32, (sources, width), 1) < windows, -1.0, 1.0)
+    none = jnp.zeros((2 * sources, width), jnp.bfloat16)
+
+    def left(f):
+        first = wide_ref[pl.ds(f, sources, stride=pitch)]
+        second = pltpu.roll(first, windows, 1) * sign
+        return jnp.concatenate([first, second], 0).astype(jnp.bfloat16)
+
+    def products(start, count):
+        def scoped(*accumulators):
+            for k, accumulator in enumerate(accumulators):
+                f = start + 4 * k
+                white = [jnp.concatenate([white_ref[0, f + j], white_ref[1, f + j]], 0) for j in range(4)]
+                pairs = [jnp.concatenate(white[j : j + 2], 0) for j in (0, 2)]
+                staged = (k // 2) % 2
+                pltpu.matmul_push_rhs(jnp.concatenate(pairs, 1), staged, k % 2)
+                rows = [jnp.concatenate([left(f + j), none] if j % 2 == 0 else [none, left(f + j)], 1) for j in range(4)]
+                pltpu.matmul_acc_lhs(accumulator, jnp.concatenate(rows, 0), load_staged_rhs=staged)
+            return [pltpu.matmul_pop(accumulator) for accumulator in accumulators]
+
+        shape = (8 * sources, 2 * width)
+        return pl.run_scoped(scoped, *[pltpu.ACC(k % 2)(shape, jnp.float32) for k in range(count // 4)])
+
     copies = []
     start = 0
     for end in ends:
+        found = products(start, end - start)
         for f in range(start, end):
-            first = wide_ref[pl.ds(f, sources, stride=pitch)]
-            second = pltpu.roll(first, windows, 1) * sign
-            left = jnp.concatenate([first, second], 0).astype(jnp.bfloat16)
-            right = jnp.concatenate([white_ref[0, f], white_ref[1, f]], 0)
-            product = jnp.dot(left, right, preferred_element_type=jnp.float32).astype(jnp.bfloat16)
+            j = (f - start) % 4
+            columns = slice(j // 2 * width, (j // 2 + 1) * width)
+            product = found[(f - start) // 4][2 * sources * j : 2 * sources * (j + 1), columns].astype(jnp.bfloat16)
             buffer[0, f] = product[:sources]
             buffer[1, f] = product[sources:]
         part = (slice(None), pl.ds(start, end - start))
@@ -391,7 +412,7 @@
     sources = len(offsets)
     _, bins, width = blocks[0].shape
     channels = whitened.shape[-1]
-    ends = [k * bins // 32 for k in (8, 16, 24, 30, 32)]
+    ends = [k * bins // 32 for k in (8, 16, 24, 28, 32)]
     shape = (2, bins, sources, channels)
     return pl.pallas_call(
         functools.partial(cross_kernel, offsets, ends),

time: 22.4 us -> 22.1 us (0.987)
  Pallas kernels: 7.74 us -> 7.39 us
    pallas_call x1, Pallas kernels: 2.02 us -> 1.66 us  [cross_spectra(): pl.pallas_call(functools.partial(cross_kernel, offsets, ends), in_specs=[...]
where the time goes in v8:
time: 22.1 us; the launch traced here: 22 us
  starting transfers between devices  11.3 us (51%)
  Pallas kernels  7.39 us (33%)
  waiting for transfers between devices  3.21 us (15%)
    ppermute x5, starting transfers between devices, send(): return lax.ppermute(rows, 'rx', [(i, i ^ bit) for i in range(count)])  6.65 us
    ppermute x2, starting transfers between devices, band_neighbours(): received = lax.ppermute(ends[0], 'band', [(0, 1), (1, 0)])  4.62 us
    ppermute x5, waiting for transfers between devices, send(): return lax.ppermute(rows, 'rx', [(i, i ^ bit) for i in range(count)])  3.2 us
    pallas_call x1, Pallas kernels, whiten(): pl.pallas_call(whiten_kernel, in_specs=[VMEM] * (5 + len(after)), out_spe...  1.97 us
    pallas_call x1, Pallas kernels, cross_spectra(): pl.pallas_call(functools.partial(cross_kernel, offsets, ends), in_specs=[...  1.66 us
    pallas_call x2, Pallas kernels, amplitudes(): pl.pallas_call(functools.partial(amplitude_kernel, half * windows // 2),...  1.45 us
    pallas_call x1, Pallas kernels, edge_amplitudes(): pl.pallas_call(edge_kernel, in_specs=[HBM, HBM], out_specs=[VMEM] * (2 *...  1.17 us
    pallas_call x1, Pallas kernels, extract_row(): pl.pallas_call(functools.partial(extract_kernel, chunks), in_specs=[VMEM]...  0.9 us
  transfers between devices with their start and end apart: 7, of which 4 were waited for; matrix products, arithmetic and copies ran while one was open for 0% of the time, Pallas kernels for 20%

profile of v8, /device:TPU:0, one launch (start us, length us, event | category | flops | bytes accessed | tf_op | source)
XLA Modules:
  0.0 22.0 jit_solution(12589185598909404150)
XLA Ops:
  0.0 0.0 copy-start
  0.0 1.2 %edge_amplitude.1 = (bf16[2,4,64,128]{3,2,1,0:T(8,128)(2,1)S(1)}, bf16[16,256]{1,0:T(8,128)(2,1)S(1)}, s32[8,128]{1,0:T(8,128)S(1)}) custom-call(s32[16]{0:T(128)} %index_ref.1, bf16[2,128,64,128]{3,2,1,0:T(8,128)(2,1)} %spectra_ref.9), custom_call_target="tpu_custom_call" | custom-call | tf_op jit(solution)/shard_map/edge_amplitude/pallas_call | solution.py:82
  1.2 3.0 %collective-permute-start = (bf16[16,256]{1,0:T(8,128)(2,1)S(1)}, bf16[16,256]{1,0:T(8,128)(2,1)S(1)}, u32[]{:S(2)}, u32[]{:S(2)}) collective-permute-start(bf16[16,256]{1,0:T(8,128)(2,1)S(1)} %get-tuple-element.13), channel_id=1, source_target_pairs={{0,1},{1,0},{2,3},{3,2},{4,5},{5,4},{6,7},{7,6},{8,9},{9,8},{10,11... | collective-permute-start | bytes 24584 | tf_op jit(solution)/shard_map/ppermute | solution.py:119
  4.2 0.0 copy-done
  4.2 0.9 %extract_row.1 = (f32[128,128]{1,0:T(8,128)S(1)}, f32[128,128]{1,0:T(8,128)S(1)}) custom-call(s32[8,128]{1,0:T(8,128)S(1)} %get-tuple-element.10.column_ref, bf16[2,128,64,128]{3,2,1,0:T(8,128)(2,1)S(1)} %copy-done), custom_call_target="tpu_custom_call" | custom-call | bytes 8388608 | tf_op jit(solution)/shard_map/extract_row/pallas_call | solution.py:185
  5.1 0.7 %amplitude.2.after_ref.first_ref = f32[128,32,128]{2,1,0:T(8,128)S(1)} custom-call(bf16[2,128,64,128]{3,2,1,0:T(8,128)(2,1)S(1)} %copy-done, f32[128,128]{1,0:T(8,128)S(1)} %get-tuple-element.11.refs_0_.row_ref), custom_call_target="tpu_custom_call" | custom-call | flops 5242880 | bytes 2097152 | tf_op jit(solution)/shard_map/amplitude/pallas_call | solution.py:248
  5.9 0.0 collective-permute-done.below_ref.above_ref
  5.9 0.2 whiten_row.1.refs_0_.after_ref
  6.0 3.1 %collective-permute-start.1 = (bf16[1,128,128]{2,1,0:T(8,128)(2,1)S(1)}, bf16[1,128,128]{2,1,0:T(8,128)(2,1)S(1)}, u32[]{:S(2)}, u32[]{:S(2)}) collective-permute-start(bf16[1,128,128]{2,1,0:T(8,128)(2,1)S(1)} %whiten_row.1.refs_0_.after_ref), channel_id=1, source_target_pairs={{0,16},{2,18},{4,20},{6,22},{8,24},{10,26},{12,28},{14,30},{16,0},... | collective-permute-start | bytes 98312 | tf_op jit(solution)/shard_map/ppermute | solution.py:331
  9.2 1.6 %collective-permute-start.5 = (bf16[4,64,128]{2,1,0:T(8,128)(2,1)S(1)}, bf16[4,64,128]{2,1,0:T(8,128)(2,1)S(1)}, u32[]{:S(2)}, u32[]{:S(2)}) collective-permute-start(bf16[4,64,128]{2,1,0:T(8,128)(2,1)S(1)} %end_amplitude.1), channel_id=1, source_target_pairs={{0,1},{1,0},{2,3},{3,2},{4,5},{5,4},{6,7},{7,6},{8,9},{9,8},{10,11... | collective-permute-start | bytes 196616 | tf_op jit(solution)/shard_map/ppermute | solution.py:119
  10.8 0.3 %collective-permute-done.1.refs_1_ = bf16[1,128,128]{2,1,0:T(8,128)(2,1)S(1)} collective-permute-done((bf16[1,128,128]{2,1,0:T(8,128)(2,1)S(1)}, bf16[1,128,128]{2,1,0:T(8,128)(2,1)S(1)}, u32[]{:S(2)}, u32[]{:S(2)}) %collective-permute-start.1) | collective-permute-done | bytes 32800 | tf_op jit(solution)/shard_map/ppermute | solution.py:331
  11.0 2.8 %collective-permute-start.2 = (bf16[2,128,128]{2,1,0:T(8,128)(2,1)S(1)}, bf16[2,128,128]{2,1,0:T(8,128)(2,1)S(1)}, u32[]{:S(2)}, u32[]{:S(2)}) collective-permute-start(bf16[2,128,128]{2,1,0:T(8,128)(2,1)S(1)} %merge_rows.2.refs_0_), channel_id=1, source_target_pairs={{0,12},{2,14},{4,8},{6,10},{8,4},{10,6},{12,0},{14,2},{16,28},{18,... | collective-permute-start | bytes 196616 | tf_op jit(solution)/shard_map/ppermute | solution.py:331
  13.9 0.5 %collective-permute-start.3 = (bf16[2,128,128]{2,1,0:T(8,128)(2,1)S(1)}, bf16[2,128,128]{2,1,0:T(8,128)(2,1)S(1)}, u32[]{:S(2)}, u32[]{:S(2)}) collective-permute-start(bf16[2,128,128]{2,1,0:T(8,128)(2,1)S(1)} %merge_rows.2.refs_0_), channel_id=1, source_target_pairs={{0,4},{2,6},{4,0},{6,2},{8,12},{10,14},{12,8},{14,10},{16,20},{18,... | collective-permute-start | bytes 196616 | tf_op jit(solution)/shard_map/ppermute | solution.py:331
  14.4 0.1 collective-permute-start.4
  14.5 0.7 %amplitude.3.second_ref = f32[128,32,128]{2,1,0:T(8,128)S(1)} custom-call(bf16[2,128,64,128]{3,2,1,0:T(8,128)(2,1)S(1)} %copy-done, bf16[2,128,128]{2,1,0:T(8,128)(2,1)S(1)} %merge_rows.2.refs_0_), custom_call_target="tpu_custom_call" | custom-call | flops 5242880 | bytes 2097152 | tf_op jit(solution)/shard_map/amplitude/pallas_call | solution.py:248
  15.3 0.0 collective-permute-done.5.below_ref.above_ref
  15.3 2.0 %whiten_windows.1.refs_4_.refs_2_ = bf16[2,128,64,128]{3,2,1,0:T(8,128)(2,1)S(1)} custom-call(bf16[2,128,64,128]{3,2,1,0:T(8,128)(2,1)S(1)} %copy-done, f32[128,32,128]{2,1,0:T(8,128)S(1)} %amplitude.2.after_ref.first_ref, f32[128,32,128]{2,1,0:T(8,128)S(1)} %amplitude.3.second_ref, bf16[4,64,128]{2,1,0:T(8,128)(2,1)S(1)} %collective-permute-done.5.below_ref.above_ref, ...), custom_call_target="tpu_custom_call" | custom-call | flops 14680064 | bytes 4194304 | tf_op jit(solution)/shard_map/whiten_windows/pallas_call | solution.py:299
  17.2 0.0 collective-permute-done.2.refs_1_
  17.2 0.9 %collective-permute-done.3.refs_2_ = bf16[2,128,128]{2,1,0:T(8,128)(2,1)S(1)} collective-permute-done((bf16[2,128,128]{2,1,0:T(8,128)(2,1)S(1)}, bf16[2,128,128]{2,1,0:T(8,128)(2,1)S(1)}, u32[]{:S(2)}, u32[]{:S(2)}) %collective-permute-start.3) | collective-permute-done | bytes 65568 | tf_op jit(solution)/shard_map/ppermute | solution.py:331
  18.1 0.5 %collective-permute-done.4.refs_3_ = bf16[2,128,128]{2,1,0:T(8,128)(2,1)S(1)} collective-permute-done((bf16[2,128,128]{2,1,0:T(8,128)(2,1)S(1)}, bf16[2,128,128]{2,1,0:T(8,128)(2,1)S(1)}, u32[]{:S(2)}, u32[]{:S(2)}) %collective-permute-start.4) | collective-permute-done | bytes 65568 | tf_op jit(solution)/shard_map/ppermute | solution.py:331
  18.7 0.1 collective-permute-start.6
  18.8 1.5 %collective-permute-done.6.refs_1_ = bf16[8,128,128]{2,1,0:T(8,128)(2,1)S(1)} collective-permute-done((bf16[8,128,128]{2,1,0:T(8,128)(2,1)S(1)}, bf16[8,128,128]{2,1,0:T(8,128)(2,1)S(1)}, u32[]{:S(2)}, u32[]{:S(2)}) %collective-permute-start.6) | collective-permute-done | bytes 262176 | tf_op jit(solution)/shard_map/ppermute | solution.py:331
  20.3 1.7 %cross_spectra.1 = bf16[2,128,16,128]{3,2,1,0:T(8,128)(2,1)} custom-call(bf16[8,128,128]{2,1,0:T(8,128)(2,1)S(1)} %merge_rows.3.refs_0_, bf16[8,128,128]{2,1,0:T(8,128)(2,1)S(1)} %collective-permute-done.6.refs_1_, bf16[2,128,64,128]{3,2,1,0:T(8,128)(2,1)S(1)} %whiten_windows.1.refs_4_.refs_2_), custom_call_target="tpu_custom_call" | custom-call | tf_op jit(solution)/shard_map/cross_spectra/pallas_call | solution.py:417
  (3 shorter events, 0.1 us)
Async XLA Ops:
  0.0 4.2 %copy-start = (bf16[2,128,64,128]{3,2,1,0:T(8,128)(2,1)S(1)}, bf16[2,128,64,128]{3,2,1,0:T(8,128)(2,1)}, u32[]{:S(2)}) copy-start(bf16[2,128,64,128]{3,2,1,0:T(8,128)(2,1)} %spectra_ref.9) | copy-start | bytes 12582916
  1.2 4.7 %collective-permute-start = (bf16[16,256]{1,0:T(8,128)(2,1)S(1)}, bf16[16,256]{1,0:T(8,128)(2,1)S(1)}, u32[]{:S(2)}, u32[]{:S(2)}) collective-permute-start(bf16[16,256]{1,0:T(8,128)(2,1)S(1)} %get-tuple-element.13), channel_id=1, source_target_pairs={{0,1},{1,0},{2,3},{3,2},{4,5},{5,4},{6,7},{7,6},{8,9},{9,8},{10,11... | collective-permute-start | bytes 24584 | tf_op jit(solution)/shard_map/ppermute | solution.py:119
  6.0 5.0 %collective-permute-start.1 = (bf16[1,128,128]{2,1,0:T(8,128)(2,1)S(1)}, bf16[1,128,128]{2,1,0:T(8,128)(2,1)S(1)}, u32[]{:S(2)}, u32[]{:S(2)}) collective-permute-start(bf16[1,128,128]{2,1,0:T(8,128)(2,1)S(1)} %whiten_row.1.refs_0_.after_ref), channel_id=1, source_target_pairs={{0,16},{2,18},{4,20},{6,22},{8,24},{10,26},{12,28},{14,30},{16,0},... | collective-permute-start | bytes 98312 | tf_op jit(solution)/shard_map/ppermute | solution.py:331
  9.2 6.1 %collective-permute-start.5 = (bf16[4,64,128]{2,1,0:T(8,128)(2,1)S(1)}, bf16[4,64,128]{2,1,0:T(8,128)(2,1)S(1)}, u32[]{:S(2)}, u32[]{:S(2)}) collective-permute-start(bf16[4,64,128]{2,1,0:T(8,128)(2,1)S(1)} %end_amplitude.1), channel_id=1, source_target_pairs={{0,1},{1,0},{2,3},{3,2},{4,5},{5,4},{6,7},{7,6},{8,9},{9,8},{10,11... | collective-permute-start | bytes 196616 | tf_op jit(solution)/shard_map/ppermute | solution.py:119
  11.0 6.2 %collective-permute-start.2 = (bf16[2,128,128]{2,1,0:T(8,128)(2,1)S(1)}, bf16[2,128,128]{2,1,0:T(8,128)(2,1)S(1)}, u32[]{:S(2)}, u32[]{:S(2)}) collective-permute-start(bf16[2,128,128]{2,1,0:T(8,128)(2,1)S(1)} %merge_rows.2.refs_0_), channel_id=1, source_target_pairs={{0,12},{2,14},{4,8},{6,10},{8,4},{10,6},{12,0},{14,2},{16,28},{18,... | collective-permute-start | bytes 196616 | tf_op jit(solution)/shard_map/ppermute | solution.py:331
  13.9 4.3 %collective-permute-start.3 = (bf16[2,128,128]{2,1,0:T(8,128)(2,1)S(1)}, bf16[2,128,128]{2,1,0:T(8,128)(2,1)S(1)}, u32[]{:S(2)}, u32[]{:S(2)}) collective-permute-start(bf16[2,128,128]{2,1,0:T(8,128)(2,1)S(1)} %merge_rows.2.refs_0_), channel_id=1, source_target_pairs={{0,4},{2,6},{4,0},{6,2},{8,12},{10,14},{12,8},{14,10},{16,20},{18,... | collective-permute-start | bytes 196616 | tf_op jit(solution)/shard_map/ppermute | solution.py:331
  14.4 4.3 %collective-permute-start.4 = (bf16[2,128,128]{2,1,0:T(8,128)(2,1)S(1)}, bf16[2,128,128]{2,1,0:T(8,128)(2,1)S(1)}, u32[]{:S(2)}, u32[]{:S(2)}) collective-permute-start(bf16[2,128,128]{2,1,0:T(8,128)(2,1)S(1)} %merge_rows.2.refs_0_), channel_id=1, source_target_pairs={{0,8},{2,10},{4,12},{6,14},{8,0},{10,2},{12,4},{14,6},{16,24},{18,... | collective-permute-start | bytes 196616 | tf_op jit(solution)/shard_map/ppermute | solution.py:331
  18.7 1.6 %collective-permute-start.6 = (bf16[8,128,128]{2,1,0:T(8,128)(2,1)S(1)}, bf16[8,128,128]{2,1,0:T(8,128)(2,1)S(1)}, u32[]{:S(2)}, u32[]{:S(2)}) collective-permute-start(bf16[8,128,128]{2,1,0:T(8,128)(2,1)S(1)} %merge_rows.3.refs_0_), channel_id=1, source_target_pairs={{0,2},{2,0},{4,6},{6,4},{8,10},{10,8},{12,14},{14,12},{16,18},{18,... | collective-permute-start | bytes 786440 | tf_op jit(solution)/shard_map/ppermute | solution.py:331

commit v9 on v8

--- a/solution.py
+++ b/solution.py
@@ -412,7 +412,7 @@
     sources = len(offsets)
     _, bins, width = blocks[0].shape
     channels = whitened.shape[-1]
-    ends = [k * bins // 32 for k in (8, 16, 24, 28, 32)]
+    ends = sorted({k * bins // 128 * 4 for k in (10, 20, 28, 31, 32)})
     shape = (2, bins, sources, channels)
     return pl.pallas_call(
         functools.partial(cross_kernel, offsets, ends),

time: 22.1 us -> 22.1 us (level)
  no operation moved by 1% of the time
where the time goes in v9:
time: 22.1 us; the launch traced here: 21.9 us
  starting transfers between devices  11.3 us (51%)
  Pallas kernels  7.35 us (33%)
  waiting for transfers between devices  3.21 us (15%)
    ppermute x5, starting transfers between devices, send(): return lax.ppermute(rows, 'rx', [(i, i ^ bit) for i in range(count)])  6.65 us
    ppermute x2, starting transfers between devices, band_neighbours(): received = lax.ppermute(ends[0], 'band', [(0, 1), (1, 0)])  4.62 us
    ppermute x5, waiting for transfers between devices, send(): return lax.ppermute(rows, 'rx', [(i, i ^ bit) for i in range(count)])  3.2 us
    pallas_call x1, Pallas kernels, whiten(): pl.pallas_call(whiten_kernel, in_specs=[VMEM] * (5 + len(after)), out_spe...  1.97 us
    pallas_call x1, Pallas kernels, cross_spectra(): pl.pallas_call(functools.partial(cross_kernel, offsets, ends), in_specs=[...  1.63 us
    pallas_call x2, Pallas kernels, amplitudes(): pl.pallas_call(functools.partial(amplitude_kernel, half * windows // 2),...  1.45 us
    pallas_call x1, Pallas kernels, edge_amplitudes(): pl.pallas_call(edge_kernel, in_specs=[HBM, HBM], out_specs=[VMEM] * (2 *...  1.17 us
    pallas_call x1, Pallas kernels, extract_row(): pl.pallas_call(functools.partial(extract_kernel, chunks), in_specs=[VMEM]...  0.9 us
  transfers between devices with their start and end apart: 7, of which 4 were waited for; matrix products, arithmetic and copies ran while one was open for 0% of the time, Pallas kernels for 20%

profile of v9, /device:TPU:0, one launch (start us, length us, event | category | flops | bytes accessed | tf_op | source)
XLA Modules:
  0.0 21.9 jit_solution(12639375754574321172)
XLA Ops:
  0.0 0.0 copy-start
  0.0 1.2 %edge_amplitude.1 = (bf16[2,4,64,128]{3,2,1,0:T(8,128)(2,1)S(1)}, bf16[16,256]{1,0:T(8,128)(2,1)S(1)}, s32[8,128]{1,0:T(8,128)S(1)}) custom-call(s32[16]{0:T(128)} %index_ref.1, bf16[2,128,64,128]{3,2,1,0:T(8,128)(2,1)} %spectra_ref.9), custom_call_target="tpu_custom_call" | custom-call | tf_op jit(solution)/shard_map/edge_amplitude/pallas_call | solution.py:82
  1.2 3.0 %collective-permute-start = (bf16[16,256]{1,0:T(8,128)(2,1)S(1)}, bf16[16,256]{1,0:T(8,128)(2,1)S(1)}, u32[]{:S(2)}, u32[]{:S(2)}) collective-permute-start(bf16[16,256]{1,0:T(8,128)(2,1)S(1)} %get-tuple-element.13), channel_id=1, source_target_pairs={{0,1},{1,0},{2,3},{3,2},{4,5},{5,4},{6,7},{7,6},{8,9},{9,8},{10,11... | collective-permute-start | bytes 24584 | tf_op jit(solution)/shard_map/ppermute | solution.py:119
  4.2 0.0 copy-done
  4.2 0.9 %extract_row.1 = (f32[128,128]{1,0:T(8,128)S(1)}, f32[128,128]{1,0:T(8,128)S(1)}) custom-call(s32[8,128]{1,0:T(8,128)S(1)} %get-tuple-element.10.column_ref, bf16[2,128,64,128]{3,2,1,0:T(8,128)(2,1)S(1)} %copy-done), custom_call_target="tpu_custom_call" | custom-call | bytes 8388608 | tf_op jit(solution)/shard_map/extract_row/pallas_call | solution.py:185
  5.1 0.7 %amplitude.2.after_ref.first_ref = f32[128,32,128]{2,1,0:T(8,128)S(1)} custom-call(bf16[2,128,64,128]{3,2,1,0:T(8,128)(2,1)S(1)} %copy-done, f32[128,128]{1,0:T(8,128)S(1)} %get-tuple-element.11.refs_0_.row_ref), custom_call_target="tpu_custom_call" | custom-call | flops 5242880 | bytes 2097152 | tf_op jit(solution)/shard_map/amplitude/pallas_call | solution.py:248
  5.9 0.0 collective-permute-done.below_ref.above_ref
  5.9 0.2 whiten_row.1.refs_0_.after_ref
  6.0 3.1 %collective-permute-start.1 = (bf16[1,128,128]{2,1,0:T(8,128)(2,1)S(1)}, bf16[1,128,128]{2,1,0:T(8,128)(2,1)S(1)}, u32[]{:S(2)}, u32[]{:S(2)}) collective-permute-start(bf16[1,128,128]{2,1,0:T(8,128)(2,1)S(1)} %whiten_row.1.refs_0_.after_ref), channel_id=1, source_target_pairs={{0,16},{2,18},{4,20},{6,22},{8,24},{10,26},{12,28},{14,30},{16,0},... | collective-permute-start | bytes 98312 | tf_op jit(solution)/shard_map/ppermute | solution.py:331
  9.2 1.6 %collective-permute-start.5 = (bf16[4,64,128]{2,1,0:T(8,128)(2,1)S(1)}, bf16[4,64,128]{2,1,0:T(8,128)(2,1)S(1)}, u32[]{:S(2)}, u32[]{:S(2)}) collective-permute-start(bf16[4,64,128]{2,1,0:T(8,128)(2,1)S(1)} %end_amplitude.1), channel_id=1, source_target_pairs={{0,1},{1,0},{2,3},{3,2},{4,5},{5,4},{6,7},{7,6},{8,9},{9,8},{10,11... | collective-permute-start | bytes 196616 | tf_op jit(solution)/shard_map/ppermute | solution.py:119
  10.8 0.3 %collective-permute-done.1.refs_1_ = bf16[1,128,128]{2,1,0:T(8,128)(2,1)S(1)} collective-permute-done((bf16[1,128,128]{2,1,0:T(8,128)(2,1)S(1)}, bf16[1,128,128]{2,1,0:T(8,128)(2,1)S(1)}, u32[]{:S(2)}, u32[]{:S(2)}) %collective-permute-start.1) | collective-permute-done | bytes 32800 | tf_op jit(solution)/shard_map/ppermute | solution.py:331
  11.0 2.8 %collective-permute-start.2 = (bf16[2,128,128]{2,1,0:T(8,128)(2,1)S(1)}, bf16[2,128,128]{2,1,0:T(8,128)(2,1)S(1)}, u32[]{:S(2)}, u32[]{:S(2)}) collective-permute-start(bf16[2,128,128]{2,1,0:T(8,128)(2,1)S(1)} %merge_rows.2.refs_0_), channel_id=1, source_target_pairs={{0,12},{2,14},{4,8},{6,10},{8,4},{10,6},{12,0},{14,2},{16,28},{18,... | collective-permute-start | bytes 196616 | tf_op jit(solution)/shard_map/ppermute | solution.py:331
  13.9 0.5 %collective-permute-start.3 = (bf16[2,128,128]{2,1,0:T(8,128)(2,1)S(1)}, bf16[2,128,128]{2,1,0:T(8,128)(2,1)S(1)}, u32[]{:S(2)}, u32[]{:S(2)}) collective-permute-start(bf16[2,128,128]{2,1,0:T(8,128)(2,1)S(1)} %merge_rows.2.refs_0_), channel_id=1, source_target_pairs={{0,4},{2,6},{4,0},{6,2},{8,12},{10,14},{12,8},{14,10},{16,20},{18,... | collective-permute-start | bytes 196616 | tf_op jit(solution)/shard_map/ppermute | solution.py:331
  14.4 0.1 collective-permute-start.4
  14.5 0.7 %amplitude.3.second_ref = f32[128,32,128]{2,1,0:T(8,128)S(1)} custom-call(bf16[2,128,64,128]{3,2,1,0:T(8,128)(2,1)S(1)} %copy-done, bf16[2,128,128]{2,1,0:T(8,128)(2,1)S(1)} %merge_rows.2.refs_0_), custom_call_target="tpu_custom_call" | custom-call | flops 5242880 | bytes 2097152 | tf_op jit(solution)/shard_map/amplitude/pallas_call | solution.py:248
  15.3 0.0 collective-permute-done.5.below_ref.above_ref
  15.3 2.0 %whiten_windows.1.refs_4_.refs_2_ = bf16[2,128,64,128]{3,2,1,0:T(8,128)(2,1)S(1)} custom-call(bf16[2,128,64,128]{3,2,1,0:T(8,128)(2,1)S(1)} %copy-done, f32[128,32,128]{2,1,0:T(8,128)S(1)} %amplitude.2.after_ref.first_ref, f32[128,32,128]{2,1,0:T(8,128)S(1)} %amplitude.3.second_ref, bf16[4,64,128]{2,1,0:T(8,128)(2,1)S(1)} %collective-permute-done.5.below_ref.above_ref, ...), custom_call_target="tpu_custom_call" | custom-call | flops 14680064 | bytes 4194304 | tf_op jit(solution)/shard_map/whiten_windows/pallas_call | solution.py:299
  17.2 0.0 collective-permute-done.2.refs_1_
  17.2 0.9 %collective-permute-done.3.refs_2_ = bf16[2,128,128]{2,1,0:T(8,128)(2,1)S(1)} collective-permute-done((bf16[2,128,128]{2,1,0:T(8,128)(2,1)S(1)}, bf16[2,128,128]{2,1,0:T(8,128)(2,1)S(1)}, u32[]{:S(2)}, u32[]{:S(2)}) %collective-permute-start.3) | collective-permute-done | bytes 65568 | tf_op jit(solution)/shard_map/ppermute | solution.py:331
  18.1 0.5 %collective-permute-done.4.refs_3_ = bf16[2,128,128]{2,1,0:T(8,128)(2,1)S(1)} collective-permute-done((bf16[2,128,128]{2,1,0:T(8,128)(2,1)S(1)}, bf16[2,128,128]{2,1,0:T(8,128)(2,1)S(1)}, u32[]{:S(2)}, u32[]{:S(2)}) %collective-permute-start.4) | collective-permute-done | bytes 65568 | tf_op jit(solution)/shard_map/ppermute | solution.py:331
  18.7 0.1 collective-permute-start.6
  18.8 1.5 %collective-permute-done.6.refs_1_ = bf16[8,128,128]{2,1,0:T(8,128)(2,1)S(1)} collective-permute-done((bf16[8,128,128]{2,1,0:T(8,128)(2,1)S(1)}, bf16[8,128,128]{2,1,0:T(8,128)(2,1)S(1)}, u32[]{:S(2)}, u32[]{:S(2)}) %collective-permute-start.6) | collective-permute-done | bytes 262176 | tf_op jit(solution)/shard_map/ppermute | solution.py:331
  20.3 1.6 %cross_spectra.1 = bf16[2,128,16,128]{3,2,1,0:T(8,128)(2,1)} custom-call(bf16[8,128,128]{2,1,0:T(8,128)(2,1)S(1)} %merge_rows.3.refs_0_, bf16[8,128,128]{2,1,0:T(8,128)(2,1)S(1)} %collective-permute-done.6.refs_1_, bf16[2,128,64,128]{3,2,1,0:T(8,128)(2,1)S(1)} %whiten_windows.1.refs_4_.refs_2_), custom_call_target="tpu_custom_call" | custom-call | tf_op jit(solution)/shard_map/cross_spectra/pallas_call | solution.py:417
  (3 shorter events, 0.1 us)
Async XLA Ops:
  0.0 4.2 %copy-start = (bf16[2,128,64,128]{3,2,1,0:T(8,128)(2,1)S(1)}, bf16[2,128,64,128]{3,2,1,0:T(8,128)(2,1)}, u32[]{:S(2)}) copy-start(bf16[2,128,64,128]{3,2,1,0:T(8,128)(2,1)} %spectra_ref.9) | copy-start | bytes 12582916
  1.2 4.7 %collective-permute-start = (bf16[16,256]{1,0:T(8,128)(2,1)S(1)}, bf16[16,256]{1,0:T(8,128)(2,1)S(1)}, u32[]{:S(2)}, u32[]{:S(2)}) collective-permute-start(bf16[16,256]{1,0:T(8,128)(2,1)S(1)} %get-tuple-element.13), channel_id=1, source_target_pairs={{0,1},{1,0},{2,3},{3,2},{4,5},{5,4},{6,7},{7,6},{8,9},{9,8},{10,11... | collective-permute-start | bytes 24584 | tf_op jit(solution)/shard_map/ppermute | solution.py:119
  6.0 5.0 %collective-permute-start.1 = (bf16[1,128,128]{2,1,0:T(8,128)(2,1)S(1)}, bf16[1,128,128]{2,1,0:T(8,128)(2,1)S(1)}, u32[]{:S(2)}, u32[]{:S(2)}) collective-permute-start(bf16[1,128,128]{2,1,0:T(8,128)(2,1)S(1)} %whiten_row.1.refs_0_.after_ref), channel_id=1, source_target_pairs={{0,16},{2,18},{4,20},{6,22},{8,24},{10,26},{12,28},{14,30},{16,0},... | collective-permute-start | bytes 98312 | tf_op jit(solution)/shard_map/ppermute | solution.py:331
  9.2 6.1 %collective-permute-start.5 = (bf16[4,64,128]{2,1,0:T(8,128)(2,1)S(1)}, bf16[4,64,128]{2,1,0:T(8,128)(2,1)S(1)}, u32[]{:S(2)}, u32[]{:S(2)}) collective-permute-start(bf16[4,64,128]{2,1,0:T(8,128)(2,1)S(1)} %end_amplitude.1), channel_id=1, source_target_pairs={{0,1},{1,0},{2,3},{3,2},{4,5},{5,4},{6,7},{7,6},{8,9},{9,8},{10,11... | collective-permute-start | bytes 196616 | tf_op jit(solution)/shard_map/ppermute | solution.py:119
  11.0 6.2 %collective-permute-start.2 = (bf16[2,128,128]{2,1,0:T(8,128)(2,1)S(1)}, bf16[2,128,128]{2,1,0:T(8,128)(2,1)S(1)}, u32[]{:S(2)}, u32[]{:S(2)}) collective-permute-start(bf16[2,128,128]{2,1,0:T(8,128)(2,1)S(1)} %merge_rows.2.refs_0_), channel_id=1, source_target_pairs={{0,12},{2,14},{4,8},{6,10},{8,4},{10,6},{12,0},{14,2},{16,28},{18,... | collective-permute-start | bytes 196616 | tf_op jit(solution)/shard_map/ppermute | solution.py:331
  13.9 4.3 %collective-permute-start.3 = (bf16[2,128,128]{2,1,0:T(8,128)(2,1)S(1)}, bf16[2,128,128]{2,1,0:T(8,128)(2,1)S(1)}, u32[]{:S(2)}, u32[]{:S(2)}) collective-permute-start(bf16[2,128,128]{2,1,0:T(8,128)(2,1)S(1)} %merge_rows.2.refs_0_), channel_id=1, source_target_pairs={{0,4},{2,6},{4,0},{6,2},{8,12},{10,14},{12,8},{14,10},{16,20},{18,... | collective-permute-start | bytes 196616 | tf_op jit(solution)/shard_map/ppermute | solution.py:331
  14.4 4.3 %collective-permute-start.4 = (bf16[2,128,128]{2,1,0:T(8,128)(2,1)S(1)}, bf16[2,128,128]{2,1,0:T(8,128)(2,1)S(1)}, u32[]{:S(2)}, u32[]{:S(2)}) collective-permute-start(bf16[2,128,128]{2,1,0:T(8,128)(2,1)S(1)} %merge_rows.2.refs_0_), channel_id=1, source_target_pairs={{0,8},{2,10},{4,12},{6,14},{8,0},{10,2},{12,4},{14,6},{16,24},{18,... | collective-permute-start | bytes 196616 | tf_op jit(solution)/shard_map/ppermute | solution.py:331
  18.7 1.6 %collective-permute-start.6 = (bf16[8,128,128]{2,1,0:T(8,128)(2,1)S(1)}, bf16[8,128,128]{2,1,0:T(8,128)(2,1)S(1)}, u32[]{:S(2)}, u32[]{:S(2)}) collective-permute-start(bf16[8,128,128]{2,1,0:T(8,128)(2,1)S(1)} %merge_rows.3.refs_0_), channel_id=1, source_target_pairs={{0,2},{2,0},{4,6},{6,4},{8,10},{10,8},{12,14},{14,12},{16,18},{18,... | collective-permute-start | bytes 786440 | tf_op jit(solution)/shard_map/ppermute | solution.py:331

commit v10 on v9

--- a/solution.py
+++ b/solution.py
@@ -347,11 +347,11 @@
     edges = band_neighbours([end_amplitudes(end, rows) for end in ends])
     rows = merge([rows, from_far], [])
     held = held + shifted(held, far)
-    others = [send(rows, bit) for bit in (near ^ across, across, near)]
+    others = [send(rows, bit) for bit in (near ^ across, near, across)]
     second = amplitudes(spectra, 1, rows)
     whitened = whiten(spectra, (first, second), edges, [rows])
     rows = merge([rows, *others], [whitened])
-    held = held + shifted(held, near ^ across) + shifted(held, across) + shifted(held, near)
+    held = held + shifted(held, near ^ across) + shifted(held, near) + shifted(held, across)
     return [rows, send(rows, core)], held + shifted(held, core), whitened
 
 

time: 22.1 us -> 22 us (level)
  no operation moved by 1% of the time
where the time goes in v10:
time: 22 us; the launch traced here: 21.8 us
  starting transfers between devices  11.3 us (51%)
  Pallas kernels  7.36 us (33%)
  waiting for transfers between devices  3.12 us (14%)
    ppermute x5, starting transfers between devices, send(): return lax.ppermute(rows, 'rx', [(i, i ^ bit) for i in range(count)])  6.65 us
    ppermute x2, starting transfers between devices, band_neighbours(): received = lax.ppermute(ends[0], 'band', [(0, 1), (1, 0)])  4.62 us
    ppermute x5, waiting for transfers between devices, send(): return lax.ppermute(rows, 'rx', [(i, i ^ bit) for i in range(count)])  3.12 us
    pallas_call x1, Pallas kernels, whiten(): pl.pallas_call(whiten_kernel, in_specs=[VMEM] * (5 + len(after)), out_spe...  1.97 us
    pallas_call x1, Pallas kernels, cross_spectra(): pl.pallas_call(functools.partial(cross_kernel, offsets, ends), in_specs=[...  1.63 us
    pallas_call x2, Pallas kernels, amplitudes(): pl.pallas_call(functools.partial(amplitude_kernel, half * windows // 2),...  1.45 us
    pallas_call x1, Pallas kernels, edge_amplitudes(): pl.pallas_call(edge_kernel, in_specs=[HBM, HBM], out_specs=[VMEM] * (2 *...  1.17 us
    pallas_call x1, Pallas kernels, extract_row(): pl.pallas_call(functools.partial(extract_kernel, chunks), in_specs=[VMEM]...  0.9 us
  transfers between devices with their start and end apart: 7, of which 4 were waited for; matrix products, arithmetic and copies ran while one was open for 0% of the time, Pallas kernels for 20%

profile of v10, /device:TPU:0, one launch (start us, length us, event | category | flops | bytes accessed | tf_op | source)
XLA Modules:
  0.0 21.8 jit_solution(13281639629392587283)
XLA Ops:
  0.0 0.0 copy-start
  0.0 1.2 %edge_amplitude.1 = (bf16[2,4,64,128]{3,2,1,0:T(8,128)(2,1)S(1)}, bf16[16,256]{1,0:T(8,128)(2,1)S(1)}, s32[8,128]{1,0:T(8,128)S(1)}) custom-call(s32[16]{0:T(128)} %index_ref.1, bf16[2,128,64,128]{3,2,1,0:T(8,128)(2,1)} %spectra_ref.9), custom_call_target="tpu_custom_call" | custom-call | tf_op jit(solution)/shard_map/edge_amplitude/pallas_call | solution.py:82
  1.2 3.0 %collective-permute-start = (bf16[16,256]{1,0:T(8,128)(2,1)S(1)}, bf16[16,256]{1,0:T(8,128)(2,1)S(1)}, u32[]{:S(2)}, u32[]{:S(2)}) collective-permute-start(bf16[16,256]{1,0:T(8,128)(2,1)S(1)} %get-tuple-element.13), channel_id=1, source_target_pairs={{0,1},{1,0},{2,3},{3,2},{4,5},{5,4},{6,7},{7,6},{8,9},{9,8},{10,11... | collective-permute-start | bytes 24584 | tf_op jit(solution)/shard_map/ppermute | solution.py:119
  4.2 0.0 copy-done
  4.2 0.9 %extract_row.1 = (f32[128,128]{1,0:T(8,128)S(1)}, f32[128,128]{1,0:T(8,128)S(1)}) custom-call(s32[8,128]{1,0:T(8,128)S(1)} %get-tuple-element.10.column_ref, bf16[2,128,64,128]{3,2,1,0:T(8,128)(2,1)S(1)} %copy-done), custom_call_target="tpu_custom_call" | custom-call | bytes 8388608 | tf_op jit(solution)/shard_map/extract_row/pallas_call | solution.py:185
  5.1 0.7 %amplitude.2.after_ref.first_ref = f32[128,32,128]{2,1,0:T(8,128)S(1)} custom-call(bf16[2,128,64,128]{3,2,1,0:T(8,128)(2,1)S(1)} %copy-done, f32[128,128]{1,0:T(8,128)S(1)} %get-tuple-element.11.refs_0_.row_ref), custom_call_target="tpu_custom_call" | custom-call | flops 5242880 | bytes 2097152 | tf_op jit(solution)/shard_map/amplitude/pallas_call | solution.py:248
  5.9 0.0 collective-permute-done.below_ref.above_ref
  5.9 0.2 whiten_row.1.refs_0_.after_ref
  6.0 3.1 %collective-permute-start.1 = (bf16[1,128,128]{2,1,0:T(8,128)(2,1)S(1)}, bf16[1,128,128]{2,1,0:T(8,128)(2,1)S(1)}, u32[]{:S(2)}, u32[]{:S(2)}) collective-permute-start(bf16[1,128,128]{2,1,0:T(8,128)(2,1)S(1)} %whiten_row.1.refs_0_.after_ref), channel_id=1, source_target_pairs={{0,16},{2,18},{4,20},{6,22},{8,24},{10,26},{12,28},{14,30},{16,0},... | collective-permute-start | bytes 98312 | tf_op jit(solution)/shard_map/ppermute | solution.py:331
  9.2 1.6 %collective-permute-start.5 = (bf16[4,64,128]{2,1,0:T(8,128)(2,1)S(1)}, bf16[4,64,128]{2,1,0:T(8,128)(2,1)S(1)}, u32[]{:S(2)}, u32[]{:S(2)}) collective-permute-start(bf16[4,64,128]{2,1,0:T(8,128)(2,1)S(1)} %end_amplitude.1), channel_id=1, source_target_pairs={{0,1},{1,0},{2,3},{3,2},{4,5},{5,4},{6,7},{7,6},{8,9},{9,8},{10,11... | collective-permute-start | bytes 196616 | tf_op jit(solution)/shard_map/ppermute | solution.py:119
  10.8 0.3 %collective-permute-done.1.refs_1_ = bf16[1,128,128]{2,1,0:T(8,128)(2,1)S(1)} collective-permute-done((bf16[1,128,128]{2,1,0:T(8,128)(2,1)S(1)}, bf16[1,128,128]{2,1,0:T(8,128)(2,1)S(1)}, u32[]{:S(2)}, u32[]{:S(2)}) %collective-permute-start.1) | collective-permute-done | bytes 32800 | tf_op jit(solution)/shard_map/ppermute | solution.py:331
  11.0 2.8 %collective-permute-start.2 = (bf16[2,128,128]{2,1,0:T(8,128)(2,1)S(1)}, bf16[2,128,128]{2,1,0:T(8,128)(2,1)S(1)}, u32[]{:S(2)}, u32[]{:S(2)}) collective-permute-start(bf16[2,128,128]{2,1,0:T(8,128)(2,1)S(1)} %merge_rows.2.refs_0_), channel_id=1, source_target_pairs={{0,12},{2,14},{4,8},{6,10},{8,4},{10,6},{12,0},{14,2},{16,28},{18,... | collective-permute-start | bytes 196616 | tf_op jit(solution)/shard_map/ppermute | solution.py:331
  13.9 0.4 %collective-permute-start.3 = (bf16[2,128,128]{2,1,0:T(8,128)(2,1)S(1)}, bf16[2,128,128]{2,1,0:T(8,128)(2,1)S(1)}, u32[]{:S(2)}, u32[]{:S(2)}) collective-permute-start(bf16[2,128,128]{2,1,0:T(8,128)(2,1)S(1)} %merge_rows.2.refs_0_), channel_id=1, source_target_pairs={{0,8},{2,10},{4,12},{6,14},{8,0},{10,2},{12,4},{14,6},{16,24},{18,... | collective-permute-start | bytes 196616 | tf_op jit(solution)/shard_map/ppermute | solution.py:331
  14.3 0.2 collective-permute-start.4
  14.5 0.7 %amplitude.3.second_ref = f32[128,32,128]{2,1,0:T(8,128)S(1)} custom-call(bf16[2,128,64,128]{3,2,1,0:T(8,128)(2,1)S(1)} %copy-done, bf16[2,128,128]{2,1,0:T(8,128)(2,1)S(1)} %merge_rows.2.refs_0_), custom_call_target="tpu_custom_call" | custom-call | flops 5242880 | bytes 2097152 | tf_op jit(solution)/shard_map/amplitude/pallas_call | solution.py:248
  15.3 0.0 collective-permute-done.5.below_ref.above_ref
  15.3 2.0 %whiten_windows.1.refs_4_.refs_2_ = bf16[2,128,64,128]{3,2,1,0:T(8,128)(2,1)S(1)} custom-call(bf16[2,128,64,128]{3,2,1,0:T(8,128)(2,1)S(1)} %copy-done, f32[128,32,128]{2,1,0:T(8,128)S(1)} %amplitude.2.after_ref.first_ref, f32[128,32,128]{2,1,0:T(8,128)S(1)} %amplitude.3.second_ref, bf16[4,64,128]{2,1,0:T(8,128)(2,1)S(1)} %collective-permute-done.5.below_ref.above_ref, ...), custom_call_target="tpu_custom_call" | custom-call | flops 14680064 | bytes 4194304 | tf_op jit(solution)/shard_map/whiten_windows/pallas_call | solution.py:299
  17.2 0.0 collective-permute-done.2.refs_1_
  17.2 0.9 %collective-permute-done.3.refs_2_ = bf16[2,128,128]{2,1,0:T(8,128)(2,1)S(1)} collective-permute-done((bf16[2,128,128]{2,1,0:T(8,128)(2,1)S(1)}, bf16[2,128,128]{2,1,0:T(8,128)(2,1)S(1)}, u32[]{:S(2)}, u32[]{:S(2)}) %collective-permute-start.3) | collective-permute-done | bytes 65568 | tf_op jit(solution)/shard_map/ppermute | solution.py:331
  18.1 0.4 %collective-permute-done.4.refs_3_ = bf16[2,128,128]{2,1,0:T(8,128)(2,1)S(1)} collective-permute-done((bf16[2,128,128]{2,1,0:T(8,128)(2,1)S(1)}, bf16[2,128,128]{2,1,0:T(8,128)(2,1)S(1)}, u32[]{:S(2)}, u32[]{:S(2)}) %collective-permute-start.4) | collective-permute-done | bytes 65568 | tf_op jit(solution)/shard_map/ppermute | solution.py:331
  18.6 0.1 collective-permute-start.6
  18.7 1.5 %collective-permute-done.6.refs_1_ = bf16[8,128,128]{2,1,0:T(8,128)(2,1)S(1)} collective-permute-done((bf16[8,128,128]{2,1,0:T(8,128)(2,1)S(1)}, bf16[8,128,128]{2,1,0:T(8,128)(2,1)S(1)}, u32[]{:S(2)}, u32[]{:S(2)}) %collective-permute-start.6) | collective-permute-done | bytes 262176 | tf_op jit(solution)/shard_map/ppermute | solution.py:331
  20.2 1.6 %cross_spectra.1 = bf16[2,128,16,128]{3,2,1,0:T(8,128)(2,1)} custom-call(bf16[8,128,128]{2,1,0:T(8,128)(2,1)S(1)} %merge_rows.3.refs_0_, bf16[8,128,128]{2,1,0:T(8,128)(2,1)S(1)} %collective-permute-done.6.refs_1_, bf16[2,128,64,128]{3,2,1,0:T(8,128)(2,1)S(1)} %whiten_windows.1.refs_4_.refs_2_), custom_call_target="tpu_custom_call" | custom-call | tf_op jit(solution)/shard_map/cross_spectra/pallas_call | solution.py:417
  (3 shorter events, 0.1 us)
Async XLA Ops:
  0.0 4.2 %copy-start = (bf16[2,128,64,128]{3,2,1,0:T(8,128)(2,1)S(1)}, bf16[2,128,64,128]{3,2,1,0:T(8,128)(2,1)}, u32[]{:S(2)}) copy-start(bf16[2,128,64,128]{3,2,1,0:T(8,128)(2,1)} %spectra_ref.9) | copy-start | bytes 12582916
  1.2 4.7 %collective-permute-start = (bf16[16,256]{1,0:T(8,128)(2,1)S(1)}, bf16[16,256]{1,0:T(8,128)(2,1)S(1)}, u32[]{:S(2)}, u32[]{:S(2)}) collective-permute-start(bf16[16,256]{1,0:T(8,128)(2,1)S(1)} %get-tuple-element.13), channel_id=1, source_target_pairs={{0,1},{1,0},{2,3},{3,2},{4,5},{5,4},{6,7},{7,6},{8,9},{9,8},{10,11... | collective-permute-start | bytes 24584 | tf_op jit(solution)/shard_map/ppermute | solution.py:119
  6.0 5.0 %collective-permute-start.1 = (bf16[1,128,128]{2,1,0:T(8,128)(2,1)S(1)}, bf16[1,128,128]{2,1,0:T(8,128)(2,1)S(1)}, u32[]{:S(2)}, u32[]{:S(2)}) collective-permute-start(bf16[1,128,128]{2,1,0:T(8,128)(2,1)S(1)} %whiten_row.1.refs_0_.after_ref), channel_id=1, source_target_pairs={{0,16},{2,18},{4,20},{6,22},{8,24},{10,26},{12,28},{14,30},{16,0},... | collective-permute-start | bytes 98312 | tf_op jit(solution)/shard_map/ppermute | solution.py:331
  9.2 6.1 %collective-permute-start.5 = (bf16[4,64,128]{2,1,0:T(8,128)(2,1)S(1)}, bf16[4,64,128]{2,1,0:T(8,128)(2,1)S(1)}, u32[]{:S(2)}, u32[]{:S(2)}) collective-permute-start(bf16[4,64,128]{2,1,0:T(8,128)(2,1)S(1)} %end_amplitude.1), channel_id=1, source_target_pairs={{0,1},{1,0},{2,3},{3,2},{4,5},{5,4},{6,7},{7,6},{8,9},{9,8},{10,11... | collective-permute-start | bytes 196616 | tf_op jit(solution)/shard_map/ppermute | solution.py:119
  11.0 6.2 %collective-permute-start.2 = (bf16[2,128,128]{2,1,0:T(8,128)(2,1)S(1)}, bf16[2,128,128]{2,1,0:T(8,128)(2,1)S(1)}, u32[]{:S(2)}, u32[]{:S(2)}) collective-permute-start(bf16[2,128,128]{2,1,0:T(8,128)(2,1)S(1)} %merge_rows.2.refs_0_), channel_id=1, source_target_pairs={{0,12},{2,14},{4,8},{6,10},{8,4},{10,6},{12,0},{14,2},{16,28},{18,... | collective-permute-start | bytes 196616 | tf_op jit(solution)/shard_map/ppermute | solution.py:331
  13.9 4.3 %collective-permute-start.3 = (bf16[2,128,128]{2,1,0:T(8,128)(2,1)S(1)}, bf16[2,128,128]{2,1,0:T(8,128)(2,1)S(1)}, u32[]{:S(2)}, u32[]{:S(2)}) collective-permute-start(bf16[2,128,128]{2,1,0:T(8,128)(2,1)S(1)} %merge_rows.2.refs_0_), channel_id=1, source_target_pairs={{0,8},{2,10},{4,12},{6,14},{8,0},{10,2},{12,4},{14,6},{16,24},{18,... | collective-permute-start | bytes 196616 | tf_op jit(solution)/shard_map/ppermute | solution.py:331
  14.3 4.3 %collective-permute-start.4 = (bf16[2,128,128]{2,1,0:T(8,128)(2,1)S(1)}, bf16[2,128,128]{2,1,0:T(8,128)(2,1)S(1)}, u32[]{:S(2)}, u32[]{:S(2)}) collective-permute-start(bf16[2,128,128]{2,1,0:T(8,128)(2,1)S(1)} %merge_rows.2.refs_0_), channel_id=1, source_target_pairs={{0,4},{2,6},{4,0},{6,2},{8,12},{10,14},{12,8},{14,10},{16,20},{18,... | collective-permute-start | bytes 196616 | tf_op jit(solution)/shard_map/ppermute | solution.py:331
  18.6 1.6 %collective-permute-start.6 = (bf16[8,128,128]{2,1,0:T(8,128)(2,1)S(1)}, bf16[8,128,128]{2,1,0:T(8,128)(2,1)S(1)}, u32[]{:S(2)}, u32[]{:S(2)}) collective-permute-start(bf16[8,128,128]{2,1,0:T(8,128)(2,1)S(1)} %merge_rows.3.refs_0_), channel_id=1, source_target_pairs={{0,2},{2,0},{4,6},{6,4},{8,10},{10,8},{12,14},{14,12},{16,18},{18,... | collective-permute-start | bytes 786440 | tf_op jit(solution)/shard_map/ppermute | solution.py:331

commit v11 on v9

--- a/solution.py
+++ b/solution.py
@@ -52,17 +52,19 @@
                 copy = pltpu.make_async_copy(spectra_ref.at[part, start + j], out_refs[k].at[part, j], sem.at[len(copies)])
                 copy.start()
                 copies.append(copy)
-    index_copy.wait()
-    rank = lax.axis_index("rx")
-    column = jnp.full(column_ref.shape, scalars[rank] - rank * channels, jnp.int32)
-    column_ref[...] = column
     masks = window_masks(windows)
+    column = None
     for k in range(ends):
         for copy in copies[2 * HALF * k : 2 * HALF * (k + 1)]:
             copy.wait()
         real = out_refs[k][0].astype(jnp.float32)
         imag = out_refs[k][1].astype(jnp.float32)
         amplitude = amplitude_of(real * real + imag * imag).astype(jnp.float32)
+        if column is None:
+            index_copy.wait()
+            rank = lax.axis_index("rx")
+            column = jnp.full(column_ref.shape, scalars[rank] - rank * channels, jnp.int32)
+            column_ref[...] = column
         pairs = []
         for first in range(0, HALF, 2):
             total = jnp.zeros((8, 2 * windows), jnp.float32)

time: 22.1 us -> 22.1 us (level)
  no operation moved by 1% of the time
where the time goes in v11:
time: 22.1 us; the launch traced here: 22 us
  starting transfers between devices  11.3 us (51%)
  Pallas kernels  7.4 us (33%)
  waiting for transfers between devices  3.21 us (15%)
    ppermute x5, starting transfers between devices, send(): return lax.ppermute(rows, 'rx', [(i, i ^ bit) for i in range(count)])  6.65 us
    ppermute x2, starting transfers between devices, band_neighbours(): received = lax.ppermute(ends[0], 'band', [(0, 1), (1, 0)])  4.62 us
    ppermute x5, waiting for transfers between devices, send(): return lax.ppermute(rows, 'rx', [(i, i ^ bit) for i in range(count)])  3.2 us
    pallas_call x1, Pallas kernels, whiten(): pl.pallas_call(whiten_kernel, in_specs=[VMEM] * (5 + len(after)), out_spe...  1.97 us
    pallas_call x1, Pallas kernels, cross_spectra(): pl.pallas_call(functools.partial(cross_kernel, offsets, ends), in_specs=[...  1.63 us
    pallas_call x2, Pallas kernels, amplitudes(): pl.pallas_call(functools.partial(amplitude_kernel, half * windows // 2),...  1.45 us
    pallas_call x1, Pallas kernels, edge_amplitudes(): pl.pallas_call(edge_kernel, in_specs=[HBM, HBM], out_specs=[VMEM] * (2 *...  1.21 us
    pallas_call x1, Pallas kernels, extract_row(): pl.pallas_call(functools.partial(extract_kernel, chunks), in_specs=[VMEM]...  0.9 us
  transfers between devices with their start and end apart: 7, of which 4 were waited for; matrix products, arithmetic and copies ran while one was open for 0% of the time, Pallas kernels for 20%

profile of v11, /device:TPU:0, one launch (start us, length us, event | category | flops | bytes accessed | tf_op | source)
XLA Modules:
  0.0 22.0 jit_solution(10185224690856338605)
XLA Ops:
  0.0 0.0 copy-start
  0.0 1.2 %edge_amplitude.1 = (bf16[2,4,64,128]{3,2,1,0:T(8,128)(2,1)S(1)}, bf16[16,256]{1,0:T(8,128)(2,1)S(1)}, s32[8,128]{1,0:T(8,128)S(1)}) custom-call(s32[16]{0:T(128)} %index_ref.1, bf16[2,128,64,128]{3,2,1,0:T(8,128)(2,1)} %spectra_ref.9), custom_call_target="tpu_custom_call" | custom-call | tf_op jit(solution)/shard_map/edge_amplitude/pallas_call | solution.py:84
  1.2 3.0 %collective-permute-start = (bf16[16,256]{1,0:T(8,128)(2,1)S(1)}, bf16[16,256]{1,0:T(8,128)(2,1)S(1)}, u32[]{:S(2)}, u32[]{:S(2)}) collective-permute-start(bf16[16,256]{1,0:T(8,128)(2,1)S(1)} %get-tuple-element.13), channel_id=1, source_target_pairs={{0,1},{1,0},{2,3},{3,2},{4,5},{5,4},{6,7},{7,6},{8,9},{9,8},{10,11... | collective-permute-start | bytes 24584 | tf_op jit(solution)/shard_map/ppermute | solution.py:121
  4.3 0.0 copy-done
  4.3 0.9 %extract_row.1 = (f32[128,128]{1,0:T(8,128)S(1)}, f32[128,128]{1,0:T(8,128)S(1)}) custom-call(s32[8,128]{1,0:T(8,128)S(1)} %get-tuple-element.10.column_ref, bf16[2,128,64,128]{3,2,1,0:T(8,128)(2,1)S(1)} %copy-done), custom_call_target="tpu_custom_call" | custom-call | bytes 8388608 | tf_op jit(solution)/shard_map/extract_row/pallas_call | solution.py:187
  5.2 0.7 %amplitude.2.after_ref.first_ref = f32[128,32,128]{2,1,0:T(8,128)S(1)} custom-call(bf16[2,128,64,128]{3,2,1,0:T(8,128)(2,1)S(1)} %copy-done, f32[128,128]{1,0:T(8,128)S(1)} %get-tuple-element.11.refs_0_.row_ref), custom_call_target="tpu_custom_call" | custom-call | flops 5242880 | bytes 2097152 | tf_op jit(solution)/shard_map/amplitude/pallas_call | solution.py:250
  5.9 0.0 collective-permute-done.below_ref.above_ref
  5.9 0.2 whiten_row.1.refs_0_.after_ref
  6.1 3.1 %collective-permute-start.1 = (bf16[1,128,128]{2,1,0:T(8,128)(2,1)S(1)}, bf16[1,128,128]{2,1,0:T(8,128)(2,1)S(1)}, u32[]{:S(2)}, u32[]{:S(2)}) collective-permute-start(bf16[1,128,128]{2,1,0:T(8,128)(2,1)S(1)} %whiten_row.1.refs_0_.after_ref), channel_id=1, source_target_pairs={{0,16},{2,18},{4,20},{6,22},{8,24},{10,26},{12,28},{14,30},{16,0},... | collective-permute-start | bytes 98312 | tf_op jit(solution)/shard_map/ppermute | solution.py:333
  9.2 1.6 %collective-permute-start.5 = (bf16[4,64,128]{2,1,0:T(8,128)(2,1)S(1)}, bf16[4,64,128]{2,1,0:T(8,128)(2,1)S(1)}, u32[]{:S(2)}, u32[]{:S(2)}) collective-permute-start(bf16[4,64,128]{2,1,0:T(8,128)(2,1)S(1)} %end_amplitude.1), channel_id=1, source_target_pairs={{0,1},{1,0},{2,3},{3,2},{4,5},{5,4},{6,7},{7,6},{8,9},{9,8},{10,11... | collective-permute-start | bytes 196616 | tf_op jit(solution)/shard_map/ppermute | solution.py:121
  10.8 0.3 %collective-permute-done.1.refs_1_ = bf16[1,128,128]{2,1,0:T(8,128)(2,1)S(1)} collective-permute-done((bf16[1,128,128]{2,1,0:T(8,128)(2,1)S(1)}, bf16[1,128,128]{2,1,0:T(8,128)(2,1)S(1)}, u32[]{:S(2)}, u32[]{:S(2)}) %collective-permute-start.1) | collective-permute-done | bytes 32800 | tf_op jit(solution)/shard_map/ppermute | solution.py:333
  11.1 2.8 %collective-permute-start.2 = (bf16[2,128,128]{2,1,0:T(8,128)(2,1)S(1)}, bf16[2,128,128]{2,1,0:T(8,128)(2,1)S(1)}, u32[]{:S(2)}, u32[]{:S(2)}) collective-permute-start(bf16[2,128,128]{2,1,0:T(8,128)(2,1)S(1)} %merge_rows.2.refs_0_), channel_id=1, source_target_pairs={{0,12},{2,14},{4,8},{6,10},{8,4},{10,6},{12,0},{14,2},{16,28},{18,... | collective-permute-start | bytes 196616 | tf_op jit(solution)/shard_map/ppermute | solution.py:333
  13.9 0.5 %collective-permute-start.3 = (bf16[2,128,128]{2,1,0:T(8,128)(2,1)S(1)}, bf16[2,128,128]{2,1,0:T(8,128)(2,1)S(1)}, u32[]{:S(2)}, u32[]{:S(2)}) collective-permute-start(bf16[2,128,128]{2,1,0:T(8,128)(2,1)S(1)} %merge_rows.2.refs_0_), channel_id=1, source_target_pairs={{0,4},{2,6},{4,0},{6,2},{8,12},{10,14},{12,8},{14,10},{16,20},{18,... | collective-permute-start | bytes 196616 | tf_op jit(solution)/shard_map/ppermute | solution.py:333
  14.4 0.1 collective-permute-start.4
  14.6 0.7 %amplitude.3.second_ref = f32[128,32,128]{2,1,0:T(8,128)S(1)} custom-call(bf16[2,128,64,128]{3,2,1,0:T(8,128)(2,1)S(1)} %copy-done, bf16[2,128,128]{2,1,0:T(8,128)(2,1)S(1)} %merge_rows.2.refs_0_), custom_call_target="tpu_custom_call" | custom-call | flops 5242880 | bytes 2097152 | tf_op jit(solution)/shard_map/amplitude/pallas_call | solution.py:250
  15.3 0.0 collective-permute-done.5.below_ref.above_ref
  15.3 2.0 %whiten_windows.1.refs_4_.refs_2_ = bf16[2,128,64,128]{3,2,1,0:T(8,128)(2,1)S(1)} custom-call(bf16[2,128,64,128]{3,2,1,0:T(8,128)(2,1)S(1)} %copy-done, f32[128,32,128]{2,1,0:T(8,128)S(1)} %amplitude.2.after_ref.first_ref, f32[128,32,128]{2,1,0:T(8,128)S(1)} %amplitude.3.second_ref, bf16[4,64,128]{2,1,0:T(8,128)(2,1)S(1)} %collective-permute-done.5.below_ref.above_ref, ...), custom_call_target="tpu_custom_call" | custom-call | flops 14680064 | bytes 4194304 | tf_op jit(solution)/shard_map/whiten_windows/pallas_call | solution.py:301
  17.3 0.0 collective-permute-done.2.refs_1_
  17.3 0.9 %collective-permute-done.3.refs_2_ = bf16[2,128,128]{2,1,0:T(8,128)(2,1)S(1)} collective-permute-done((bf16[2,128,128]{2,1,0:T(8,128)(2,1)S(1)}, bf16[2,128,128]{2,1,0:T(8,128)(2,1)S(1)}, u32[]{:S(2)}, u32[]{:S(2)}) %collective-permute-start.3) | collective-permute-done | bytes 65568 | tf_op jit(solution)/shard_map/ppermute | solution.py:333
  18.2 0.5 %collective-permute-done.4.refs_3_ = bf16[2,128,128]{2,1,0:T(8,128)(2,1)S(1)} collective-permute-done((bf16[2,128,128]{2,1,0:T(8,128)(2,1)S(1)}, bf16[2,128,128]{2,1,0:T(8,128)(2,1)S(1)}, u32[]{:S(2)}, u32[]{:S(2)}) %collective-permute-start.4) | collective-permute-done | bytes 65568 | tf_op jit(solution)/shard_map/ppermute | solution.py:333
  18.7 0.1 collective-permute-start.6
  18.8 1.5 %collective-permute-done.6.refs_1_ = bf16[8,128,128]{2,1,0:T(8,128)(2,1)S(1)} collective-permute-done((bf16[8,128,128]{2,1,0:T(8,128)(2,1)S(1)}, bf16[8,128,128]{2,1,0:T(8,128)(2,1)S(1)}, u32[]{:S(2)}, u32[]{:S(2)}) %collective-permute-start.6) | collective-permute-done | bytes 262176 | tf_op jit(solution)/shard_map/ppermute | solution.py:333
  20.3 1.6 %cross_spectra.1 = bf16[2,128,16,128]{3,2,1,0:T(8,128)(2,1)} custom-call(bf16[8,128,128]{2,1,0:T(8,128)(2,1)S(1)} %merge_rows.3.refs_0_, bf16[8,128,128]{2,1,0:T(8,128)(2,1)S(1)} %collective-permute-done.6.refs_1_, bf16[2,128,64,128]{3,2,1,0:T(8,128)(2,1)S(1)} %whiten_windows.1.refs_4_.refs_2_), custom_call_target="tpu_custom_call" | custom-call | tf_op jit(solution)/shard_map/cross_spectra/pallas_call | solution.py:419
  (3 shorter events, 0.1 us)
Async XLA Ops:
  0.0 4.3 %copy-start = (bf16[2,128,64,128]{3,2,1,0:T(8,128)(2,1)S(1)}, bf16[2,128,64,128]{3,2,1,0:T(8,128)(2,1)}, u32[]{:S(2)}) copy-start(bf16[2,128,64,128]{3,2,1,0:T(8,128)(2,1)} %spectra_ref.9) | copy-start | bytes 12582916
  1.2 4.7 %collective-permute-start = (bf16[16,256]{1,0:T(8,128)(2,1)S(1)}, bf16[16,256]{1,0:T(8,128)(2,1)S(1)}, u32[]{:S(2)}, u32[]{:S(2)}) collective-permute-start(bf16[16,256]{1,0:T(8,128)(2,1)S(1)} %get-tuple-element.13), channel_id=1, source_target_pairs={{0,1},{1,0},{2,3},{3,2},{4,5},{5,4},{6,7},{7,6},{8,9},{9,8},{10,11... | collective-permute-start | bytes 24584 | tf_op jit(solution)/shard_map/ppermute | solution.py:121
  6.1 5.0 %collective-permute-start.1 = (bf16[1,128,128]{2,1,0:T(8,128)(2,1)S(1)}, bf16[1,128,128]{2,1,0:T(8,128)(2,1)S(1)}, u32[]{:S(2)}, u32[]{:S(2)}) collective-permute-start(bf16[1,128,128]{2,1,0:T(8,128)(2,1)S(1)} %whiten_row.1.refs_0_.after_ref), channel_id=1, source_target_pairs={{0,16},{2,18},{4,20},{6,22},{8,24},{10,26},{12,28},{14,30},{16,0},... | collective-permute-start | bytes 98312 | tf_op jit(solution)/shard_map/ppermute | solution.py:333
  9.2 6.1 %collective-permute-start.5 = (bf16[4,64,128]{2,1,0:T(8,128)(2,1)S(1)}, bf16[4,64,128]{2,1,0:T(8,128)(2,1)S(1)}, u32[]{:S(2)}, u32[]{:S(2)}) collective-permute-start(bf16[4,64,128]{2,1,0:T(8,128)(2,1)S(1)} %end_amplitude.1), channel_id=1, source_target_pairs={{0,1},{1,0},{2,3},{3,2},{4,5},{5,4},{6,7},{7,6},{8,9},{9,8},{10,11... | collective-permute-start | bytes 196616 | tf_op jit(solution)/shard_map/ppermute | solution.py:121
  11.1 6.2 %collective-permute-start.2 = (bf16[2,128,128]{2,1,0:T(8,128)(2,1)S(1)}, bf16[2,128,128]{2,1,0:T(8,128)(2,1)S(1)}, u32[]{:S(2)}, u32[]{:S(2)}) collective-permute-start(bf16[2,128,128]{2,1,0:T(8,128)(2,1)S(1)} %merge_rows.2.refs_0_), channel_id=1, source_target_pairs={{0,12},{2,14},{4,8},{6,10},{8,4},{10,6},{12,0},{14,2},{16,28},{18,... | collective-permute-start | bytes 196616 | tf_op jit(solution)/shard_map/ppermute | solution.py:333
  13.9 4.3 %collective-permute-start.3 = (bf16[2,128,128]{2,1,0:T(8,128)(2,1)S(1)}, bf16[2,128,128]{2,1,0:T(8,128)(2,1)S(1)}, u32[]{:S(2)}, u32[]{:S(2)}) collective-permute-start(bf16[2,128,128]{2,1,0:T(8,128)(2,1)S(1)} %merge_rows.2.refs_0_), channel_id=1, source_target_pairs={{0,4},{2,6},{4,0},{6,2},{8,12},{10,14},{12,8},{14,10},{16,20},{18,... | collective-permute-start | bytes 196616 | tf_op jit(solution)/shard_map/ppermute | solution.py:333
  14.4 4.3 %collective-permute-start.4 = (bf16[2,128,128]{2,1,0:T(8,128)(2,1)S(1)}, bf16[2,128,128]{2,1,0:T(8,128)(2,1)S(1)}, u32[]{:S(2)}, u32[]{:S(2)}) collective-permute-start(bf16[2,128,128]{2,1,0:T(8,128)(2,1)S(1)} %merge_rows.2.refs_0_), channel_id=1, source_target_pairs={{0,8},{2,10},{4,12},{6,14},{8,0},{10,2},{12,4},{14,6},{16,24},{18,... | collective-permute-start | bytes 196616 | tf_op jit(solution)/shard_map/ppermute | solution.py:333
  18.7 1.6 %collective-permute-start.6 = (bf16[8,128,128]{2,1,0:T(8,128)(2,1)S(1)}, bf16[8,128,128]{2,1,0:T(8,128)(2,1)S(1)}, u32[]{:S(2)}, u32[]{:S(2)}) collective-permute-start(bf16[8,128,128]{2,1,0:T(8,128)(2,1)S(1)} %merge_rows.3.refs_0_), channel_id=1, source_target_pairs={{0,2},{2,0},{4,6},{6,4},{8,10},{10,8},{12,14},{14,12},{16,18},{18,... | collective-permute-start | bytes 786440 | tf_op jit(solution)/shard_map/ppermute | solution.py:333
